TPU v7x, 128 devices: a whole 4x4x4 slice. The times are simulated.
128 devices in a mesh: tile: 16 (over x_lo, y, core), frame: 8 (over z, x_hi).
Axes of the slice: x: 4 (x_hi: 2, x_lo: 2; x = x_hi * 2 + x_lo), y: 4, z: 4, core: 2. Of those that a mesh axis runs over, the one named last changes fastest.
Arguments:
- tokens: bfloat16 [16, 24, 128, 768], P('frame', None, 'tile'), may hold values from -6 to 6
- gain_space: float32 [768], replicated, may hold values from 0.5 to 1.5
- qkv_space: bfloat16 [768, 2304], replicated, may hold values from -2 to 2
- out_space: bfloat16 [768, 768], replicated, may hold values from -0.21875 to 0.21875
- gain_time: float32 [768], replicated, may hold values from 0.5 to 1.5
- qkv_time: bfloat16 [768, 2304], replicated, may hold values from -2 to 2
- out_time: bfloat16 [768, 768], replicated, may hold values from -0.21875 to 0.21875
- cotangent: bfloat16 [16, 24, 128, 768], P('frame', None, 'tile'), may hold values from -6 to 6
Outputs:
- layer_out: bfloat16 [16, 24, 128, 768], P('frame', None, 'tile')
- grad_tokens: float32 [16, 24, 128, 768], P('frame', None, 'tile')
- grad_gain_space: float32 [768], P(('tile', 'frame'))
- grad_qkv_space: float32 [768, 2304], P(('tile', 'frame'))
- grad_out_space: float32 [768, 768], P(('tile', 'frame'))
- grad_gain_time: float32 [768], P(('tile', 'frame'))
- grad_qkv_time: float32 [768, 2304], P(('tile', 'frame'))
- grad_out_time: float32 [768, 768], P(('tile', 'frame'))
All inputs are finite; a program needn't handle non-finite values.
Results may differ from a plain program's by a relative error of at most 0.025.
Values may be sent and summed in bfloat16 or wider, within the bound.
No kernel may reach another device: no remote copies, remote signals or barrier semaphores. Data moves between devices by JAX's collectives and lax.ppermute only.
A program may use at most 192 MiB of HBM per device.

v0:
```python
import math

import jax
import jax.numpy as jnp
from jax import lax
from jax.sharding import PartitionSpec as P

HDIM = 64
BH = 8


norm_eps = 1e-05


def with_halo(shard, sides, width):
    for axis, dim in sides:
        size, length = (lax.axis_size(axis), shard.shape[dim])
        up = [(i, (i + 1) % size) for i in range(size)]
        down = [(j, i) for i, j in up]
        last = lax.slice_in_dim(shard, length - width, length, axis=dim)
        leading = lax.slice_in_dim(shard, 0, width, axis=dim)
        before = lax.ppermute(last, axis, up)
        after = lax.ppermute(leading, axis, down)
        shard = jnp.concatenate([before, shard, after], axis=dim)
    return shard


def shifted(shard, axis, by):
    size = lax.axis_size(axis)
    return lax.ppermute(shard, axis, [(i, (i + by) % size) for i in range(size)])


def layer_norm(row_vals, gain_vec):
    centre_mean = jnp.mean(row_vals, axis=-1, keepdims=True)
    centred = row_vals - centre_mean
    variance = jnp.mean(centred * centred, axis=-1, keepdims=True)
    return (centred * lax.rsqrt(variance + norm_eps) * gain_vec).astype(jnp.bfloat16)


def project(in_rows, weight):
    flat_rows = in_rows.reshape(-1, in_rows.shape[-1])
    result = jnp.dot(flat_rows, weight, preferred_element_type=jnp.float32)
    return result.astype(jnp.bfloat16).reshape(in_rows.shape[:-1] + (weight.shape[1],))


def residual_term(in_rows, weight):
    flat_rows = in_rows.reshape(-1, in_rows.shape[-1])
    result = jnp.dot(flat_rows, weight, preferred_element_type=jnp.float32)
    return result.reshape(in_rows.shape[:-1] + (weight.shape[1],))


def back_project(cot_rows, weight):
    flat_rows = cot_rows.reshape(-1, cot_rows.shape[-1])
    result = lax.dot_general(
        flat_rows, weight, (((1,), (1,)), ((), ())), preferred_element_type=jnp.float32
    )
    return result.astype(jnp.bfloat16).reshape(cot_rows.shape[:-1] + (weight.shape[0],))


def weight_term(left_rows, right_rows):
    left_flat = left_rows.reshape(-1, left_rows.shape[-1])
    right_flat = right_rows.reshape(-1, right_rows.shape[-1])
    return lax.dot_general(
        left_flat, right_flat, (((0,), (0,)), ((), ())), preferred_element_type=jnp.float32
    )


def spatial_core(queries, keyval):
    lat_rows, tile_width, features = queries.shape
    head_count = features // HDIM
    blocks = lat_rows // BH
    span_keys = BH * 3 * tile_width
    query_blocks = queries.reshape(blocks, BH * tile_width, head_count, HDIM)
    pole_pad = jnp.zeros((BH, 3 * tile_width, 2 * features), keyval.dtype)
    padded = jnp.concatenate([pole_pad, keyval, pole_pad], axis=0)
    padded = padded.reshape(blocks + 2, span_keys, 2, head_count, HDIM)
    score_parts = [
        jnp.einsum(
            "bqhd,bkhd->bhqk",
            query_blocks,
            padded[offset : offset + blocks, :, 0],
            preferred_element_type=jnp.float32,
        )
        for offset in range(3)
    ]
    scores = jnp.concatenate(score_parts, axis=-1) * HDIM ** (-0.5)
    block_index = jnp.arange(blocks)[:, None] + jnp.arange(3)[None, :] - 1
    valid_keys = jnp.repeat((block_index >= 0) & (block_index < blocks), span_keys, axis=1)
    scores = jnp.where(valid_keys[:, None, None, :], scores, -1e30)
    row_max = jnp.max(scores, axis=-1, keepdims=True)
    exponent = jnp.exp(scores - row_max)
    weights = (exponent / jnp.sum(exponent, axis=-1, keepdims=True)).astype(jnp.bfloat16)
    mixed_rows = jnp.einsum(
        "bhqk,bkhd->bqhd",
        weights[..., :span_keys],
        padded[0:blocks, :, 1],
        preferred_element_type=jnp.float32,
    )
    for offset in range(1, 3):
        mixed_rows = mixed_rows + jnp.einsum(
            "bhqk,bkhd->bqhd",
            weights[..., offset * span_keys : (offset + 1) * span_keys],
            padded[offset : offset + blocks, :, 1],
            preferred_element_type=jnp.float32,
        )
    return mixed_rows.reshape(lat_rows, tile_width, features).astype(jnp.bfloat16)


def temporal_core(packed):
    frame_count, count_tokens, triple_width = packed.shape
    features = triple_width // 3
    head_count = features // HDIM
    sections = packed.reshape(frame_count, count_tokens, 3, head_count, HDIM)
    scores = jnp.einsum(
        "fnhd,gnhd->nhfg", sections[:, :, 0], sections[:, :, 1], preferred_element_type=jnp.float32
    ) * HDIM ** (-0.5)
    row_max = jnp.max(scores, axis=-1, keepdims=True)
    exponent = jnp.exp(scores - row_max)
    weights = (exponent / jnp.sum(exponent, axis=-1, keepdims=True)).astype(jnp.bfloat16)
    mixed_rows = jnp.einsum(
        "nhfg,gnhd->fnhd", weights, sections[:, :, 2], preferred_element_type=jnp.float32
    )
    return mixed_rows.reshape(frame_count, count_tokens, features).astype(jnp.bfloat16)


def frame_attention(packed):
    frame_count, lat_rows, tile_width, triple_width = packed.shape
    result = temporal_core(packed.reshape(frame_count, lat_rows * tile_width, triple_width))
    return result.reshape(frame_count, lat_rows, tile_width, triple_width // 3)


def shards(tokens, gain_space, qkv_space, out_space, gain_time, qkv_time, out_time, cotangent):
    frames_dev, lat_rows, tile_width, features = tokens.shape
    total_tokens = (
        frames_dev * lat_rows * tile_width * lax.axis_size("tile") * lax.axis_size("frame")
    )
    grad_scale = 1.0 / math.sqrt(total_tokens)
    tokens_wide = tokens.astype(jnp.float32)
    y_space, norm_back_space = jax.vjp(layer_norm, tokens_wide, gain_space)
    packed_space = project(y_space, qkv_space)
    query_space = packed_space[..., :features]
    keyval_space = packed_space[..., features:]
    extended = with_halo(keyval_space, (("tile", 2),), tile_width)
    o_space = lax.map(lambda couple: spatial_core(couple[0], couple[1]), (query_space, extended))
    x_mid = (tokens_wide + residual_term(o_space, out_space)).astype(jnp.bfloat16)
    y_time, norm_back_time = jax.vjp(layer_norm, x_mid.astype(jnp.float32), gain_time)
    packed_home = project(y_time, qkv_time)
    arrived = lax.all_to_all(packed_home, "frame", split_axis=1, concat_axis=0, tiled=True)
    o_moved = frame_attention(arrived)
    o_time = lax.all_to_all(o_moved, "frame", split_axis=0, concat_axis=1, tiled=True)
    layer_out = (x_mid.astype(jnp.float32) + residual_term(o_time, out_time)).astype(jnp.bfloat16)
    d_proj_time = back_project(cotangent, out_time)
    d_proj_moved = lax.all_to_all(d_proj_time, "frame", split_axis=1, concat_axis=0, tiled=True)
    d_packed_moved = jax.vjp(frame_attention, arrived)[1](d_proj_moved)[0]
    d_packed_time = lax.all_to_all(d_packed_moved, "frame", split_axis=0, concat_axis=1, tiled=True)
    term_qkv_time = weight_term(y_time, d_packed_time)
    d_y_time = back_project(d_packed_time, qkv_time)
    d_norm_mid, term_gain_time = norm_back_time(d_y_time)
    d_mid = cotangent.astype(jnp.float32) + d_norm_mid
    d_mid_b = d_mid.astype(jnp.bfloat16)
    d_proj_space = back_project(d_mid_b, out_space)

    def frame_back(triple):
        return jax.vjp(spatial_core, triple[0], triple[1])[1](triple[2])

    d_query, d_extended = lax.map(frame_back, (query_space, extended, d_proj_space))
    west_part = d_extended[:, :, :tile_width]
    east_part = d_extended[:, :, 2 * tile_width :]
    d_keyval = (
        d_extended[:, :, tile_width : 2 * tile_width]
        + shifted(west_part, "tile", -1)
        + shifted(east_part, "tile", 1)
    )
    d_packed_space = jnp.concatenate([d_query, d_keyval], axis=-1)
    d_y_space = back_project(d_packed_space, qkv_space)
    d_norm_tokens, term_gain_space = norm_back_space(d_y_space)
    grad_tokens = d_mid + d_norm_tokens
    term_qkv_space = weight_term(y_space, d_packed_space)
    term_out_space = weight_term(o_space, d_mid_b)
    term_out_time = weight_term(o_time, cotangent)
    summed = (
        lax.psum_scatter(term_gain_space, ("tile", "frame"), scatter_dimension=0, tiled=True),
        lax.psum_scatter(term_qkv_space, ("tile", "frame"), scatter_dimension=0, tiled=True),
        lax.psum_scatter(term_out_space, ("tile", "frame"), scatter_dimension=0, tiled=True),
        lax.psum_scatter(term_gain_time, ("tile", "frame"), scatter_dimension=0, tiled=True),
        lax.psum_scatter(term_qkv_time, ("tile", "frame"), scatter_dimension=0, tiled=True),
        lax.psum_scatter(term_out_time, ("tile", "frame"), scatter_dimension=0, tiled=True),
    )
    return (
        layer_out,
        grad_tokens,
        summed[0] * grad_scale,
        summed[1] * grad_scale,
        summed[2] * grad_scale,
        summed[3] * grad_scale,
        summed[4] * grad_scale,
        summed[5] * grad_scale,
    )


def solution(mesh):
    in_specs = (
        P("frame", None, "tile", None),
        P(),
        P(),
        P(),
        P(),
        P(),
        P(),
        P("frame", None, "tile", None),
    )
    out_specs = (
        P("frame", None, "tile", None),
        P("frame", None, "tile", None),
        P(("tile", "frame")),
        P(("tile", "frame"), None),
        P(("tile", "frame"), None),
        P(("tile", "frame")),
        P(("tile", "frame"), None),
        P(("tile", "frame"), None),
    )
    return jax.shard_map(shards, mesh=mesh, in_specs=in_specs, out_specs=out_specs, check_vma=False)
```

profile of v0, /device:TPU:1, one launch (start us, length us, event | category | flops | bytes accessed | tf_op | source)
XLA Modules:
  0.0 1828.9 jit_solution(10377799169133677792)
XLA Ops:
  14.6 7.5 all-to-all-start.2
  31.7 195.1 %while.26 = (s32[]{:T(128)}, bf16[2,24,8,768]{3,2,1,0:T(8,128)(2,1)}, bf16[2,24,24,1536]{3,2,1,0:T(8,128)(2,1)}, bf16[2,24,8,768]{3,2,1,0:T(8,128)(2,1)}, s32[]{:T(128)}, /*index=5*/bf16[]{:T(256)}) while((s32[]{:T(128)}, bf16[2,24,8,768]{3,2,1,0:T(8,128)(2,1)}, bf16[2,24,24,1536]{3,2,1,0:T(8,128)(2,1)}, bf16[2,24,8,768]{3,2,1,0:T(8,128)(2,1)}, ...), condition=%wide.region_5.6_spmd, body=%wide.region_2.5_spmd.sunk | while | flops 353747584 | bytes 77882216 | solution.py:144
  35.5 10.6 reshape.256
  46.1 10.4 fusion.292
  83.3 14.8 fusion.297
  132.8 10.6 reshape.256
  143.5 10.4 fusion.292
  180.6 14.8 fusion.297
  233.5 7.5 all-to-all-start
  245.7 11.2 all-to-all-done
  259.7 6.5 reshape_reshape.3
  299.5 6.6 reshape.239
  306.1 6.9 all-to-all-start.3
  318.2 10.6 all-to-all-done.3
  341.6 232.5 %while.27 = (s32[]{:T(128)}, bf16[2,24,8,768]{3,2,1,0:T(8,128)(2,1)}, bf16[2,24,24,1536]{3,2,1,0:T(8,128)(2,1)}, bf16[2,24,8,768]{3,2,1,0:T(8,128)(2,1)}, bf16[2...) while((s32[]{:T(128)}, ...), condition=%wide.region_21.22_spmd, body=%wide.region_15.21_spmd.sunk | while | flops 945930304 | bytes 219926576 | solution.py:166
  346.8 8.5 reshape.259
  355.3 9.7 fusion.330
  418.4 7.1 fusion.338
  450.7 5.9 broadcast_in_dim.315
  462.8 8.5 reshape.259
  471.3 9.7 fusion.330
  534.3 7.1 fusion.338
  576.0 18.9 %collective-permute-start.3 = (bf16[2,24,8,1536]{3,2,1,0:T(8,128)(2,1)S(1)}, bf16[2,24,8,1536]{3,2,1,0:T(8,128)(2,1)S(1)}, u32[]{:S(2)}, u32[]{:S(2)}) collective-permute-start(bf16[2,24,8,1536]{3,2,1,0:T(8,128)(2,1)S(1)} %get-tuple-element.203), channel_id=1, source_target_pairs={{0,8},{8,16},{16,24},{24,32},{32,40},{40,48},{48,56},{56,64},{64,7... | collective-permute-start | bytes 3538952 | tf_op jit(solution)/shard_map/ppermute | solution.py:30
  597.2 10.9 collective-permute-done.3
  618.1 582.6 %fusion.175 = (f32[8,2304]{1,0:T(8,128)}, f32[8,768]{1,0:T(8,128)}, f32[8,2304]{1,0:T(8,128)}, f32[8,768]{1,0:T(8,128)}) fusion(f32[768,2304]{1,0:T(8,128)} %convolution_bitcast_fusion, f32[768,768]{1,0:T(8,128)} %convolution_bitcast_fusion.1, f32[768,2304]{1,0:T(8,128)} %fusion.183, f32[768,768]{1,0:T(8,128)S(1)} %copy-done.26), kind=kCustom, calls=%all-reduce-scatter.4 | all-reduce-scatter fusion | flops 6291457 | bytes 19070976
  1208.9 23.8 %collective-permute-start.63 = (f32[8,768]{1,0:T(8,128)}, f32[8,768]{1,0:T(8,128)S(1)}, u32[]{:S(2)}, u32[]{:S(2)}) collective-permute-start(f32[8,768]{1,0:T(8,128)} %get-tuple-element.175), channel_id=1, source_target_pairs={{0,28},{1,29},{2,30},{3,31},{4,32},{5,33},{6,34},{7,35},{8,36},{9,... | collective-permute-start | bytes 73736
  1242.2 7.9 collective-permute-start.56
  1516.2 72.3 %all-reduce.22 = (f32[768]{0:T(1024)S(1)}, f32[768]{0:T(1024)S(1)}) all-reduce(f32[768]{0:T(1024)S(1)} %get-tuple-element.146, f32[768]{0:T(1024)S(1)} %copy-done.180), channel_id=2, replica_groups=mesh['tile'=16,'frame'=8] {'tile','frame'}, use_global_device_ids=true, to_apply=%region_25.26.clone | all-reduce | flops 1536 | bytes 12288
  1610.8 27.2 %concatenate.33 = f32[262,768]{1,0:T(8,128)S(1)} concatenate(f32[6,768]{1,0:T(8,128)} %copy-done.136, f32[8,768]{1,0:T(8,128)} %copy-done.137, f32[8,768]{1,0:T(8,128)} %copy-done.138, f32[8,768]{1,0:T(8,128)} %copy-done.139, f32[8,768]{1,0:T(8,128)} %copy-done.140, f32[8,768]{1,0:T(8,128)} %copy-done.141, f32[8,768]{1,0:T(8,128)} %copy-done.142, f32[8,768]{1,0:T(8,128)} %copy-done.143, ...), dimensions={0} | concatenate | bytes 1609728
  1638.0 26.5 %concatenate.35 = f32[262,768]{1,0:T(8,128)S(1)} concatenate(f32[6,768]{1,0:T(8,128)S(1)} %collective-permute-done.131, f32[8,768]{1,0:T(8,128)} %copy-done.168, f32[8,768]{1,0:T(8,128)} %copy-done.169, f32[8,768]{1,0:T(8,128)} %copy-done.170, f32[8,768]{1,0:T(8,128)} %copy-done.171, f32[8,768]{1,0:T(8,128)} %copy-done.172, f32[8,768]{1,0:T(8,128)} %copy-done.173, ...), dimensions={0} | concatenate | bytes 1609728
  1697.4 52.5 %concatenate.32 = f32[262,2304]{1,0:T(8,128)} concatenate(f32[6,2304]{1,0:T(8,128)S(1)} %collective-permute-done.35, f32[8,2304]{1,0:T(8,128)S(1)} %collective-permute-done.34, f32[8,2304]{1,0:T(8,128)S(1)} %collective-permute-done.33, f32[8,2304]{1,0:T(8,128)S(1)} %copy-done.79, f32[8,2304]{1,0:T(8,128)S(1)} %copy-done.81, f32[8,2304]{1,0:T(8,128)S(1)} %copy-done.83, ...), dimensions={0} | concatenate | bytes 4829184
  1773.0 54.1 %concatenate.34 = f32[262,2304]{1,0:T(8,128)} concatenate(f32[6,2304]{1,0:T(8,128)} %copy-done.77, f32[8,2304]{1,0:T(8,128)} %copy-done.119, f32[8,2304]{1,0:T(8,128)} %copy-done.121, f32[8,2304]{1,0:T(8,128)} %copy-done.123, f32[8,2304]{1,0:T(8,128)} %copy-done.125, f32[8,2304]{1,0:T(8,128)} %copy-done.127, f32[8,2304]{1,0:T(8,128)} %copy-done.129, ...), dimensions={0} | concatenate | bytes 4829184
  (868 shorter events, 761.1 us)
Async XLA Ops:
  14.6 218.9 %all-to-all-start.2 = ((bf16[2,24,8,768]{3,2,0,1:T(8,128)(2,1)}), bf16[2,24,8,768]{3,2,0,1:T(8,128)(2,1)}, u32[]{:S(2)}, u32[]{:S(2)}) async-start(bf16[2,24,8,768]{3,2,0,1:T(8,128)(2,1)} %copy.155), calls=%async_computation.2 | async-start | bytes 1179648 | tf_op jit(solution)/shard_map/all_to_all | solution.py:153
  233.5 23.4 %all-to-all-start = ((bf16[2,24,8,2304]{3,2,0,1:T(8,128)(2,1)}), bf16[2,24,8,2304]{3,2,0,1:T(8,128)(2,1)}, u32[]{:S(2)}, u32[]{:S(2)}) async-start(bf16[2,24,8,2304]{3,2,0,1:T(8,128)(2,1)} %copy.146), calls=%async_computation | async-start | bytes 3538944 | tf_op jit(solution)/shard_map/all_to_all | solution.py:148
  278.7 27.4 %all-to-all-start.1 = ((bf16[16,3,8,768]{3,2,1,0:T(8,128)(2,1)}), bf16[16,3,8,768]{3,2,1,0:T(8,128)(2,1)}, u32[]{:S(2)}, u32[]{:S(2)}) async-start(bf16[16,3,8,768]{3,2,1,0:T(8,128)(2,1)} %convert_element_type.244), calls=%async_computation.1 | async-start | bytes 1179648 | tf_op jit(solution)/shard_map/all_to_all | solution.py:150
  306.1 22.7 %all-to-all-start.3 = ((bf16[16,3,8,2304]{3,2,1,0:T(8,128)(2,1)}), bf16[16,3,8,2304]{3,2,1,0:T(8,128)(2,1)}, u32[]{:S(2)}, u32[]{:S(2)}) async-start(bf16[16,3,8,2304]{3,2,1,0:T(8,128)(2,1)} %reshape.239), calls=%async_computation.3 | async-start | bytes 3538944 | tf_op jit(solution)/shard_map/all_to_all | solution.py:155
  576.0 32.1 %collective-permute-start.3 = (bf16[2,24,8,1536]{3,2,1,0:T(8,128)(2,1)S(1)}, bf16[2,24,8,1536]{3,2,1,0:T(8,128)(2,1)S(1)}, u32[]{:S(2)}, u32[]{:S(2)}) collective-permute-start(bf16[2,24,8,1536]{3,2,1,0:T(8,128)(2,1)S(1)} %get-tuple-element.203), channel_id=1, source_target_pairs={{0,8},{8,16},{16,24},{24,32},{32,40},{40,48},{48,56},{56,64},{64,7... | collective-permute-start | bytes 3538952 | tf_op jit(solution)/shard_map/ppermute | solution.py:30
  1202.9 31.3 %collective-permute-start.66 = (f32[8,768]{1,0:T(8,128)}, f32[8,768]{1,0:T(8,128)S(1)}, u32[]{:S(2)}, u32[]{:S(2)}) collective-permute-start(f32[8,768]{1,0:T(8,128)} %get-tuple-element.175), channel_id=1, source_target_pairs={{0,31},{1,32},{2,33},{3,34},{4,35},{5,36},{6,37},{7,38},{8,39},{9,... | collective-permute-start | bytes 73736
  1204.2 31.5 %collective-permute-start.65 = (f32[8,768]{1,0:T(8,128)}, f32[8,768]{1,0:T(8,128)S(1)}, u32[]{:S(2)}, u32[]{:S(2)}) collective-permute-start(f32[8,768]{1,0:T(8,128)} %get-tuple-element.175), channel_id=1, source_target_pairs={{0,30},{1,31},{2,32},{3,33},{4,34},{5,35},{6,36},{7,37},{8,38},{9,... | collective-permute-start | bytes 73736
  1206.3 26.4 %collective-permute-start.131 = (f32[6,768]{1,0:T(8,128)S(1)}, f32[6,768]{1,0:T(8,128)S(1)}, u32[]{:S(2)}, u32[]{:S(2)}) collective-permute-start(f32[6,768]{1,0:T(8,128)S(1)} %slice.173), channel_id=1, source_target_pairs={{0,32},{1,33},{2,34},{3,35},{4,36},{5,37},{6,38},{7,39},{8,40},{9,... | collective-permute-start | bytes 55304
  1207.6 30.7 %collective-permute-start.64 = (f32[8,768]{1,0:T(8,128)}, f32[8,768]{1,0:T(8,128)S(1)}, u32[]{:S(2)}, u32[]{:S(2)}) collective-permute-start(f32[8,768]{1,0:T(8,128)} %get-tuple-element.175), channel_id=1, source_target_pairs={{0,29},{1,30},{2,31},{3,32},{4,33},{5,34},{6,35},{7,36},{8,37},{9,... | collective-permute-start | bytes 73736
  1208.9 30.7 %collective-permute-start.63 = (f32[8,768]{1,0:T(8,128)}, f32[8,768]{1,0:T(8,128)S(1)}, u32[]{:S(2)}, u32[]{:S(2)}) collective-permute-start(f32[8,768]{1,0:T(8,128)} %get-tuple-element.175), channel_id=1, source_target_pairs={{0,28},{1,29},{2,30},{3,31},{4,32},{5,33},{6,34},{7,35},{8,36},{9,... | collective-permute-start | bytes 73736
  1242.2 18.2 collective-permute-start.56
  1379.6 32.5 %collective-permute-start.34 = (f32[8,2304]{1,0:T(8,128)}, f32[8,2304]{1,0:T(8,128)S(1)}, u32[]{:S(2)}, u32[]{:S(2)}) collective-permute-start(f32[8,2304]{1,0:T(8,128)} %get-tuple-element.174), channel_id=1, source_target_pairs={{0,31},{1,32},{2,33},{3,34},{4,35},{5,36},{6,37},{7,38},{8,39},{9,... | collective-permute-start | bytes 221192
  1382.6 30.8 %collective-permute-start.33 = (f32[8,2304]{1,0:T(8,128)}, f32[8,2304]{1,0:T(8,128)S(1)}, u32[]{:S(2)}, u32[]{:S(2)}) collective-permute-start(f32[8,2304]{1,0:T(8,128)} %get-tuple-element.174), channel_id=1, source_target_pairs={{0,30},{1,31},{2,32},{3,33},{4,34},{5,35},{6,36},{7,37},{8,38},{9,... | collective-permute-start | bytes 221192
  1386.1 21.0 %collective-permute-start.35 = (f32[6,2304]{1,0:T(8,128)S(1)}, f32[6,2304]{1,0:T(8,128)S(1)}, u32[]{:S(2)}, u32[]{:S(2)}) collective-permute-start(f32[6,2304]{1,0:T(8,128)S(1)} %slice.170), channel_id=1, source_target_pairs={{0,32},{1,33},{2,34},{3,35},{4,36},{5,37},{6,38},{7,39},{8,40},{9,... | collective-permute-start | bytes 165896
  1387.5 21.5 %collective-permute-start.99 = (f32[6,2304]{1,0:T(8,128)S(1)}, f32[6,2304]{1,0:T(8,128)S(1)}, u32[]{:S(2)}, u32[]{:S(2)}) collective-permute-start(f32[6,2304]{1,0:T(8,128)S(1)} %slice.172), channel_id=1, source_target_pairs={{0,32},{1,33},{2,34},{3,35},{4,36},{5,37},{6,38},{7,39},{8,40},{9,... | collective-permute-start | bytes 165896
  1501.1 87.4 %collective-permute-start.92 = (f32[8,2304]{1,0:T(8,128)}, f32[8,2304]{1,0:T(8,128)}, u32[]{:S(2)}, u32[]{:S(2)}) collective-permute-start(f32[8,2304]{1,0:T(8,128)} %get-tuple-element.176), channel_id=1, source_target_pairs={{0,25},{1,26},{2,27},{3,28},{4,29},{5,30},{6,31},{7,32},{8,33},{9,... | collective-permute-start | bytes 221192
  1504.8 88.7 %collective-permute-start.91 = (f32[8,2304]{1,0:T(8,128)}, f32[8,2304]{1,0:T(8,128)}, u32[]{:S(2)}, u32[]{:S(2)}) collective-permute-start(f32[8,2304]{1,0:T(8,128)} %get-tuple-element.176), channel_id=1, source_target_pairs={{0,24},{1,25},{2,26},{3,27},{4,28},{5,29},{6,30},{7,31},{8,32},{9,... | collective-permute-start | bytes 221192
  1506.7 91.0 %collective-permute-start.90 = (f32[8,2304]{1,0:T(8,128)}, f32[8,2304]{1,0:T(8,128)}, u32[]{:S(2)}, u32[]{:S(2)}) collective-permute-start(f32[8,2304]{1,0:T(8,128)} %get-tuple-element.176), channel_id=1, source_target_pairs={{0,23},{1,24},{2,25},{3,26},{4,27},{5,28},{6,29},{7,30},{8,31},{9,... | collective-permute-start | bytes 221192
  1509.4 93.8 %collective-permute-start.89 = (f32[8,2304]{1,0:T(8,128)}, f32[8,2304]{1,0:T(8,128)}, u32[]{:S(2)}, u32[]{:S(2)}) collective-permute-start(f32[8,2304]{1,0:T(8,128)} %get-tuple-element.176), channel_id=1, source_target_pairs={{0,22},{1,23},{2,24},{3,25},{4,26},{5,27},{6,28},{7,29},{8,30},{9,... | collective-permute-start | bytes 221192
  1512.0 95.6 %collective-permute-start.88 = (f32[8,2304]{1,0:T(8,128)}, f32[8,2304]{1,0:T(8,128)}, u32[]{:S(2)}, u32[]{:S(2)}) collective-permute-start(f32[8,2304]{1,0:T(8,128)} %get-tuple-element.176), channel_id=1, source_target_pairs={{0,21},{1,22},{2,23},{3,24},{4,25},{5,26},{6,27},{7,28},{8,29},{9,... | collective-permute-start | bytes 221192
  1588.5 75.9 %collective-permute-start.87 = (f32[8,2304]{1,0:T(8,128)}, f32[8,2304]{1,0:T(8,128)}, u32[]{:S(2)}, u32[]{:S(2)}) collective-permute-start(f32[8,2304]{1,0:T(8,128)} %get-tuple-element.176), channel_id=1, source_target_pairs={{0,20},{1,21},{2,22},{3,23},{4,24},{5,25},{6,26},{7,27},{8,28},{9,... | collective-permute-start | bytes 221192
  1593.5 76.4 %collective-permute-start.86 = (f32[8,2304]{1,0:T(8,128)}, f32[8,2304]{1,0:T(8,128)}, u32[]{:S(2)}, u32[]{:S(2)}) collective-permute-start(f32[8,2304]{1,0:T(8,128)} %get-tuple-element.176), channel_id=1, source_target_pairs={{0,19},{1,20},{2,21},{3,22},{4,23},{5,24},{6,25},{7,26},{8,27},{9,... | collective-permute-start | bytes 221192
  1597.7 75.7 %collective-permute-start.85 = (f32[8,2304]{1,0:T(8,128)}, f32[8,2304]{1,0:T(8,128)}, u32[]{:S(2)}, u32[]{:S(2)}) collective-permute-start(f32[8,2304]{1,0:T(8,128)} %get-tuple-element.176), channel_id=1, source_target_pairs={{0,18},{1,19},{2,20},{3,21},{4,22},{5,23},{6,24},{7,25},{8,26},{9,... | collective-permute-start | bytes 221192
  1603.3 72.6 %collective-permute-start.84 = (f32[8,2304]{1,0:T(8,128)}, f32[8,2304]{1,0:T(8,128)}, u32[]{:S(2)}, u32[]{:S(2)}) collective-permute-start(f32[8,2304]{1,0:T(8,128)} %get-tuple-element.176), channel_id=1, source_target_pairs={{0,17},{1,18},{2,19},{3,20},{4,21},{5,22},{6,23},{7,24},{8,25},{9,... | collective-permute-start | bytes 221192
  1607.6 72.5 %collective-permute-start.83 = (f32[8,2304]{1,0:T(8,128)}, f32[8,2304]{1,0:T(8,128)}, u32[]{:S(2)}, u32[]{:S(2)}) collective-permute-start(f32[8,2304]{1,0:T(8,128)} %get-tuple-element.176), channel_id=1, source_target_pairs={{0,16},{1,17},{2,18},{3,19},{4,20},{5,21},{6,22},{7,23},{8,24},{9,... | collective-permute-start | bytes 221192
  1664.4 18.5 %collective-permute-start.82 = (f32[8,2304]{1,0:T(8,128)}, f32[8,2304]{1,0:T(8,128)S(1)}, u32[]{:S(2)}, u32[]{:S(2)}) collective-permute-start(f32[8,2304]{1,0:T(8,128)} %get-tuple-element.176), channel_id=1, source_target_pairs={{0,15},{1,16},{2,17},{3,18},{4,19},{5,20},{6,21},{7,22},{8,23},{9,... | collective-permute-start | bytes 221192
  1682.9 66.9 %collective-permute-start.77 = (f32[8,2304]{1,0:T(8,128)}, f32[8,2304]{1,0:T(8,128)S(1)}, u32[]{:S(2)}, u32[]{:S(2)}) collective-permute-start(f32[8,2304]{1,0:T(8,128)} %get-tuple-element.176), channel_id=1, source_target_pairs={{0,10},{1,11},{2,12},{3,13},{4,14},{5,15},{6,16},{7,17},{8,18},{9,... | collective-permute-start | bytes 221192
  1684.7 68.8 %collective-permute-start.76 = (f32[8,2304]{1,0:T(8,128)}, f32[8,2304]{1,0:T(8,128)}, u32[]{:S(2)}, u32[]{:S(2)}) collective-permute-start(f32[8,2304]{1,0:T(8,128)} %get-tuple-element.176), channel_id=1, source_target_pairs={{0,9},{1,10},{2,11},{3,12},{4,13},{5,14},{6,15},{7,16},{8,17},{9,1... | collective-permute-start | bytes 221192
  1688.8 68.7 %collective-permute-start.75 = (f32[8,2304]{1,0:T(8,128)}, f32[8,2304]{1,0:T(8,128)}, u32[]{:S(2)}, u32[]{:S(2)}) collective-permute-start(f32[8,2304]{1,0:T(8,128)} %get-tuple-element.176), channel_id=1, source_target_pairs={{0,8},{1,9},{2,10},{3,11},{4,12},{5,13},{6,14},{7,15},{8,16},{9,17... | collective-permute-start | bytes 221192
  1690.7 69.4 %collective-permute-start.74 = (f32[8,2304]{1,0:T(8,128)}, f32[8,2304]{1,0:T(8,128)}, u32[]{:S(2)}, u32[]{:S(2)}) collective-permute-start(f32[8,2304]{1,0:T(8,128)} %get-tuple-element.176), channel_id=1, source_target_pairs={{0,7},{1,8},{2,9},{3,10},{4,11},{5,12},{6,13},{7,14},{8,15},{9,16}... | collective-permute-start | bytes 221192
  1694.7 68.7 %collective-permute-start.73 = (f32[8,2304]{1,0:T(8,128)}, f32[8,2304]{1,0:T(8,128)}, u32[]{:S(2)}, u32[]{:S(2)}) collective-permute-start(f32[8,2304]{1,0:T(8,128)} %get-tuple-element.176), channel_id=1, source_target_pairs={{0,6},{1,7},{2,8},{3,9},{4,10},{5,11},{6,12},{7,13},{8,14},{9,15},... | collective-permute-start | bytes 221192
  1750.5 18.0 collective-permute-start.72
  (302 other events, 13610.0 us)
where the time goes:
time: 1850 us; the launch traced here: 1830 us
  blocking collectives  655 us (35%)
  local copies, waits for them, and re-layouts  469 us (25%)
  starting transfers between devices  406 us (22%)
  matrix products  126 us (7%)
  other arithmetic  112 us (6%)
  waiting for transfers between devices  53.6 us (3%)
    unnamed x2, blocking collectives  655 us
    unnamed x128, starting transfers between devices  357 us
    unnamed x348, local copies, waits for them, and re-layouts  172 us
    while x80, local copies, waits for them, and re-layouts  103 us
    dot_general x24, matrix products, spatial_core(): jnp.einsum('bqhd,bkhd->bhqk', query_blocks, padded[offset:offset + blocks...  43 us
    slice x4, local copies, waits for them, and re-layouts, spatial_core(): padded[offset:offset + blocks, :, 1]  40.1 us
    reshape x4, local copies, waits for them, and re-layouts, spatial_core(): padded = padded.reshape(blocks + 2, span_keys, 2, head_count, HDIM)  38.2 us
  transfers between devices with their start and end apart: 136, of which 8 were waited for; matrix products, arithmetic and copies ran while one was open for 20% of the time, Pallas kernels for 0%

commit v1 on v0

v1 whole, which is shorter than its diff:
```python
import functools
import math

import jax
import jax.numpy as jnp
from jax import lax
from jax.experimental import pallas as pl
from jax.experimental.pallas import tpu as pltpu
from jax.sharding import Mesh
from jax.sharding import PartitionSpec as P

HDIM = 64
BH = 8
LANES = 4 * HDIM
EPS = 1e-05
F32 = jnp.float32
BF16 = jnp.bfloat16
TILE = ("xlo", "y", "core")
FRAME = ("z", "xhi")
VMEM_LIMIT = 56 * 1024 * 1024


def dot(left, right, left_dim=1, right_dim=0):
    return lax.dot_general(
        left, right, (((left_dim,), (right_dim,)), ((), ())), preferred_element_type=F32
    )


def normalized(rows):
    centred = rows - jnp.mean(rows, axis=-1, keepdims=True)
    variance = jnp.mean(centred * centred, axis=-1, keepdims=True)
    inverse = lax.rsqrt(variance + EPS)
    return centred * inverse, inverse


def norm_back(unit, inverse, gain, d_out):
    d_unit = d_out * gain
    along = jnp.mean(d_unit * unit, axis=-1, keepdims=True)
    return inverse * (d_unit - jnp.mean(d_unit, axis=-1, keepdims=True) - unit * along)


def head_mask(rows):
    row_head = lax.broadcasted_iota(jnp.int32, (4 * rows, LANES), 0) // rows
    lane_head = lax.broadcasted_iota(jnp.int32, (4 * rows, LANES), 1) // HDIM
    return row_head == lane_head


def spread(group, mask):
    stacked = jnp.concatenate([group] * 4, axis=0)
    return jnp.where(mask, stacked, jnp.zeros_like(stacked))


def gathered(wide, rows):
    lane_head = lax.broadcasted_iota(jnp.int32, (rows, LANES), 1) // HDIM
    parts = [wide[h * rows : (h + 1) * rows] for h in range(4)]
    low = jnp.where(lane_head == 0, parts[0], parts[1])
    high = jnp.where(lane_head == 2, parts[2], parts[3])
    return jnp.where(lane_head < 2, low, high)


def softmax_rows(scores):
    top = jnp.max(scores, axis=0, keepdims=True)
    exponent = jnp.exp(scores - top)
    return exponent * (1.0 / jnp.sum(exponent, axis=0, keepdims=True))


def key_ranges(blocks, step):
    return [(max(b - 1, 0) * step, min(b + 2, blocks) * step) for b in range(blocks)]


def spatial_forward_kernel(
    own_ref, west_ref, east_ref, gain_ref, qkv_ref, out_ref,
    y_ref, q_ref, kv_ref, p_ref, o_ref, mid_ref,
):
    _, lat, width, features = own_ref.shape
    rows = BH * width
    blocks = lat // BH
    step = 3 * rows
    gain = gain_ref[...]
    for tile, ref in enumerate((west_ref, own_ref, east_ref)):
        wide = ref[0].astype(F32).reshape(lat * width, features)
        unit, _ = normalized(wide)
        y = (unit * gain).astype(BF16)
        for b in range(blocks):
            at = b * step + tile * rows
            y_ref[0, at : at + rows] = y[b * rows : (b + 1) * rows]
        if tile == 1:
            q_ref[0] = (dot(y, qkv_ref[:, :features]).astype(BF16) * HDIM ** (-0.5)).astype(BF16)
    for b in range(blocks):
        part = slice(b * step, (b + 1) * step)
        kv_ref[0, part] = dot(y_ref[0, part], qkv_ref[:, features:]).astype(BF16)
    mask = head_mask(rows)
    offset = 0
    for b, (low, high) in enumerate(key_ranges(blocks, step)):
        span = high - low
        for g in range(features // LANES):
            lanes = slice(g * LANES, (g + 1) * LANES)
            queries = spread(q_ref[0, b * rows : (b + 1) * rows, lanes], mask)
            keys = kv_ref[0, low:high, lanes]
            values = kv_ref[0, low:high, features + g * LANES : features + (g + 1) * LANES]
            weights = softmax_rows(dot(keys, queries, 1, 1)).astype(BF16)
            p_ref[0, g, offset : offset + span] = weights
            mixed = dot(weights, values, 0, 0)
            o_ref[0, b * rows : (b + 1) * rows, lanes] = gathered(mixed, rows).astype(BF16)
        offset += span
    wide = own_ref[0].astype(F32).reshape(lat * width, features)
    mid = wide + dot(o_ref[0], out_ref[...])
    mid_ref[0] = mid.reshape(lat, width, features).astype(BF16)


def full(shape):
    return pl.BlockSpec(shape, lambda *_: (0,) * len(shape))


def per_step(shape):
    return pl.BlockSpec((1,) + shape, lambda i: (i,) + (0,) * len(shape))


def spatial_forward(own, west, east, gain, qkv, out):
    frames, lat, width, features = own.shape
    rows = lat * width
    blocks = lat // BH
    spans = sum(h - l for l, h in key_ranges(blocks, 3 * BH * width))
    groups = features // LANES
    outs = (
        ((3 * rows, features), BF16),
        ((rows, features), BF16),
        ((3 * rows, 2 * features), BF16),
        ((groups, spans, LANES), BF16),
        ((rows, features), BF16),
        ((lat, width, features), BF16),
    )
    return pl.pallas_call(
        spatial_forward_kernel,
        grid=(frames,),
        in_specs=[per_step((lat, width, features))] * 3
        + [full((1, features)), full(qkv.shape), full(out.shape)],
        out_specs=[per_step(shape) for shape, _ in outs],
        out_shape=[jax.ShapeDtypeStruct((frames,) + shape, kind) for shape, kind in outs],
        compiler_params=pltpu.CompilerParams(vmem_limit_bytes=VMEM_LIMIT),
        name="spatial_forward",
    )(own, west, east, gain, qkv, out)


def temporal_kernel(
    mid_ref, cot_ref, gain_ref, qkv_ref, out_ref,
    layer_ref, dmid_ref, y_ref, dpacked_ref, o_ref,
    packed_ref, dproj_ref,
):
    frames, _, width, features = mid_ref.shape
    rows = frames * width
    gain = gain_ref[...]
    mid = mid_ref[:, 0].astype(F32).reshape(rows, features)
    cot = cot_ref[:, 0].astype(F32).reshape(rows, features)
    unit, inverse = normalized(mid)
    y = (unit * gain).astype(BF16)
    y_ref[...] = y
    packed_ref[...] = dot(y, qkv_ref[...]).astype(BF16)
    dproj_ref[...] = dot(cot.astype(BF16), out_ref[...], 1, 1).astype(BF16)
    mask = head_mask(rows)
    key_col = lax.broadcasted_iota(jnp.int32, (rows, 4 * rows), 0) % width
    query_col = lax.broadcasted_iota(jnp.int32, (rows, 4 * rows), 1) % width
    same = key_col == query_col
    scale = HDIM ** (-0.5)
    for g in range(features // LANES):
        lanes = [slice(s * features + g * LANES, s * features + (g + 1) * LANES) for s in range(3)]
        queries = spread((packed_ref[:, lanes[0]] * scale).astype(BF16), mask)
        keys = packed_ref[:, lanes[1]]
        values = packed_ref[:, lanes[2]]
        scores = jnp.where(same, dot(keys, queries, 1, 1), -1e30)
        wide = softmax_rows(scores)
        weights = wide.astype(BF16)
        mixed = dot(weights, values, 0, 0)
        o_ref[:, lanes[0]] = gathered(mixed, rows).astype(BF16)
        d_out = spread(dproj_ref[:, lanes[0]], mask)
        d_weights = dot(values, d_out, 1, 1)
        delta = jnp.sum(wide * d_weights, axis=0, keepdims=True)
        d_scores = (wide * (d_weights - delta)).astype(BF16)
        d_query = gathered(dot(d_scores, keys, 0, 0), rows) * scale
        dpacked_ref[:, lanes[0]] = d_query.astype(BF16)
        dpacked_ref[:, lanes[1]] = dot(d_scores, queries).astype(BF16)
        dpacked_ref[:, lanes[2]] = dot(weights, d_out).astype(BF16)
    layer = mid + dot(o_ref[...], out_ref[...])
    layer_ref[:, 0] = layer.reshape(frames, width, features).astype(BF16)
    d_y = dot(dpacked_ref[...], qkv_ref[...], 1, 1)
    d_mid = cot + norm_back(unit, inverse, gain, d_y)
    dmid_ref[:, 0] = d_mid.reshape(frames, width, features).astype(BF16)


def temporal(mid, cot, gain, qkv, out):
    frames, lat, width, features = mid.shape
    rows = frames * width
    moved = pl.BlockSpec((frames, 1, width, features), lambda i: (0, i, 0, 0))

    def flat(columns):
        return pl.BlockSpec((rows, columns), lambda i: (i, 0))

    return pl.pallas_call(
        temporal_kernel,
        grid=(lat,),
        in_specs=[moved, moved, full((1, features)), full(qkv.shape), full(out.shape)],
        out_specs=[moved, moved, flat(features), flat(3 * features), flat(features)],
        out_shape=[
            jax.ShapeDtypeStruct(mid.shape, BF16),
            jax.ShapeDtypeStruct(mid.shape, BF16),
            jax.ShapeDtypeStruct((lat * rows, features), BF16),
            jax.ShapeDtypeStruct((lat * rows, 3 * features), BF16),
            jax.ShapeDtypeStruct((lat * rows, features), BF16),
        ],
        scratch_shapes=[
            pltpu.VMEM((rows, 3 * features), BF16),
            pltpu.VMEM((rows, features), BF16),
        ],
        compiler_params=pltpu.CompilerParams(vmem_limit_bytes=VMEM_LIMIT),
        name="temporal",
    )(mid, cot, gain, qkv, out)


def spatial_backward_kernel(
    dmid_ref, out_ref, qkv_ref, q_ref, kv_ref, p_ref,
    dq_ref, dkv_ref, own_ref, west_ref, east_ref,
    dproj_ref, acc_ref,
):
    _, lat, width, features = dmid_ref.shape
    rows = BH * width
    blocks = lat // BH
    step = 3 * rows
    dmid = dmid_ref[0].astype(F32).reshape(lat * width, features).astype(BF16)
    dproj_ref[...] = dot(dmid, out_ref[...], 1, 1).astype(BF16)
    mask = head_mask(rows)
    acc_ref[...] = jnp.zeros_like(acc_ref)
    offset = 0
    for b, (low, high) in enumerate(key_ranges(blocks, step)):
        span = high - low
        block = slice(b * rows, (b + 1) * rows)
        for g in range(features // LANES):
            lanes = slice(g * LANES, (g + 1) * LANES)
            late = slice(features + g * LANES, features + (g + 1) * LANES)
            queries = spread(q_ref[0, block, lanes], mask)
            d_out = spread(dproj_ref[block, lanes], mask)
            keys = kv_ref[0, low:high, lanes]
            values = kv_ref[0, low:high, late]
            weights = p_ref[0, g, offset : offset + span]
            wide = weights.astype(F32)
            d_weights = dot(values, d_out, 1, 1)
            delta = jnp.sum(wide * d_weights, axis=0, keepdims=True)
            d_scores = (wide * (d_weights - delta)).astype(BF16)
            d_query = gathered(dot(d_scores, keys, 0, 0), rows) * HDIM ** (-0.5)
            dq_ref[0, block, lanes] = d_query.astype(BF16)
            acc_ref[low:high, lanes] += dot(d_scores, queries)
            acc_ref[low:high, late] += dot(weights, d_out)
        offset += span
    dkv_ref[0] = acc_ref[...].astype(BF16)
    for b in range(blocks):
        part = slice(b * step, (b + 1) * step)
        d_y = dot(dkv_ref[0, part], qkv_ref[:, features:], 1, 1)
        block = slice(b * rows, (b + 1) * rows)
        d_own = d_y[rows : 2 * rows] + dot(dq_ref[0, block], qkv_ref[:, :features], 1, 1)
        for ref, value in ((west_ref, d_y[:rows]), (own_ref, d_own), (east_ref, d_y[2 * rows :])):
            ref[0, b * BH : (b + 1) * BH] = value.reshape(BH, width, features).astype(BF16)


def spatial_backward(dmid, out, qkv, q, kv, p):
    frames, lat, width, features = dmid.shape
    rows = lat * width
    outs = (
        (rows, features),
        (3 * rows, 2 * features),
        (lat, width, features),
        (lat, width, features),
        (lat, width, features),
    )
    return pl.pallas_call(
        spatial_backward_kernel,
        grid=(frames,),
        in_specs=[
            per_step((lat, width, features)),
            full(out.shape),
            full(qkv.shape),
            per_step(q.shape[1:]),
            per_step(kv.shape[1:]),
            per_step(p.shape[1:]),
        ],
        out_specs=[per_step(shape) for shape in outs],
        out_shape=[jax.ShapeDtypeStruct((frames,) + shape, BF16) for shape in outs],
        scratch_shapes=[
            pltpu.VMEM((rows, features), BF16),
            pltpu.VMEM((3 * rows, 2 * features), F32),
        ],
        compiler_params=pltpu.CompilerParams(vmem_limit_bytes=VMEM_LIMIT),
        name="spatial_backward",
    )(dmid, out, qkv, q, kv, p)


def final_kernel(tokens_ref, gain_ref, dmid_ref, own_ref, first_ref, second_ref, grad_ref):
    _, lat, width, features = tokens_ref.shape

    def flat(ref):
        return ref[0].astype(F32).reshape(lat * width, features)

    unit, inverse = normalized(flat(tokens_ref))
    d_y = flat(own_ref) + flat(first_ref) + flat(second_ref)
    grad = flat(dmid_ref) + norm_back(unit, inverse, gain_ref[...], d_y)
    grad_ref[0] = grad.reshape(lat, width, features)


def final_norm(tokens, gain, dmid, own, first, second):
    frames, lat, width, features = tokens.shape
    block = per_step((lat, width, features))
    return pl.pallas_call(
        final_kernel,
        grid=(frames,),
        in_specs=[block, full((1, features))] + [block] * 4,
        out_specs=block,
        out_shape=jax.ShapeDtypeStruct(tokens.shape, F32),
        compiler_params=pltpu.CompilerParams(vmem_limit_bytes=VMEM_LIMIT),
        name="final_norm",
    )(tokens, gain, dmid, own, first, second)


def exchanged_sum(parts, axis):
    arrived = lax.all_to_all(parts, axis, 0, 0, tiled=False)
    return jnp.sum(arrived.astype(F32), axis=0)


def scattered(term):
    columns = term.shape[1]
    cores = lax.axis_size("core")
    core = lax.axis_index("core")
    tiles = lax.axis_size(TILE)
    frames = lax.axis_size(FRAME)
    per_tile = term.shape[0] // tiles
    pairs = term.reshape(tiles // cores, cores, per_tile, columns)
    keep = lax.dynamic_index_in_dim(pairs, core, 1, keepdims=False)
    send = lax.dynamic_index_in_dim(pairs, 1 - core, 1, keepdims=False)
    got = lax.ppermute(send.astype(BF16), "core", [(0, 1), (1, 0)])
    mine = (keep.astype(F32) + got.astype(F32)).astype(BF16)
    summed = exchanged_sum(mine, ("xlo", "y")).astype(BF16)
    return exchanged_sum(summed.reshape(frames, per_tile // frames, columns), FRAME)


def shifted(shard, by):
    size = lax.axis_size(TILE)
    return lax.ppermute(shard, TILE, [(i, (i + by) % size) for i in range(size)])


def own_rows(weight):
    count = lax.axis_size(TILE + FRAME)
    per_device = weight.shape[0] // count
    at = lax.axis_index(TILE + FRAME) * per_device
    return lax.dynamic_slice_in_dim(weight, at, per_device, axis=0).astype(F32)


def finished(summed, qkv, gain, total):
    features, wide = qkv.shape
    d_qkv = summed[:, :wide]
    d_out = summed[:, wide:]
    scale = 1.0 / math.sqrt(total)
    d_gain = jnp.sum(own_rows(qkv) * d_qkv, axis=1) / own_rows(gain)
    return d_gain * scale, d_qkv * scale, d_out * scale


def shards(tokens, gain_space, qkv_space, out_space, gain_time, qkv_time, out_time, cotangent):
    frames, lat, width, features = tokens.shape
    total = frames * lat * width * lax.axis_size(TILE) * lax.axis_size(FRAME)
    gain_s = gain_space.reshape(1, features)
    gain_t = gain_time.reshape(1, features)

    def to_rows(shard):
        return lax.all_to_all(shard, FRAME, split_axis=1, concat_axis=0, tiled=True)

    def to_frames(shard):
        return lax.all_to_all(shard, FRAME, split_axis=0, concat_axis=1, tiled=True)

    west = shifted(tokens, 1)
    east = shifted(tokens, -1)
    cot_rows = to_rows(cotangent)
    y_s, q_s, kv_s, p_s, o_s, mid = spatial_forward(tokens, west, east, gain_s, qkv_space, out_space)
    layer_rows, dmid_rows, y_t, dpacked_t, o_t = temporal(
        to_rows(mid), cot_rows, gain_t, qkv_time, out_time
    )
    dmid = to_frames(dmid_rows)
    layer_out = to_frames(layer_rows)
    cot_flat = cot_rows.transpose(1, 0, 2, 3).reshape(-1, features)
    term_time = jnp.concatenate([dot(y_t, dpacked_t, 0, 0), dot(o_t, cot_flat, 0, 0)], axis=1)
    summed_time = scattered(term_time)
    dq, dkv, own, for_west, for_east = spatial_backward(dmid, out_space, qkv_space, q_s, kv_s, p_s)
    from_east = shifted(for_west, -1)
    from_west = shifted(for_east, 1)
    rows = lat * width
    y_ext = y_s.reshape(-1, features)
    y_own = y_s.reshape(frames, lat // BH, 3, BH * width, features)[:, :, 1].reshape(-1, features)
    term_space = jnp.concatenate(
        [
            dot(y_own, dq.reshape(-1, features), 0, 0),
            dot(y_ext, dkv.reshape(-1, 2 * features), 0, 0),
            dot(o_s.reshape(-1, features), dmid.reshape(-1, features), 0, 0),
        ],
        axis=1,
    )
    summed_space = scattered(term_space)
    grad_tokens = final_norm(tokens, gain_s, dmid, own, from_east, from_west)
    return (
        (layer_out, grad_tokens)
        + finished(summed_space, qkv_space, gain_space, total)
        + finished(summed_time, qkv_time, gain_time, total)
    )


def solution(mesh):
    fine = Mesh(mesh.devices.reshape(2, 4, 2, 4, 2), TILE + FRAME)
    token_spec = P(FRAME, None, TILE, None)
    row_spec = P(TILE + FRAME)
    return jax.shard_map(
        shards,
        mesh=fine,
        in_specs=(token_spec, P(), P(), P(), P(), P(), P(), token_spec),
        out_specs=(token_spec, token_spec) + (row_spec,) * 6,
        check_vma=False,
    )
```

time: 1850 us -> 265 us (0.14)
  blocking collectives: 655 us -> 0 us
  local copies, waits for them, and re-layouts: 469 us -> 21.1 us
  starting transfers between devices: 406 us -> 52.3 us
  matrix products: 126 us -> 15 us
  other arithmetic: 112 us -> 34 us
  Pallas kernels: 0 us -> 54.9 us
  waiting for transfers between devices: 53.6 us -> 83.2 us
    unnamed x2 -> x0, blocking collectives: 655 us -> none
    unnamed x128 -> x0, starting transfers between devices: 357 us -> none
    unnamed x348 -> x23, local copies, waits for them, and re-layouts: 172 us -> 3.77 us
    dot_general x60 -> x5, matrix products: 126 us -> 15 us  [dot(): lax.dot_general(left, right, (((left_dim,), (right_dim,)), ((), ())), pre...]
    while x80 -> x0, local copies, waits for them, and re-layouts: 103 us -> none
    reshape x16 -> x4, local copies, waits for them, and re-layouts: 59.2 us -> 3.55 us  [the longest x2 1.7 us: scattered(): summed.reshape(frames, per_tile // frames, columns)]
    pallas_call x0 -> x4, Pallas kernels: none -> 54.9 us  [the longest x1 19.4 us: spatial_backward(): pl.pallas_call(spatial_backward_kernel, grid=(frames,), in_specs=[per_ste...]
    slice x8 -> x1, local copies, waits for them, and re-layouts: 48.4 us -> 1.1 us  [shards(): y_s.reshape(frames, lat // BH, 3, BH * width, features)[:, :, 1]]
  transfers between devices with their start and end apart: 136 -> 14, of which waited for: 8 -> 6; matrix products, arithmetic and copies ran while one was open for 20% -> 22% of each run, Pallas kernels for 0% -> 14%
where the time goes in v1:
time: 265 us; the launch traced here: 261 us
  waiting for transfers between devices  83.2 us (31%)
  Pallas kernels  54.9 us (21%)
  starting transfers between devices  52.3 us (20%)
  other arithmetic  34 us (13%)
  local copies, waits for them, and re-layouts  21.1 us (8%)
  matrix products  15 us (6%)
    all_to_all x4, waiting for transfers between devices, exchanged_sum(): arrived = lax.all_to_all(parts, axis, 0, 0, tiled=False)  35 us
    ppermute x4, waiting for transfers between devices, shifted(): lax.ppermute(shard, TILE, [(i, (i + by) % size) for i in range(size)])  29.3 us
    pallas_call x1, Pallas kernels, spatial_backward(): pl.pallas_call(spatial_backward_kernel, grid=(frames,), in_specs=[per_ste...  19.4 us
    pallas_call x1, Pallas kernels, temporal(): pl.pallas_call(temporal_kernel, grid=(lat,), in_specs=[moved, moved, full...  18 us
    all_to_all x4, starting transfers between devices, exchanged_sum(): arrived = lax.all_to_all(parts, axis, 0, 0, tiled=False)  15.4 us
    dot_general x5, matrix products, dot(): lax.dot_general(left, right, (((left_dim,), (right_dim,)), ((), ())), pre...  15 us
    pallas_call x1, Pallas kernels, spatial_forward(): pl.pallas_call(spatial_forward_kernel, grid=(frames,), in_specs=[per_step...  14.3 us
    all_to_all x2, starting transfers between devices, to_rows(): return lax.all_to_all(shard, FRAME, split_axis=1, concat_axis=0, tiled=True)  14.1 us
  transfers between devices with their start and end apart: 14, of which 6 were waited for; matrix products, arithmetic and copies ran while one was open for 22% of the time, Pallas kernels for 14%

profile of v1, /device:TPU:1, one launch (start us, length us, event | category | flops | bytes accessed | tf_op | source)
XLA Modules:
  0.0 261.4 jit_solution(17436060881128312106)
XLA Ops:
  0.6 2.8 %collective-permute-start = (bf16[2,24,8,768]{3,2,1,0:T(8,128)(2,1)}, bf16[2,24,8,768]{3,2,1,0:T(8,128)(2,1)S(1)}, u32[]{:S(2)}, u32[]{:S(2)}) collective-permute-start(bf16[2,24,8,768]{3,2,1,0:T(8,128)(2,1)} %tokens_ref.1), channel_id=1, source_target_pairs={{0,8},{8,16},{16,24},{24,32},{32,40},{40,48},{48,56},{56,64},{64,7... | collective-permute-start | bytes 1769480 | tf_op jit(solution)/shard_map/ppermute | solution.py:344
  5.3 7.5 %all-to-all-start.1 = ((bf16[2,24,8,768]{3,2,0,1:T(8,128)(2,1)}), bf16[2,24,8,768]{3,2,0,1:T(8,128)(2,1)S(1)}, u32[]{:S(2)}, u32[]{:S(2)}) async-start(bf16[2,24,8,768]{3,2,0,1:T(8,128)(2,1)} %copy.33), calls=%async_computation.1 | async-start | bytes 1179648 | tf_op jit(solution)/shard_map/all_to_all | solution.py:370
  15.7 14.3 %spatial_forward.1 = (bf16[2,576,768]{2,1,0:T(8,128)(2,1)}, bf16[2,192,768]{2,1,0:T(8,128)(2,1)}, bf16[2,576,1536]{2,1,0:T(8,128)(2,1)}, bf16[2,3,1344,256]{3,2,...) custom-call(bf16[2,24,8,768]{3,2,1,0:T(8,128)(2,1)} %tokens_ref.1, ...), custom_call_target="tpu_custom_call" | custom-call | tf_op jit(solution)/shard_map/spatial_forward/pallas_call | solution.py:133
  30.0 1.9 copy.31
  31.9 6.6 %all-to-all-start = ((bf16[2,24,8,768]{3,2,0,1:T(8,128)(2,1)}), bf16[2,24,8,768]{3,2,0,1:T(8,128)(2,1)S(1)}, u32[]{:S(2)}, u32[]{:S(2)}) async-start(bf16[2,24,8,768]{3,2,0,1:T(8,128)(2,1)} %copy.31), calls=%async_computation | async-start | bytes 1179648 | tf_op jit(solution)/shard_map/all_to_all | solution.py:370
  39.2 8.8 %all-to-all-done = bf16[2,24,8,768]{3,2,0,1:T(8,128)(2,1)S(1)} async-done(((bf16[2,24,8,768]{3,2,0,1:T(8,128)(2,1)}), bf16[2,24,8,768]{3,2,0,1:T(8,128)(2,1)S(1)}, u32[]{:S(2)}, u32[]{:S(2)}) %all-to-all-start) | async-done | bytes 589856 | tf_op jit(solution)/shard_map/all_to_all | solution.py:370
  48.9 18.0 %temporal.1 = (bf16[16,3,8,768]{3,2,1,0:T(8,128)(2,1)}, bf16[16,3,8,768]{3,2,1,0:T(8,128)(2,1)}, bf16[384,768]{1,0:T(8,128)(2,1)}, bf16[384,2304]{1,0:T(8,128)(2,1)}, bf16[384,768]{1,0:T(8,128)(2,1)}) custom-call(bf16[16,3,8,768]{3,2,1,0:T(8,128)(2,1)} %bitcast.60, bf16[16,3,8,768]{3,2,1,0:T(8,128)(2,1)} %bitcast.59, f32[1,768]{1,0:T(1,128)} %reshape.55.gain_ref, ...), custom_call_target="tpu_custom_call" | custom-call | tf_op jit(solution)/shard_map/temporal/pallas_call | solution.py:198
  66.9 3.9 %all-to-all-start.3 = ((bf16[16,3,8,768]{3,2,1,0:T(8,128)(2,1)}), bf16[16,3,8,768]{3,2,1,0:T(8,128)(2,1)S(1)}, u32[]{:S(2)}, u32[]{:S(2)}) async-start(bf16[16,3,8,768]{3,2,1,0:T(8,128)(2,1)} %get-tuple-element.26), calls=%async_computation.3 | async-start | bytes 1179648 | tf_op jit(solution)/shard_map/all_to_all | solution.py:373
  70.8 2.0 fusion.9
  72.8 4.9 %fusion.8 = f32[768,2304]{1,0:T(8,128)} fusion(bf16[384,768]{1,0:T(8,128)(2,1)S(1)} %copy-done.5, bf16[384,2304]{1,0:T(8,128)(2,1)S(1)} %copy-done.2), kind=kOutput, calls=%fused_computation.25 | convolution fusion | flops 1358954496 | bytes 9437184 | tf_op jit(solution)/shard_map/dot_general | solution.py:24
  77.7 8.0 %pad_maximum_fusion.1 = f32[768,3072]{1,0:T(8,128)} fusion(f32[768,768]{1,0:T(8,128)S(1)} %fusion.9, f32[768,2304]{1,0:T(8,128)} %fusion.8), kind=kLoop, calls=%fused_computation.1 | loop fusion | flops 2359296 | bytes 18874368 | tf_op jit(solution)/shard_map/concatenate | solution.py:385
  85.7 4.0 %fusion.3 = bf16[8,48,3072]{2,1,0:T(8,128)(2,1)} fusion(f32[8,2,48,3072]{3,2,1,0:T(8,128)} %bitcast.53, s32[]{:T(128)S(6)} %select_n.17), kind=kLoop, calls=%fused_computation.10 | loop fusion | bytes 4718596 | tf_op jit(solution)/shard_map/convert_element_type | solution.py:336
  89.8 4.5 %collective-permute-start.5 = (bf16[8,48,3072]{2,1,0:T(8,128)(2,1)}, bf16[8,48,3072]{2,1,0:T(8,128)(2,1)}, u32[]{:S(2)}, u32[]{:S(2)}) collective-permute-start(bf16[8,48,3072]{2,1,0:T(8,128)(2,1)} %fusion.3), channel_id=1, source_target_pairs={{0,8},{8,0},{1,9},{9,1},{2,10},{10,2},{3,11},{11,3},{4,12},{12,4},... | collective-permute-start | bytes 7077896 | tf_op jit(solution)/shard_map/ppermute | solution.py:336
  96.3 19.4 %spatial_backward.1 = (bf16[2,192,768]{2,1,0:T(8,128)(2,1)}, bf16[2,576,1536]{2,1,0:T(8,128)(2,1)}, bf16[2,24,8,768]{3,2,1,0:T(8,128)(2,1)}, bf16[2,24,8,768]{3,2,1,0:T(8,128)(2,1)}, bf16[2,24,8,768]{3,2,1,0:T(8,128)(2,1)}) custom-call(bf16[2,24,8,768]{3,2,1,0:T(8,128)(2,1)} %bitcast.55, bf16[768,768]{1,0:T(8,128)(2,1)} %out_ref.5, ...), custom_call_target="tpu_custom_call" | custom-call | tf_op jit(solution)/shard_map/spatial_backward/pallas_call | solution.py:273
  116.7 2.2 fusion.6
  118.9 5.1 %convolution_bitcast_fusion = f32[768,1536]{1,0:T(8,128)} fusion(bf16[2,576,768]{2,1,0:T(8,128)(2,1)S(1)} %copy-done.8, bf16[2,576,1536]{2,1,0:T(8,128)(2,1)S(1)} %copy-done.10), kind=kOutput, calls=%fused_computation.8 | convolution fusion | flops 2717908992 | bytes 10027008 | tf_op jit(solution)/shard_map/dot_general | solution.py:24
  124.0 8.2 %pad_maximum_fusion = f32[768,3072]{1,0:T(8,128)} fusion(f32[768,768]{1,0:T(8,128)S(1)} %fusion.7, f32[768,1536]{1,0:T(8,128)} %convolution_bitcast_fusion, f32[768,768]{1,0:T(8,128)} %fusion.6), kind=kLoop, calls=%fused_computation | loop fusion | flops 4718592 | bytes 18874368 | tf_op jit(solution)/shard_map/concatenate | solution.py:393
  132.2 5.2 %fusion = bf16[8,48,3072]{2,1,0:T(8,128)(2,1)} fusion(bf16[8,48,3072]{2,1,0:T(8,128)(2,1)} %collective-permute-done.5, f32[8,2,48,3072]{3,2,1,0:T(8,128)} %bitcast.54, s32[]{:T(128)S(6)} %select_n.16), kind=kLoop, calls=%fused_computation.3 | loop fusion | flops 3538944 | bytes 9437188 | tf_op jit(solution)/shard_map/convert_element_type | solution.py:337
  137.4 4.6 %all-to-all-start.6 = ((bf16[8,48,3072]{2,1,0:T(8,128)(2,1)}), bf16[8,48,3072]{2,1,0:T(8,128)(2,1)S(1)}, u32[]{:S(2)}, u32[]{:S(2)}) async-start(bf16[8,48,3072]{2,1,0:T(8,128)(2,1)} %fusion), calls=%async_computation.6 | async-start | bytes 4718592 | tf_op jit(solution)/shard_map/all_to_all | solution.py:322
  142.0 4.1 %fusion.2 = bf16[8,48,3072]{2,1,0:T(8,128)(2,1)} fusion(f32[8,2,48,3072]{3,2,1,0:T(8,128)} %bitcast.51, s32[]{:T(128)S(6)} %select_n.17), kind=kLoop, calls=%fused_computation.9 | loop fusion | bytes 4718596 | tf_op jit(solution)/shard_map/convert_element_type | solution.py:336
  146.4 24.6 %all-to-all-done.6 = bf16[8,48,3072]{2,1,0:T(8,128)(2,1)S(1)} async-done(((bf16[8,48,3072]{2,1,0:T(8,128)(2,1)}), bf16[8,48,3072]{2,1,0:T(8,128)(2,1)S(1)}, u32[]{:S(2)}, u32[]{:S(2)}) %all-to-all-start.6) | async-done | bytes 2359328 | tf_op jit(solution)/shard_map/all_to_all | solution.py:322
  171.1 6.9 %all-to-all-start.2 = ((bf16[16,3,8,768]{3,2,1,0:T(8,128)(2,1)}), bf16[16,3,8,768]{3,2,1,0:T(8,128)(2,1)S(1)}, u32[]{:S(2)}, u32[]{:S(2)}) async-start(bf16[16,3,8,768]{3,2,1,0:T(8,128)(2,1)} %get-tuple-element.25), calls=%async_computation.2 | async-start | bytes 1179648 | tf_op jit(solution)/shard_map/all_to_all | solution.py:373
  179.2 10.0 %all-to-all-done.2 = bf16[16,3,8,768]{3,2,1,0:T(8,128)(2,1)S(1)} async-done(((bf16[16,3,8,768]{3,2,1,0:T(8,128)(2,1)}), bf16[16,3,8,768]{3,2,1,0:T(8,128)(2,1)S(1)}, u32[]{:S(2)}, u32[]{:S(2)}) %all-to-all-start.2) | async-done | bytes 589856 | tf_op jit(solution)/shard_map/all_to_all | solution.py:373
  189.3 3.7 %all-to-all-start.7 = ((bf16[8,6,3072]{2,1,0:T(8,128)(2,1)}), bf16[8,6,3072]{2,1,0:T(8,128)(2,1)S(1)}, u32[]{:S(2)}, u32[]{:S(2)}) async-start(bf16[8,6,3072]{2,1,0:T(8,128)(2,1)} %reshape.64), calls=%async_computation.7 | async-start | bytes 786432 | tf_op jit(solution)/shard_map/all_to_all | solution.py:322
  193.0 5.2 %fusion.1 = bf16[8,48,3072]{2,1,0:T(8,128)(2,1)} fusion(bf16[8,48,3072]{2,1,0:T(8,128)(2,1)} %collective-permute-done.4, f32[8,2,48,3072]{3,2,1,0:T(8,128)} %bitcast.52, s32[]{:T(128)S(6)} %select_n.16), kind=kLoop, calls=%fused_computation.5 | loop fusion | flops 3538944 | bytes 9437188 | tf_op jit(solution)/shard_map/convert_element_type | solution.py:337
  198.2 3.1 %all-to-all-done.7 = bf16[8,6,3072]{2,1,0:T(8,128)(2,1)S(1)} async-done(((bf16[8,6,3072]{2,1,0:T(8,128)(2,1)}), bf16[8,6,3072]{2,1,0:T(8,128)(2,1)S(1)}, u32[]{:S(2)}, u32[]{:S(2)}) %all-to-all-start.7) | async-done | bytes 294944 | tf_op jit(solution)/shard_map/all_to_all | solution.py:322
  201.3 3.6 %all-to-all-start.4 = ((bf16[8,48,3072]{2,1,0:T(8,128)(2,1)}), bf16[8,48,3072]{2,1,0:T(8,128)(2,1)S(1)}, u32[]{:S(2)}, u32[]{:S(2)}) async-start(bf16[8,48,3072]{2,1,0:T(8,128)(2,1)} %fusion.1), calls=%async_computation.4 | async-start | bytes 4718592 | tf_op jit(solution)/shard_map/all_to_all | solution.py:322
  204.9 2.9 %collective-permute-start.2 = (bf16[2,24,8,768]{3,2,1,0:T(8,128)(2,1)}, bf16[2,24,8,768]{3,2,1,0:T(8,128)(2,1)}, u32[]{:S(2)}, u32[]{:S(2)}) collective-permute-start(bf16[2,24,8,768]{3,2,1,0:T(8,128)(2,1)} %get-tuple-element.31), channel_id=1, source_target_pairs={{0,120},{8,0},{16,8},{24,16},{32,24},{40,32},{48,40},{56,48},{64,5... | collective-permute-start | bytes 1769480 | tf_op jit(solution)/shard_map/ppermute | solution.py:344
  210.1 29.3 %collective-permute-done.2.first_ref = bf16[2,24,8,768]{3,2,1,0:T(8,128)(2,1)} collective-permute-done((bf16[2,24,8,768]{3,2,1,0:T(8,128)(2,1)}, bf16[2,24,8,768]{3,2,1,0:T(8,128)(2,1)}, u32[]{:S(2)}, u32[]{:S(2)}) %collective-permute-start.2) | collective-permute-done | bytes 589856 | tf_op jit(solution)/shard_map/ppermute | solution.py:344
  239.4 3.3 %final_norm.1 = f32[2,24,8,768]{3,2,1,0:T(8,128)} custom-call(bf16[2,24,8,768]{3,2,1,0:T(8,128)(2,1)} %tokens_ref.1, f32[1,768]{1,0:T(1,128)} %reshape.54.gain_ref, bf16[2,24,8,768]{3,2,1,0:T(8,128)(2,1)} %bitcast.56, bf16[2,24,8,768]{3,2,1,0:T(8,128)(2,1)} %get-tuple-element.30.own_ref, bf16[2,24,8,768]{3,2,1,0:T(8,128)(2,1)} %collective-permute-done.2.first_ref, ...), custom_call_target="tpu_custom_call" | custom-call | tf_op jit(solution)/shard_map/final_norm/pallas_call | solution.py:310
  245.7 3.5 %all-to-all-start.5 = ((bf16[8,6,3072]{2,1,0:T(8,128)(2,1)}), bf16[8,6,3072]{2,1,0:T(8,128)(2,1)S(1)}, u32[]{:S(2)}, u32[]{:S(2)}) async-start(bf16[8,6,3072]{2,1,0:T(8,128)(2,1)} %reshape.61), calls=%async_computation.5 | async-start | bytes 786432 | tf_op jit(solution)/shard_map/all_to_all | solution.py:322
  250.5 7.3 %all-to-all-done.5 = bf16[8,6,3072]{2,1,0:T(8,128)(2,1)S(1)} async-done(((bf16[8,6,3072]{2,1,0:T(8,128)(2,1)}), bf16[8,6,3072]{2,1,0:T(8,128)(2,1)S(1)}, u32[]{:S(2)}, u32[]{:S(2)}) %all-to-all-start.5) | async-done | bytes 294944 | tf_op jit(solution)/shard_map/all_to_all | solution.py:322
  (55 shorter events, 21.0 us)
Async XLA Ops:
  0.6 13.4 %collective-permute-start = (bf16[2,24,8,768]{3,2,1,0:T(8,128)(2,1)}, bf16[2,24,8,768]{3,2,1,0:T(8,128)(2,1)S(1)}, u32[]{:S(2)}, u32[]{:S(2)}) collective-permute-start(bf16[2,24,8,768]{3,2,1,0:T(8,128)(2,1)} %tokens_ref.1), channel_id=1, source_target_pairs={{0,8},{8,16},{16,24},{24,32},{32,40},{40,48},{48,56},{56,64},{64,7... | collective-permute-start | bytes 1769480 | tf_op jit(solution)/shard_map/ppermute | solution.py:344
  3.4 10.7 %collective-permute-start.1 = (bf16[2,24,8,768]{3,2,1,0:T(8,128)(2,1)}, bf16[2,24,8,768]{3,2,1,0:T(8,128)(2,1)S(1)}, u32[]{:S(2)}, u32[]{:S(2)}) collective-permute-start(bf16[2,24,8,768]{3,2,1,0:T(8,128)(2,1)} %tokens_ref.1), channel_id=1, source_target_pairs={{0,120},{8,0},{16,8},{24,16},{32,24},{40,32},{48,40},{56,48},{64,5... | collective-permute-start | bytes 1769480 | tf_op jit(solution)/shard_map/ppermute | solution.py:344
  5.3 26.6 %all-to-all-start.1 = ((bf16[2,24,8,768]{3,2,0,1:T(8,128)(2,1)}), bf16[2,24,8,768]{3,2,0,1:T(8,128)(2,1)S(1)}, u32[]{:S(2)}, u32[]{:S(2)}) async-start(bf16[2,24,8,768]{3,2,0,1:T(8,128)(2,1)} %copy.33), calls=%async_computation.1 | async-start | bytes 1179648 | tf_op jit(solution)/shard_map/all_to_all | solution.py:370
  14.1 24.5 %copy-start.9 = (f32[768]{0:T(1024)S(1)}, f32[768]{0:T(1024)}, u32[]{:S(2)}) copy-start(f32[768]{0:T(1024)} %param.12) | copy-start | bytes 9220
  14.1 0.8 copy-start.3
  14.9 0.8 copy-start.4
  31.9 16.2 %all-to-all-start = ((bf16[2,24,8,768]{3,2,0,1:T(8,128)(2,1)}), bf16[2,24,8,768]{3,2,0,1:T(8,128)(2,1)S(1)}, u32[]{:S(2)}, u32[]{:S(2)}) async-start(bf16[2,24,8,768]{3,2,0,1:T(8,128)(2,1)} %copy.31), calls=%async_computation | async-start | bytes 1179648 | tf_op jit(solution)/shard_map/all_to_all | solution.py:370
  39.2 9.8 %copy-start.1 = (bf16[2,8,3,8,768]{4,3,2,0,1:T(8,128)(2,1)}, bf16[2,8,3,8,768]{4,3,2,0,1:T(8,128)(2,1)S(1)}, u32[]{:S(2)}) copy-start(bf16[2,8,3,8,768]{4,3,2,0,1:T(8,128)(2,1)S(1)} %copy.34) | copy-start | bytes 1769476
  66.9 5.9 %copy-start.5 = (bf16[384,768]{1,0:T(8,128)(2,1)S(1)}, bf16[384,768]{1,0:T(8,128)(2,1)}, u32[]{:S(2)}) copy-start(bf16[384,768]{1,0:T(8,128)(2,1)} %get-tuple-element.37) | copy-start | bytes 1769476
  66.9 28.5 %all-to-all-start.3 = ((bf16[16,3,8,768]{3,2,1,0:T(8,128)(2,1)}), bf16[16,3,8,768]{3,2,1,0:T(8,128)(2,1)S(1)}, u32[]{:S(2)}, u32[]{:S(2)}) async-start(bf16[16,3,8,768]{3,2,1,0:T(8,128)(2,1)} %get-tuple-element.26), calls=%async_computation.3 | async-start | bytes 1179648 | tf_op jit(solution)/shard_map/all_to_all | solution.py:373
  70.8 2.0 copy-start.2
  89.8 42.4 %collective-permute-start.5 = (bf16[8,48,3072]{2,1,0:T(8,128)(2,1)}, bf16[8,48,3072]{2,1,0:T(8,128)(2,1)}, u32[]{:S(2)}, u32[]{:S(2)}) collective-permute-start(bf16[8,48,3072]{2,1,0:T(8,128)(2,1)} %fusion.3), channel_id=1, source_target_pairs={{0,8},{8,0},{1,9},{9,1},{2,10},{10,2},{3,11},{11,3},{4,12},{12,4},... | collective-permute-start | bytes 7077896 | tf_op jit(solution)/shard_map/ppermute | solution.py:336
  96.3 19.4 %copy-start = (bf16[8,2,3,8,768]{4,3,2,0,1:T(8,128)(2,1)S(1)}, bf16[8,2,3,8,768]{4,3,2,0,1:T(8,128)(2,1)}, u32[]{:S(2)}) copy-start(bf16[8,2,3,8,768]{4,3,2,0,1:T(8,128)(2,1)} %copy.36) | copy-start | bytes 1769476
  96.3 19.4 %copy-start.6 = (bf16[2,192,768]{2,1,0:T(8,128)(2,1)S(1)}, bf16[2,192,768]{2,1,0:T(8,128)(2,1)}, u32[]{:S(2)}) copy-start(bf16[2,192,768]{2,1,0:T(8,128)(2,1)} %get-tuple-element.36) | copy-start | bytes 1769476
  115.7 1.1 copy-start.7
  115.7 3.3 %copy-start.8 = (bf16[2,576,768]{2,1,0:T(8,128)(2,1)S(1)}, bf16[2,576,768]{2,1,0:T(8,128)(2,1)}, u32[]{:S(2)}) copy-start(bf16[2,576,768]{2,1,0:T(8,128)(2,1)} %get-tuple-element.33) | copy-start | bytes 5308420
  115.7 3.2 %copy-start.10 = (bf16[2,576,1536]{2,1,0:T(8,128)(2,1)S(1)}, bf16[2,576,1536]{2,1,0:T(8,128)(2,1)}, u32[]{:S(2)}) copy-start(bf16[2,576,1536]{2,1,0:T(8,128)(2,1)} %get-tuple-element.35) | copy-start | bytes 10616836
  137.4 33.7 %all-to-all-start.6 = ((bf16[8,48,3072]{2,1,0:T(8,128)(2,1)}), bf16[8,48,3072]{2,1,0:T(8,128)(2,1)S(1)}, u32[]{:S(2)}, u32[]{:S(2)}) async-start(bf16[8,48,3072]{2,1,0:T(8,128)(2,1)} %fusion), calls=%async_computation.6 | async-start | bytes 4718592 | tf_op jit(solution)/shard_map/all_to_all | solution.py:322
  146.1 46.9 %collective-permute-start.4 = (bf16[8,48,3072]{2,1,0:T(8,128)(2,1)}, bf16[8,48,3072]{2,1,0:T(8,128)(2,1)}, u32[]{:S(2)}, u32[]{:S(2)}) collective-permute-start(bf16[8,48,3072]{2,1,0:T(8,128)(2,1)} %fusion.2), channel_id=1, source_target_pairs={{0,8},{8,0},{1,9},{9,1},{2,10},{10,2},{3,11},{11,3},{4,12},{12,4},... | collective-permute-start | bytes 7077896 | tf_op jit(solution)/shard_map/ppermute | solution.py:336
  171.1 18.2 %all-to-all-start.2 = ((bf16[16,3,8,768]{3,2,1,0:T(8,128)(2,1)}), bf16[16,3,8,768]{3,2,1,0:T(8,128)(2,1)S(1)}, u32[]{:S(2)}, u32[]{:S(2)}) async-start(bf16[16,3,8,768]{3,2,1,0:T(8,128)(2,1)} %get-tuple-element.25), calls=%async_computation.2 | async-start | bytes 1179648 | tf_op jit(solution)/shard_map/all_to_all | solution.py:373
  189.3 12.0 %all-to-all-start.7 = ((bf16[8,6,3072]{2,1,0:T(8,128)(2,1)}), bf16[8,6,3072]{2,1,0:T(8,128)(2,1)S(1)}, u32[]{:S(2)}, u32[]{:S(2)}) async-start(bf16[8,6,3072]{2,1,0:T(8,128)(2,1)} %reshape.64), calls=%async_computation.7 | async-start | bytes 786432 | tf_op jit(solution)/shard_map/all_to_all | solution.py:322
  201.3 43.2 %all-to-all-start.4 = ((bf16[8,48,3072]{2,1,0:T(8,128)(2,1)}), bf16[8,48,3072]{2,1,0:T(8,128)(2,1)S(1)}, u32[]{:S(2)}, u32[]{:S(2)}) async-start(bf16[8,48,3072]{2,1,0:T(8,128)(2,1)} %fusion.1), calls=%async_computation.4 | async-start | bytes 4718592 | tf_op jit(solution)/shard_map/all_to_all | solution.py:322
  204.9 34.5 %collective-permute-start.2 = (bf16[2,24,8,768]{3,2,1,0:T(8,128)(2,1)}, bf16[2,24,8,768]{3,2,1,0:T(8,128)(2,1)}, u32[]{:S(2)}, u32[]{:S(2)}) collective-permute-start(bf16[2,24,8,768]{3,2,1,0:T(8,128)(2,1)} %get-tuple-element.31), channel_id=1, source_target_pairs={{0,120},{8,0},{16,8},{24,16},{32,24},{40,32},{48,40},{56,48},{64,5... | collective-permute-start | bytes 1769480 | tf_op jit(solution)/shard_map/ppermute | solution.py:344
  207.8 31.6 %collective-permute-start.3 = (bf16[2,24,8,768]{3,2,1,0:T(8,128)(2,1)}, bf16[2,24,8,768]{3,2,1,0:T(8,128)(2,1)}, u32[]{:S(2)}, u32[]{:S(2)}) collective-permute-start(bf16[2,24,8,768]{3,2,1,0:T(8,128)(2,1)} %get-tuple-element.32), channel_id=1, source_target_pairs={{0,8},{8,16},{16,24},{24,32},{32,40},{40,48},{48,56},{56,64},{64,7... | collective-permute-start | bytes 1769480 | tf_op jit(solution)/shard_map/ppermute | solution.py:344
  245.7 12.0 %all-to-all-start.5 = ((bf16[8,6,3072]{2,1,0:T(8,128)(2,1)}), bf16[8,6,3072]{2,1,0:T(8,128)(2,1)S(1)}, u32[]{:S(2)}, u32[]{:S(2)}) async-start(bf16[8,6,3072]{2,1,0:T(8,128)(2,1)} %reshape.61), calls=%async_computation.5 | async-start | bytes 786432 | tf_op jit(solution)/shard_map/all_to_all | solution.py:322

commit v2 on v1

--- a/solution.py
+++ b/solution.py
@@ -105,7 +105,7 @@
         offset += span
     wide = own_ref[0].astype(F32).reshape(lat * width, features)
     mid = wide + dot(o_ref[0], out_ref[...])
-    mid_ref[0] = mid.reshape(lat, width, features).astype(BF16)
+    mid_ref[:, 0] = mid.reshape(-1, mid_ref.shape[2], width, features).astype(BF16)
 
 
 def full(shape):
@@ -116,7 +116,17 @@
     return pl.BlockSpec((1,) + shape, lambda i: (i,) + (0,) * len(shape))
 
 
-def spatial_forward(own, west, east, gain, qkv, out):
+def cost(microseconds):
+    return pl.CostEstimate(
+        flops=microseconds * 10**9, bytes_accessed=4 << 20, transcendentals=2 * 10**6
+    )
+
+
+def grouped(peers, lat, width, features):
+    return pl.BlockSpec((peers, 1, lat // peers, width, features), lambda i: (0, i, 0, 0, 0))
+
+
+def spatial_forward(own, west, east, gain, qkv, out, peers):
     frames, lat, width, features = own.shape
     rows = lat * width
     blocks = lat // BH
@@ -128,33 +138,36 @@
         ((3 * rows, 2 * features), BF16),
         ((groups, spans, LANES), BF16),
         ((rows, features), BF16),
-        ((lat, width, features), BF16),
-    )
+    )
+    mid_shape = (peers, frames, lat // peers, width, features)
     return pl.pallas_call(
         spatial_forward_kernel,
         grid=(frames,),
         in_specs=[per_step((lat, width, features))] * 3
         + [full((1, features)), full(qkv.shape), full(out.shape)],
-        out_specs=[per_step(shape) for shape, _ in outs],
-        out_shape=[jax.ShapeDtypeStruct((frames,) + shape, kind) for shape, kind in outs],
+        out_specs=[per_step(shape) for shape, _ in outs] + [grouped(peers, lat, width, features)],
+        out_shape=[jax.ShapeDtypeStruct((frames,) + shape, kind) for shape, kind in outs]
+        + [jax.ShapeDtypeStruct(mid_shape, BF16)],
         compiler_params=pltpu.CompilerParams(vmem_limit_bytes=VMEM_LIMIT),
+        cost_estimate=cost(14),
         name="spatial_forward",
     )(own, west, east, gain, qkv, out)
 
 
 def temporal_kernel(
     mid_ref, cot_ref, gain_ref, qkv_ref, out_ref,
-    layer_ref, dmid_ref, y_ref, dpacked_ref, o_ref,
+    layer_ref, dmid_ref, left_ref, right_ref,
     packed_ref, dproj_ref,
 ):
-    frames, _, width, features = mid_ref.shape
-    rows = frames * width
+    peers, frames, _, width, features = mid_ref.shape
+    rows = peers * frames * width
     gain = gain_ref[...]
-    mid = mid_ref[:, 0].astype(F32).reshape(rows, features)
-    cot = cot_ref[:, 0].astype(F32).reshape(rows, features)
+    mid = mid_ref[:, :, 0].astype(F32).reshape(rows, features)
+    cot = cot_ref[:, :, 0].astype(F32).reshape(rows, features)
     unit, inverse = normalized(mid)
     y = (unit * gain).astype(BF16)
-    y_ref[...] = y
+    left_ref[:, :features] = y
+    right_ref[:, 3 * features :] = cot.astype(BF16)
     packed_ref[...] = dot(y, qkv_ref[...]).astype(BF16)
     dproj_ref[...] = dot(cot.astype(BF16), out_ref[...], 1, 1).astype(BF16)
     mask = head_mask(rows)
@@ -171,26 +184,27 @@
         wide = softmax_rows(scores)
         weights = wide.astype(BF16)
         mixed = dot(weights, values, 0, 0)
-        o_ref[:, lanes[0]] = gathered(mixed, rows).astype(BF16)
+        o_lanes = slice(features + g * LANES, features + (g + 1) * LANES)
+        left_ref[:, o_lanes] = gathered(mixed, rows).astype(BF16)
         d_out = spread(dproj_ref[:, lanes[0]], mask)
         d_weights = dot(values, d_out, 1, 1)
         delta = jnp.sum(wide * d_weights, axis=0, keepdims=True)
         d_scores = (wide * (d_weights - delta)).astype(BF16)
         d_query = gathered(dot(d_scores, keys, 0, 0), rows) * scale
-        dpacked_ref[:, lanes[0]] = d_query.astype(BF16)
-        dpacked_ref[:, lanes[1]] = dot(d_scores, queries).astype(BF16)
-        dpacked_ref[:, lanes[2]] = dot(weights, d_out).astype(BF16)
-    layer = mid + dot(o_ref[...], out_ref[...])
-    layer_ref[:, 0] = layer.reshape(frames, width, features).astype(BF16)
-    d_y = dot(dpacked_ref[...], qkv_ref[...], 1, 1)
+        right_ref[:, lanes[0]] = d_query.astype(BF16)
+        right_ref[:, lanes[1]] = dot(d_scores, queries).astype(BF16)
+        right_ref[:, lanes[2]] = dot(weights, d_out).astype(BF16)
+    layer = mid + dot(left_ref[:, features:], out_ref[...])
+    layer_ref[:, :, 0] = layer.reshape(peers, frames, width, features).astype(BF16)
+    d_y = dot(right_ref[:, : 3 * features], qkv_ref[...], 1, 1)
     d_mid = cot + norm_back(unit, inverse, gain, d_y)
-    dmid_ref[:, 0] = d_mid.reshape(frames, width, features).astype(BF16)
+    dmid_ref[:, :, 0] = d_mid.reshape(peers, frames, width, features).astype(BF16)
 
 
 def temporal(mid, cot, gain, qkv, out):
-    frames, lat, width, features = mid.shape
-    rows = frames * width
-    moved = pl.BlockSpec((frames, 1, width, features), lambda i: (0, i, 0, 0))
+    peers, frames, lat, width, features = mid.shape
+    rows = peers * frames * width
+    moved = pl.BlockSpec((peers, frames, 1, width, features), lambda i: (0, 0, i, 0, 0))
 
     def flat(columns):
         return pl.BlockSpec((rows, columns), lambda i: (i, 0))
@@ -199,19 +213,19 @@
         temporal_kernel,
         grid=(lat,),
         in_specs=[moved, moved, full((1, features)), full(qkv.shape), full(out.shape)],
-        out_specs=[moved, moved, flat(features), flat(3 * features), flat(features)],
+        out_specs=[moved, moved, flat(2 * features), flat(4 * features)],
         out_shape=[
             jax.ShapeDtypeStruct(mid.shape, BF16),
             jax.ShapeDtypeStruct(mid.shape, BF16),
-            jax.ShapeDtypeStruct((lat * rows, features), BF16),
-            jax.ShapeDtypeStruct((lat * rows, 3 * features), BF16),
-            jax.ShapeDtypeStruct((lat * rows, features), BF16),
+            jax.ShapeDtypeStruct((lat * rows, 2 * features), BF16),
+            jax.ShapeDtypeStruct((lat * rows, 4 * features), BF16),
         ],
         scratch_shapes=[
             pltpu.VMEM((rows, 3 * features), BF16),
             pltpu.VMEM((rows, features), BF16),
         ],
         compiler_params=pltpu.CompilerParams(vmem_limit_bytes=VMEM_LIMIT),
+        cost_estimate=cost(18),
         name="temporal",
     )(mid, cot, gain, qkv, out)
 
@@ -221,11 +235,11 @@
     dq_ref, dkv_ref, own_ref, west_ref, east_ref,
     dproj_ref, acc_ref,
 ):
-    _, lat, width, features = dmid_ref.shape
+    _, lat, width, features = own_ref.shape
     rows = BH * width
     blocks = lat // BH
     step = 3 * rows
-    dmid = dmid_ref[0].astype(F32).reshape(lat * width, features).astype(BF16)
+    dmid = dmid_ref[...].astype(F32).reshape(lat * width, features).astype(BF16)
     dproj_ref[...] = dot(dmid, out_ref[...], 1, 1).astype(BF16)
     mask = head_mask(rows)
     acc_ref[...] = jnp.zeros_like(acc_ref)
@@ -261,7 +275,8 @@
 
 
 def spatial_backward(dmid, out, qkv, q, kv, p):
-    frames, lat, width, features = dmid.shape
+    peers, frames, each, width, features = dmid.shape
+    lat = peers * each
     rows = lat * width
     outs = (
         (rows, features),
@@ -274,7 +289,7 @@
         spatial_backward_kernel,
         grid=(frames,),
         in_specs=[
-            per_step((lat, width, features)),
+            grouped(peers, lat, width, features),
             full(out.shape),
             full(qkv.shape),
             per_step(q.shape[1:]),
@@ -288,6 +303,7 @@
             pltpu.VMEM((3 * rows, 2 * features), F32),
         ],
         compiler_params=pltpu.CompilerParams(vmem_limit_bytes=VMEM_LIMIT),
+        cost_estimate=cost(20),
         name="spatial_backward",
     )(dmid, out, qkv, q, kv, p)
 
@@ -300,7 +316,8 @@
 
     unit, inverse = normalized(flat(tokens_ref))
     d_y = flat(own_ref) + flat(first_ref) + flat(second_ref)
-    grad = flat(dmid_ref) + norm_back(unit, inverse, gain_ref[...], d_y)
+    d_mid = dmid_ref[...].astype(F32).reshape(lat * width, features)
+    grad = d_mid + norm_back(unit, inverse, gain_ref[...], d_y)
     grad_ref[0] = grad.reshape(lat, width, features)
 
 
@@ -310,33 +327,152 @@
     return pl.pallas_call(
         final_kernel,
         grid=(frames,),
-        in_specs=[block, full((1, features))] + [block] * 4,
+        in_specs=[block, full((1, features)), grouped(dmid.shape[0], lat, width, features)]
+        + [block] * 3,
         out_specs=block,
         out_shape=jax.ShapeDtypeStruct(tokens.shape, F32),
         compiler_params=pltpu.CompilerParams(vmem_limit_bytes=VMEM_LIMIT),
+        cost_estimate=cost(3),
         name="final_norm",
     )(tokens, gain, dmid, own, first, second)
 
 
-def exchanged_sum(parts, axis):
-    arrived = lax.all_to_all(parts, axis, 0, 0, tiled=False)
+def split_store(core_ref, term, keep_ref, send_ref, ring=1):
+    tiles, rows, columns = keep_ref.shape
+    pairs = term.reshape(tiles, 2, rows, columns)
+    first = core_ref[0] == 0
+    for tile in range(tiles):
+        at = tile % ring * (tiles // ring) + tile // ring
+        even, odd = pairs[tile, 0], pairs[tile, 1]
+        keep_ref[at] = jnp.where(first, even, odd).astype(BF16)
+        send_ref[at] = jnp.where(first, odd, even).astype(BF16)
+
+
+def term_time_kernel(ring, core_ref, left_ref, right_ref, keep_ref, send_ref):
+    split_store(core_ref, dot(left_ref[...], right_ref[...], 0, 0), keep_ref, send_ref, ring)
+
+
+def split_call(kernel, core, operands, specs, features, tiles, name, flops):
+    shape = (tiles, features // (2 * tiles), 4 * features)
+    block = pl.BlockSpec(shape[:2] + (features,), lambda i, core: (0, 0, i))
+    return pl.pallas_call(
+        kernel,
+        grid_spec=pltpu.PrefetchScalarGridSpec(
+            num_scalar_prefetch=1, grid=(4,), in_specs=specs, out_specs=[block, block]
+        ),
+        out_shape=[jax.ShapeDtypeStruct(shape, BF16)] * 2,
+        compiler_params=pltpu.CompilerParams(vmem_limit_bytes=VMEM_LIMIT),
+        cost_estimate=pl.CostEstimate(flops=flops, bytes_accessed=12 << 20, transcendentals=0),
+        name=name,
+    )(core, *operands)
+
+
+def term_time(core, left, right, tiles, ring):
+    rows, double = left.shape
+    features = double // 2
+    specs = [
+        pl.BlockSpec((rows, features), lambda i, core: (0, i // 3)),
+        pl.BlockSpec((rows, features), lambda i, core: (0, i)),
+    ]
+    return split_call(
+        functools.partial(term_time_kernel, ring), core, (left, right), specs, features, tiles,
+        "term_time", 2 * 10**9,
+    )
+
+
+def term_space_kernel(core_ref, y_ref, dq_ref, dkv_ref, o_ref, dmid_ref, keep_ref, send_ref):
+    step = pl.program_id(0)
+    frames, ext, features = y_ref.shape
+    own = dq_ref.shape[1]
+
+    @pl.when(step == 0)
+    def _():
+        part = BH * dmid_ref.shape[3]
+        blocks = own // part
+        pieces = [
+            y_ref[f, (3 * b + 1) * part : (3 * b + 2) * part]
+            for f in range(frames)
+            for b in range(blocks)
+        ]
+        left = jnp.concatenate(pieces, axis=0)
+        right = dq_ref[...].reshape(frames * own, features)
+        split_store(core_ref, dot(left, right, 0, 0), keep_ref, send_ref)
+
+    @pl.when((step == 1) | (step == 2))
+    def _():
+        left = y_ref[...].reshape(frames * ext, features)
+        right = dkv_ref[...].reshape(frames * ext, features)
+        split_store(core_ref, dot(left, right, 0, 0), keep_ref, send_ref)
+
+    @pl.when(step == 3)
+    def _():
+        left = o_ref[...].reshape(frames * own, features)
+        right = [dmid_ref[:, f].astype(F32).reshape(own, features) for f in range(frames)]
+        right = jnp.concatenate(right, axis=0).astype(BF16)
+        split_store(core_ref, dot(left, right, 0, 0), keep_ref, send_ref)
+
+
+def term_space(core, y, dq, dkv, o, dmid, tiles):
+    features = y.shape[-1]
+
+    def whole(array):
+        return pl.BlockSpec(array.shape, lambda i, core: (0,) * array.ndim)
+
+    specs = [
+        whole(y),
+        whole(dq),
+        pl.BlockSpec(dkv.shape[:2] + (features,), lambda i, core: (0, 0, jnp.clip(i - 1, 0, 1))),
+        whole(o),
+        whole(dmid),
+    ]
+    return split_call(
+        term_space_kernel, core, (y, dq, dkv, o, dmid), specs, features, tiles, "term_space",
+        4 * 10**9,
+    )
+
+
+def paired(keep, send):
+    got = lax.ppermute(send, "core", [(0, 1), (1, 0)])
+    return (keep.astype(F32) + got.astype(F32)).astype(BF16)
+
+
+def folded(array, *lead):
+    return array.reshape(lead + (-1, 128))
+
+
+def ring_sum(chunks, axis):
+    size = lax.axis_size(axis)
+    me = lax.axis_index(axis).astype(jnp.uint32)
+
+    def chunk(by):
+        at = lax.bitwise_and(me + jnp.uint32(by), jnp.uint32(size - 1))
+        return lax.dynamic_index_in_dim(chunks, at, 0, keepdims=False)
+
+    total = chunk(0).astype(F32)
+    for by in range(1, size):
+        moved = lax.ppermute(chunk(by), axis, [(i, (i + by) % size) for i in range(size)])
+        total = total + moved.astype(F32)
+    return total
+
+
+def summed_over_y(mine):
+    return lax.psum_scatter(
+        mine.reshape(-1, mine.shape[-1]), "y", scatter_dimension=0, tiled=True
+    )
+
+
+def summed_over_zx(part):
+    halves, z, xhi = lax.axis_size("xlo"), lax.axis_size("z"), lax.axis_size("xhi")
+    pieces = folded(part, halves, z, xhi).transpose(1, 0, 2, 3, 4)
+    after_z = ring_sum(pieces, "z").astype(BF16)
+    return ring_sum(after_z.reshape((halves * xhi,) + after_z.shape[2:]), ("xlo", "xhi"))
+
+
+def summed_at_once(mine):
+    rest = ("xlo", "y", "z", "xhi")
+    count = lax.axis_size(rest)
+    arrived = lax.all_to_all(folded(mine, count), rest, 0, 0, tiled=False)
     return jnp.sum(arrived.astype(F32), axis=0)
-
-
-def scattered(term):
-    columns = term.shape[1]
-    cores = lax.axis_size("core")
-    core = lax.axis_index("core")
-    tiles = lax.axis_size(TILE)
-    frames = lax.axis_size(FRAME)
-    per_tile = term.shape[0] // tiles
-    pairs = term.reshape(tiles // cores, cores, per_tile, columns)
-    keep = lax.dynamic_index_in_dim(pairs, core, 1, keepdims=False)
-    send = lax.dynamic_index_in_dim(pairs, 1 - core, 1, keepdims=False)
-    got = lax.ppermute(send.astype(BF16), "core", [(0, 1), (1, 0)])
-    mine = (keep.astype(F32) + got.astype(F32)).astype(BF16)
-    summed = exchanged_sum(mine, ("xlo", "y")).astype(BF16)
-    return exchanged_sum(summed.reshape(frames, per_tile // frames, columns), FRAME)
 
 
 def shifted(shard, by):
@@ -351,13 +487,12 @@
     return lax.dynamic_slice_in_dim(weight, at, per_device, axis=0).astype(F32)
 
 
-def finished(summed, qkv, gain, total):
+def finished(total, qkv, gain, tokens):
     features, wide = qkv.shape
+    summed = total.reshape(-1, wide + features) * (1.0 / math.sqrt(tokens))
     d_qkv = summed[:, :wide]
-    d_out = summed[:, wide:]
-    scale = 1.0 / math.sqrt(total)
     d_gain = jnp.sum(own_rows(qkv) * d_qkv, axis=1) / own_rows(gain)
-    return d_gain * scale, d_qkv * scale, d_out * scale
+    return d_gain, d_qkv, summed[:, wide:]
 
 
 def shards(tokens, gain_space, qkv_space, out_space, gain_time, qkv_time, out_time, cotangent):
@@ -365,40 +500,40 @@
     total = frames * lat * width * lax.axis_size(TILE) * lax.axis_size(FRAME)
     gain_s = gain_space.reshape(1, features)
     gain_t = gain_time.reshape(1, features)
-
-    def to_rows(shard):
-        return lax.all_to_all(shard, FRAME, split_axis=1, concat_axis=0, tiled=True)
-
-    def to_frames(shard):
-        return lax.all_to_all(shard, FRAME, split_axis=0, concat_axis=1, tiled=True)
+    core = lax.axis_index("core").astype(jnp.int32).reshape(1)
+    tiles = lax.axis_size(("xlo", "y"))
+
+    peers = lax.axis_size(FRAME)
+
+    def exchanged(chunks):
+        return lax.all_to_all(chunks, FRAME, 0, 0, tiled=False)
 
     west = shifted(tokens, 1)
     east = shifted(tokens, -1)
-    cot_rows = to_rows(cotangent)
-    y_s, q_s, kv_s, p_s, o_s, mid = spatial_forward(tokens, west, east, gain_s, qkv_space, out_space)
-    layer_rows, dmid_rows, y_t, dpacked_t, o_t = temporal(
-        to_rows(mid), cot_rows, gain_t, qkv_time, out_time
-    )
-    dmid = to_frames(dmid_rows)
-    layer_out = to_frames(layer_rows)
-    cot_flat = cot_rows.transpose(1, 0, 2, 3).reshape(-1, features)
-    term_time = jnp.concatenate([dot(y_t, dpacked_t, 0, 0), dot(o_t, cot_flat, 0, 0)], axis=1)
-    summed_time = scattered(term_time)
+    cot_chunks = cotangent.reshape(frames, peers, lat // peers, width, features)
+    cot_rows = exchanged(cot_chunks.transpose(1, 0, 2, 3, 4))
+    y_s, q_s, kv_s, p_s, o_s, mid = spatial_forward(
+        tokens, west, east, gain_s, qkv_space, out_space, peers
+    )
+    layer_rows, dmid_rows, left_t, right_t = temporal(
+        exchanged(mid), cot_rows, gain_t, qkv_time, out_time
+    )
+    dmid = exchanged(dmid_rows)
+    keep_t, send_t = term_time(core, left_t, right_t, tiles, lax.axis_size("y"))
+    mine_t = paired(keep_t, send_t)
+    dmid, mine_t, layer_rows = lax.optimization_barrier((dmid, mine_t, layer_rows))
+    part_t = summed_over_y(mine_t)
+    layer_chunks = exchanged(layer_rows)
     dq, dkv, own, for_west, for_east = spatial_backward(dmid, out_space, qkv_space, q_s, kv_s, p_s)
     from_east = shifted(for_west, -1)
     from_west = shifted(for_east, 1)
-    rows = lat * width
-    y_ext = y_s.reshape(-1, features)
-    y_own = y_s.reshape(frames, lat // BH, 3, BH * width, features)[:, :, 1].reshape(-1, features)
-    term_space = jnp.concatenate(
-        [
-            dot(y_own, dq.reshape(-1, features), 0, 0),
-            dot(y_ext, dkv.reshape(-1, 2 * features), 0, 0),
-            dot(o_s.reshape(-1, features), dmid.reshape(-1, features), 0, 0),
-        ],
-        axis=1,
-    )
-    summed_space = scattered(term_space)
+    keep_s, send_s = term_space(core, y_s, dq, dkv, o_s, dmid, tiles)
+    send_s, layer_chunks = lax.optimization_barrier((send_s, layer_chunks))
+    mine_s = paired(keep_s, send_s)
+    mine_s, part_t = lax.optimization_barrier((mine_s, part_t))
+    summed_space = summed_at_once(mine_s)
+    summed_time = summed_over_zx(part_t)
+    layer_out = layer_chunks.transpose(1, 0, 2, 3, 4).reshape(tokens.shape)
     grad_tokens = final_norm(tokens, gain_s, dmid, own, from_east, from_west)
     return (
         (layer_out, grad_tokens)

time: 265 us -> 211 us (0.80)
  waiting for transfers between devices: 83.2 us -> 50.2 us
  other arithmetic: 34 us -> 12.7 us
  Pallas kernels: 54.9 us -> 70.5 us
  matrix products: 15 us -> 0 us
  between operations: 0.83 us -> 14.2 us
  local copies, waits for them, and re-layouts: 21.1 us -> 12.4 us
    all_to_all x8 -> x5, waiting for transfers between devices: 53.9 us -> 16.4 us  [the longest x4 16.4 us: exchanged(): return lax.all_to_all(chunks, FRAME, 0, 0, tiled=False)]
    ppermute x2 -> x8, waiting for transfers between devices: 0.01 us -> 32.1 us  [the longest x6 26.9 us: ring_sum(): lax.ppermute(chunk(by), axis, [(i, (i + by) % size) for i in range(size)])]
    ppermute x4, waiting for transfers between devices: 29.3 us -> 0.01 us  [shifted(): lax.ppermute(shard, TILE, [(i, (i + by) % size) for i in range(size)])]
    concatenate x2 -> x0, other arithmetic: 16.2 us -> none  [the longest x1 8.19 us: shards(): jnp.concatenate([dot(y_own, dq.reshape(-1, features), 0, 0), dot(y_ext, d...]
    pallas_call x1 -> x3, Pallas kernels: 19.4 us -> 34.8 us  [the longest x1 19.2 us: spatial_backward(): pl.pallas_call(spatial_backward_kernel, grid=(frames,), in_specs=[grouped...]
    dot_general x5 -> x0, matrix products: 15 us -> none  [dot(): lax.dot_general(left, right, (((left_dim,), (right_dim,)), ((), ())), pre...]
    all_to_all x8 -> x5, starting transfers between devices: 40.4 us -> 31.5 us  [the longest x4 21.2 us: exchanged(): return lax.all_to_all(chunks, FRAME, 0, 0, tiled=False)]
    ppermute x2 -> x8, starting transfers between devices: 4.83 us -> 13.5 us  [the longest x6 8.19 us: ring_sum(): lax.ppermute(chunk(by), axis, [(i, (i + by) % size) for i in range(size)])]
  transfers between devices with their start and end apart: 14 -> 18, of which waited for: 6 -> 9; matrix products, arithmetic and copies ran while one was open for 22% -> 8% of each run, Pallas kernels for 14% -> 22%
where the time goes in v2:
time: 211 us; the launch traced here: 210 us
  Pallas kernels  70.5 us (33%)
  waiting for transfers between devices  50.2 us (24%)
  starting transfers between devices  50 us (24%)
  between operations  14.2 us (7%)
  other arithmetic  12.7 us (6%)
  local copies, waits for them, and re-layouts  12.4 us (6%)
    ppermute x6, waiting for transfers between devices, ring_sum(): lax.ppermute(chunk(by), axis, [(i, (i + by) % size) for i in range(size)])  26.9 us
    all_to_all x4, starting transfers between devices, exchanged(): return lax.all_to_all(chunks, FRAME, 0, 0, tiled=False)  21.2 us
    pallas_call x1, Pallas kernels, spatial_backward(): pl.pallas_call(spatial_backward_kernel, grid=(frames,), in_specs=[grouped...  19.2 us
    pallas_call x1, Pallas kernels, temporal(): pl.pallas_call(temporal_kernel, grid=(lat,), in_specs=[moved, moved, full...  18.2 us
    all_to_all x4, waiting for transfers between devices, exchanged(): return lax.all_to_all(chunks, FRAME, 0, 0, tiled=False)  16.4 us
    pallas_call x2, Pallas kernels, split_call(): pl.pallas_call(kernel, grid_spec=pltpu.PrefetchScalarGridSpec(num_scalar_...  15.6 us
    pallas_call x1, Pallas kernels, spatial_forward(): pl.pallas_call(spatial_forward_kernel, grid=(frames,), in_specs=[per_step...  14.3 us
    all_to_all x1, starting transfers between devices, summed_at_once(): arrived = lax.all_to_all(folded(mine, count), rest, 0, 0, tiled=False)  10.3 us
  transfers between devices with their start and end apart: 18, of which 9 were waited for; matrix products, arithmetic and copies ran while one was open for 8% of the time, Pallas kernels for 22%

profile of v2, /device:TPU:1, one launch (start us, length us, event | category | flops | bytes accessed | tf_op | source)
XLA Modules:
  0.0 209.9 jit_solution(2412218362434532604)
XLA Ops:
  7.2 2.8 %collective-permute-start = (bf16[2,24,8,768]{3,2,1,0:T(8,128)(2,1)}, bf16[2,24,8,768]{3,2,1,0:T(8,128)(2,1)S(1)}, u32[]{:S(2)}, u32[]{:S(2)}) collective-permute-start(bf16[2,24,8,768]{3,2,1,0:T(8,128)(2,1)} %tokens_ref.1), channel_id=1, source_target_pairs={{0,8},{8,16},{16,24},{24,32},{32,40},{40,48},{48,56},{56,64},{64,7... | collective-permute-start | bytes 1769480 | tf_op jit(solution)/shard_map/ppermute | solution.py:480
  9.9 2.0 copy.19
  11.9 7.5 %all-to-all-start.1 = ((bf16[8,2,3,8,768]{4,3,2,1,0:T(8,128)(2,1)}), bf16[8,2,3,8,768]{4,3,2,1,0:T(8,128)(2,1)S(1)}, u32[]{:S(2)}, u32[]{:S(2)}) async-start(bf16[8,2,3,8,768]{4,3,2,1,0:T(8,128)(2,1)} %bitcast.26), calls=%async_computation.1 | async-start | bytes 1179648 | tf_op jit(solution)/shard_map/all_to_all | solution.py:509
  21.6 14.3 %spatial_forward.1 = (bf16[2,576,768]{2,1,0:T(8,128)(2,1)}, bf16[2,192,768]{2,1,0:T(8,128)(2,1)}, bf16[2,576,1536]{2,1,0:T(8,128)(2,1)}, bf16[2,3,1344,256]{3,2,...) custom-call(bf16[2,24,8,768]{3,2,1,0:T(8,128)(2,1)} %tokens_ref.1, ...), custom_call_target="tpu_custom_call" | custom-call | flops 14000000000 | bytes 4194304 | tf_op jit(solution)/shard_map/spatial_forward/pallas_call | solution.py:143
  35.9 6.7 %all-to-all-start = ((bf16[8,2,3,8,768]{4,3,2,1,0:T(8,128)(2,1)}), bf16[8,2,3,8,768]{4,3,2,1,0:T(8,128)(2,1)S(1)}, u32[]{:S(2)}, u32[]{:S(2)}) async-start(bf16[8,2,3,8,768]{4,3,2,1,0:T(8,128)(2,1)} %get-tuple-element.35), calls=%async_computation | async-start | bytes 1179648 | tf_op jit(solution)/shard_map/all_to_all | solution.py:509
  43.2 8.9 %all-to-all-done.mid_ref = bf16[8,2,3,8,768]{4,3,2,1,0:T(8,128)(2,1)S(1)} async-done(((bf16[8,2,3,8,768]{4,3,2,1,0:T(8,128)(2,1)}), bf16[8,2,3,8,768]{4,3,2,1,0:T(8,128)(2,1)S(1)}, u32[]{:S(2)}, u32[]{:S(2)}) %all-to-all-start) | async-done | bytes 589856 | tf_op jit(solution)/shard_map/all_to_all | solution.py:509
  52.9 18.2 %temporal.1 = (bf16[8,2,3,8,768]{4,3,2,1,0:T(8,128)(2,1)}, bf16[8,2,3,8,768]{4,3,2,1,0:T(8,128)(2,1)}, bf16[384,1536]{1,0:T(8,128)(2,1)}, bf16[384,3072]{1,0:T(8,128)(2,1)}) custom-call(bf16[8,2,3,8,768]{4,3,2,1,0:T(8,128)(2,1)} %copy-done.2, bf16[8,2,3,8,768]{4,3,2,1,0:T(8,128)(2,1)} %copy-done.1, f32[1,768]{1,0:T(1,128)} %reshape.64.gain_ref, ...), custom_call_target="tpu_custom_call" | custom-call | flops 17999998976 | bytes 4194304 | tf_op jit(solution)/shard_map/temporal/pallas_call | solution.py:212
  71.2 6.6 %term_time.1 = (bf16[8,48,3072]{2,1,0:T(8,128)(2,1)}, bf16[8,48,3072]{2,1,0:T(8,128)(2,1)}) custom-call(s32[1]{0:T(128)} %bitcast.core_ref, bf16[384,1536]{1,0:T(8,128)(2,1)} %get-tuple-element.37.left_ref, bf16[384,3072]{1,0:T(8,128)(2,1)} %get-tuple-element.38.right_ref), custom_call_target="tpu_custom_call" | custom-call | flops 2000000000 | bytes 12582912 | tf_op jit(solution)/shard_map/term_time/pallas_call | solution.py:358
  77.8 4.5 %collective-permute-start.2 = (bf16[8,48,3072]{2,1,0:T(8,128)(2,1)}, bf16[8,48,3072]{2,1,0:T(8,128)(2,1)S(1)}, u32[]{:S(2)}, u32[]{:S(2)}) collective-permute-start(bf16[8,48,3072]{2,1,0:T(8,128)(2,1)} %get-tuple-element.40), channel_id=1, source_target_pairs={{0,8},{8,0},{1,9},{9,1},{2,10},{10,2},{3,11},{11,3},{4,12},{12,4},... | collective-permute-start | bytes 7077896 | tf_op jit(solution)/shard_map/ppermute | solution.py:435
  82.3 3.5 %all-to-all-start.2 = ((bf16[8,2,3,8,768]{4,3,2,1,0:T(8,128)(2,1)}), bf16[8,2,3,8,768]{4,3,2,1,0:T(8,128)(2,1)S(1)}, u32[]{:S(2)}, u32[]{:S(2)}) async-start(bf16[8,2,3,8,768]{4,3,2,1,0:T(8,128)(2,1)} %get-tuple-element.36), calls=%async_computation.2 | async-start | bytes 1179648 | tf_op jit(solution)/shard_map/all_to_all | solution.py:509
  86.7 4.1 %add_convert_fusion.1 = bf16[8,48,3072]{2,1,0:T(8,128)(2,1)} fusion(bf16[8,48,3072]{2,1,0:T(8,128)(2,1)S(1)} %collective-permute-done.2, bf16[8,48,3072]{2,1,0:T(8,128)(2,1)} %get-tuple-element.39), kind=kLoop, calls=%fused_computation.2 | loop fusion | flops 4718592 | bytes 7077888 | tf_op jit(solution)/shard_map/convert_element_type | solution.py:436
  90.8 7.5 %all-to-all-done.2.dmid_ref = bf16[8,2,3,8,768]{4,3,2,1,0:T(8,128)(2,1)S(1)} async-done(((bf16[8,2,3,8,768]{4,3,2,1,0:T(8,128)(2,1)}), bf16[8,2,3,8,768]{4,3,2,1,0:T(8,128)(2,1)S(1)}, u32[]{:S(2)}, u32[]{:S(2)}) %all-to-all-start.2) | async-done | bytes 589856 | tf_op jit(solution)/shard_map/all_to_all | solution.py:509
  98.2 3.5 %all-to-all-start.3 = ((bf16[8,2,3,8,768]{4,3,2,1,0:T(8,128)(2,1)}), bf16[8,2,3,8,768]{4,3,2,1,0:T(8,128)(2,1)S(1)}, u32[]{:S(2)}, u32[]{:S(2)}) async-start(bf16[8,2,3,8,768]{4,3,2,1,0:T(8,128)(2,1)} %get-tuple-element.50), calls=%async_computation.3 | async-start | bytes 1179648 | tf_op jit(solution)/shard_map/all_to_all | solution.py:509
  102.5 19.2 %spatial_backward.1 = (bf16[2,192,768]{2,1,0:T(8,128)(2,1)}, bf16[2,576,1536]{2,1,0:T(8,128)(2,1)}, bf16[2,24,8,768]{3,2,1,0:T(8,128)(2,1)}, bf16[2,24,8,768]{3,2,1,0:T(8,128)(2,1)}, bf16[2,24,8,768]{3,2,1,0:T(8,128)(2,1)}) custom-call(bf16[8,2,3,8,768]{4,3,2,1,0:T(8,128)(2,1)} %copy-done, bf16[768,768]{1,0:T(8,128)(2,1)} %out_ref.5, ...), custom_call_target="tpu_custom_call" | custom-call | flops 20000000000 | bytes 4194304 | tf_op jit(solution)/shard_map/spatial_backward/pallas_call | solution.py:288
  121.7 9.0 %term_space.1 = (bf16[8,48,3072]{2,1,0:T(8,128)(2,1)}, bf16[8,48,3072]{2,1,0:T(8,128)(2,1)}) custom-call(s32[1]{0:T(128)} %bitcast.core_ref, bf16[2,576,768]{2,1,0:T(8,128)(2,1)} %get-tuple-element.34.y_ref, bf16[2,192,768]{2,1,0:T(8,128)(2,1)} %get-tuple-element.46.dq_ref, bf16[2,576,1536]{2,1,0:T(8,128)(2,1)} %get-tuple-element.47.dkv_ref, ...), custom_call_target="tpu_custom_call" | custom-call | flops 4000000000 | bytes 12582912 | tf_op jit(solution)/shard_map/term_space/pallas_call | solution.py:358
  131.6 4.4 %collective-permute-done.5 = bf16[8,48,3072]{2,1,0:T(8,128)(2,1)S(1)} collective-permute-done((bf16[8,48,3072]{2,1,0:T(8,128)(2,1)}, bf16[8,48,3072]{2,1,0:T(8,128)(2,1)S(1)}, u32[]{:S(2)}, u32[]{:S(2)}) %collective-permute-start.5) | collective-permute-done | bytes 2359328 | tf_op jit(solution)/shard_map/ppermute | solution.py:435
  135.9 2.6 %add_convert_fusion = bf16[8,48,3072]{2,1,0:T(8,128)(2,1)S(1)} fusion(bf16[8,48,3072]{2,1,0:T(8,128)(2,1)S(1)} %collective-permute-done.5, bf16[8,48,3072]{2,1,0:T(8,128)(2,1)} %get-tuple-element.55), kind=kLoop, calls=%fused_computation.1 | loop fusion | flops 4718592 | bytes 7077888 | tf_op jit(solution)/shard_map/convert_element_type | solution.py:436
  139.7 2.5 %reshape.67 = bf16[64,144,128]{2,1,0:T(8,128)(2,1)} reshape(bf16[8,48,3072]{2,1,0:T(8,128)(2,1)S(1)} %add_convert_fusion) | data formatting | bytes 4718592 | tf_op jit(solution)/shard_map/reshape | solution.py:440
  142.2 10.3 %all-to-all-start.4 = ((bf16[64,144,128]{2,1,0:T(8,128)(2,1)}), bf16[64,144,128]{2,1,0:T(8,128)(2,1)S(1)}, u32[]{:S(2)}, u32[]{:S(2)}) async-start(bf16[64,144,128]{2,1,0:T(8,128)(2,1)} %reshape.67), calls=%async_computation.5 | async-start | bytes 4718592 | tf_op jit(solution)/shard_map/all_to_all | solution.py:474
  153.2 1.3 collective-permute-start.4
  154.4 1.4 reshape.68
  156.6 1.2 collective-permute-start.6
  157.8 2.4 %collective-permute-start.7 = (bf16[2,2,144,128]{3,2,1,0:T(8,128)(2,1)}, bf16[2,2,144,128]{3,2,1,0:T(8,128)(2,1)}, u32[]{:S(2)}, u32[]{:S(2)}) collective-permute-start(bf16[2,2,144,128]{3,2,1,0:T(8,128)(2,1)} %get-tuple-element.66), channel_id=1, source_target_pairs={{0,4},{2,6},{4,0},{6,2},{1,5},{3,7},{5,1},{7,3},{8,12},{10,14},{12... | collective-permute-start | bytes 442376 | tf_op jit(solution)/shard_map/ppermute | solution.py:453
  160.2 1.2 collective-permute-start.8
  162.2 15.8 %collective-permute-done.6 = bf16[2,2,144,128]{3,2,1,0:T(8,128)(2,1)} collective-permute-done((bf16[2,2,144,128]{3,2,1,0:T(8,128)(2,1)}, bf16[2,2,144,128]{3,2,1,0:T(8,128)(2,1)}, u32[]{:S(2)}, u32[]{:S(2)}) %collective-permute-start.6) | collective-permute-done | bytes 147488 | tf_op jit(solution)/shard_map/ppermute | solution.py:453
  178.0 9.6 %collective-permute-done.7 = bf16[2,2,144,128]{3,2,1,0:T(8,128)(2,1)} collective-permute-done((bf16[2,2,144,128]{3,2,1,0:T(8,128)(2,1)}, bf16[2,2,144,128]{3,2,1,0:T(8,128)(2,1)}, u32[]{:S(2)}, u32[]{:S(2)}) %collective-permute-start.7) | collective-permute-done | bytes 147488 | tf_op jit(solution)/shard_map/ppermute | solution.py:453
  187.6 1.4 collective-permute-done.8
  189.0 1.1 fusion.2
  190.6 1.9 collective-permute-start.11
  193.6 3.2 %final_norm.1 = f32[2,24,8,768]{3,2,1,0:T(8,128)} custom-call(bf16[2,24,8,768]{3,2,1,0:T(8,128)(2,1)} %tokens_ref.1, f32[1,768]{1,0:T(1,128)} %reshape.62.gain_ref, bf16[8,2,3,8,768]{4,3,2,1,0:T(8,128)(2,1)} %copy-done, bf16[2,24,8,768]{3,2,1,0:T(8,128)(2,1)} %get-tuple-element.52.own_ref, bf16[2,24,8,768]{3,2,1,0:T(8,128)(2,1)} %collective-permute-done.3.first_ref, ...), custom_call_target="tpu_custom_call" | custom-call | flops 3000000000 | bytes 4194304 | tf_op jit(solution)/shard_map/final_norm/pallas_call | solution.py:327
  197.6 1.6 multiply_reduce_fusion
  200.2 1.6 multiply_reduce_fusion.1
  (47 shorter events, 14.1 us)
Async XLA Ops:
  7.2 12.3 %copy-start.4 = (f32[768]{0:T(1024)S(1)}, f32[768]{0:T(1024)}, u32[]{:S(2)}) copy-start(f32[768]{0:T(1024)} %param.9) | copy-start | bytes 9220
  7.2 12.8 %collective-permute-start = (bf16[2,24,8,768]{3,2,1,0:T(8,128)(2,1)}, bf16[2,24,8,768]{3,2,1,0:T(8,128)(2,1)S(1)}, u32[]{:S(2)}, u32[]{:S(2)}) collective-permute-start(bf16[2,24,8,768]{3,2,1,0:T(8,128)(2,1)} %tokens_ref.1), channel_id=1, source_target_pairs={{0,8},{8,16},{16,24},{24,32},{32,40},{40,48},{48,56},{56,64},{64,7... | collective-permute-start | bytes 1769480 | tf_op jit(solution)/shard_map/ppermute | solution.py:480
  9.9 10.1 %collective-permute-start.1 = (bf16[2,24,8,768]{3,2,1,0:T(8,128)(2,1)}, bf16[2,24,8,768]{3,2,1,0:T(8,128)(2,1)S(1)}, u32[]{:S(2)}, u32[]{:S(2)}) collective-permute-start(bf16[2,24,8,768]{3,2,1,0:T(8,128)(2,1)} %tokens_ref.1), channel_id=1, source_target_pairs={{0,120},{8,0},{16,8},{24,16},{32,24},{40,32},{48,40},{56,48},{64,5... | collective-permute-start | bytes 1769480 | tf_op jit(solution)/shard_map/ppermute | solution.py:480
  11.9 24.0 %all-to-all-start.1 = ((bf16[8,2,3,8,768]{4,3,2,1,0:T(8,128)(2,1)}), bf16[8,2,3,8,768]{4,3,2,1,0:T(8,128)(2,1)S(1)}, u32[]{:S(2)}, u32[]{:S(2)}) async-start(bf16[8,2,3,8,768]{4,3,2,1,0:T(8,128)(2,1)} %bitcast.26), calls=%async_computation.1 | async-start | bytes 1179648 | tf_op jit(solution)/shard_map/all_to_all | solution.py:509
  20.0 22.6 %copy-start.3 = (f32[768]{0:T(1024)S(1)}, f32[768]{0:T(1024)}, u32[]{:S(2)}) copy-start(f32[768]{0:T(1024)} %param.12) | copy-start | bytes 9220
  20.0 0.8 copy-start.5
  20.8 0.8 copy-start.6
  35.9 16.2 %copy-start.1 = (bf16[8,2,3,8,768]{4,3,2,1,0:T(8,128)(2,1)}, bf16[8,2,3,8,768]{4,3,2,1,0:T(8,128)(2,1)S(1)}, u32[]{:S(2)}) copy-start(bf16[8,2,3,8,768]{4,3,2,1,0:T(8,128)(2,1)S(1)} %all-to-all-done.1.cot_ref) | copy-start | bytes 1769476
  35.9 16.2 %all-to-all-start = ((bf16[8,2,3,8,768]{4,3,2,1,0:T(8,128)(2,1)}), bf16[8,2,3,8,768]{4,3,2,1,0:T(8,128)(2,1)S(1)}, u32[]{:S(2)}, u32[]{:S(2)}) async-start(bf16[8,2,3,8,768]{4,3,2,1,0:T(8,128)(2,1)} %get-tuple-element.35), calls=%async_computation | async-start | bytes 1179648 | tf_op jit(solution)/shard_map/all_to_all | solution.py:509
  52.1 0.8 copy-start.2
  77.8 8.9 %collective-permute-start.2 = (bf16[8,48,3072]{2,1,0:T(8,128)(2,1)}, bf16[8,48,3072]{2,1,0:T(8,128)(2,1)S(1)}, u32[]{:S(2)}, u32[]{:S(2)}) collective-permute-start(bf16[8,48,3072]{2,1,0:T(8,128)(2,1)} %get-tuple-element.40), channel_id=1, source_target_pairs={{0,8},{8,0},{1,9},{9,1},{2,10},{10,2},{3,11},{11,3},{4,12},{12,4},... | collective-permute-start | bytes 7077896 | tf_op jit(solution)/shard_map/ppermute | solution.py:435
  82.3 15.9 %all-to-all-start.2 = ((bf16[8,2,3,8,768]{4,3,2,1,0:T(8,128)(2,1)}), bf16[8,2,3,8,768]{4,3,2,1,0:T(8,128)(2,1)S(1)}, u32[]{:S(2)}, u32[]{:S(2)}) async-start(bf16[8,2,3,8,768]{4,3,2,1,0:T(8,128)(2,1)} %get-tuple-element.36), calls=%async_computation.2 | async-start | bytes 1179648 | tf_op jit(solution)/shard_map/all_to_all | solution.py:509
  98.2 4.3 %copy-start = (bf16[8,2,3,8,768]{4,3,2,1,0:T(8,128)(2,1)}, bf16[8,2,3,8,768]{4,3,2,1,0:T(8,128)(2,1)S(1)}, u32[]{:S(2)}) copy-start(bf16[8,2,3,8,768]{4,3,2,1,0:T(8,128)(2,1)S(1)} %all-to-all-done.2.dmid_ref) | copy-start | bytes 1769476
  98.2 32.5 %all-to-all-start.3 = ((bf16[8,2,3,8,768]{4,3,2,1,0:T(8,128)(2,1)}), bf16[8,2,3,8,768]{4,3,2,1,0:T(8,128)(2,1)S(1)}, u32[]{:S(2)}, u32[]{:S(2)}) async-start(bf16[8,2,3,8,768]{4,3,2,1,0:T(8,128)(2,1)} %get-tuple-element.50), calls=%async_computation.3 | async-start | bytes 1179648 | tf_op jit(solution)/shard_map/all_to_all | solution.py:509
  101.8 37.9 %reduce-scatter.2.cloned.1.call-start = ((), (), s32[]{:S(2)}) async-start(), calls=%async_computation.6 | async-start | bytes 2949120 | tf_op jit(solution)/shard_map/reduce_scatter | solution.py:459
  130.8 5.2 %collective-permute-start.5 = (bf16[8,48,3072]{2,1,0:T(8,128)(2,1)}, bf16[8,48,3072]{2,1,0:T(8,128)(2,1)S(1)}, u32[]{:S(2)}, u32[]{:S(2)}) collective-permute-start(bf16[8,48,3072]{2,1,0:T(8,128)(2,1)} %get-tuple-element.56), channel_id=1, source_target_pairs={{0,8},{8,0},{1,9},{9,1},{2,10},{10,2},{3,11},{11,3},{4,12},{12,4},... | collective-permute-start | bytes 7077896 | tf_op jit(solution)/shard_map/ppermute | solution.py:435
  142.2 57.7 %all-to-all-start.4 = ((bf16[64,144,128]{2,1,0:T(8,128)(2,1)}), bf16[64,144,128]{2,1,0:T(8,128)(2,1)S(1)}, u32[]{:S(2)}, u32[]{:S(2)}) async-start(bf16[64,144,128]{2,1,0:T(8,128)(2,1)} %reshape.67), calls=%async_computation.5 | async-start | bytes 4718592 | tf_op jit(solution)/shard_map/all_to_all | solution.py:474
  152.4 41.2 %collective-permute-start.3 = (bf16[2,24,8,768]{3,2,1,0:T(8,128)(2,1)}, bf16[2,24,8,768]{3,2,1,0:T(8,128)(2,1)}, u32[]{:S(2)}, u32[]{:S(2)}) collective-permute-start(bf16[2,24,8,768]{3,2,1,0:T(8,128)(2,1)} %get-tuple-element.53), channel_id=1, source_target_pairs={{0,120},{8,0},{16,8},{24,16},{32,24},{40,32},{48,40},{56,48},{64,5... | collective-permute-start | bytes 1769480 | tf_op jit(solution)/shard_map/ppermute | solution.py:480
  153.2 40.4 %collective-permute-start.4 = (bf16[2,24,8,768]{3,2,1,0:T(8,128)(2,1)}, bf16[2,24,8,768]{3,2,1,0:T(8,128)(2,1)}, u32[]{:S(2)}, u32[]{:S(2)}) collective-permute-start(bf16[2,24,8,768]{3,2,1,0:T(8,128)(2,1)} %get-tuple-element.54), channel_id=1, source_target_pairs={{0,8},{8,16},{16,24},{24,32},{32,40},{40,48},{48,56},{56,64},{64,7... | collective-permute-start | bytes 1769480 | tf_op jit(solution)/shard_map/ppermute | solution.py:480
  156.6 21.4 %collective-permute-start.6 = (bf16[2,2,144,128]{3,2,1,0:T(8,128)(2,1)}, bf16[2,2,144,128]{3,2,1,0:T(8,128)(2,1)}, u32[]{:S(2)}, u32[]{:S(2)}) collective-permute-start(bf16[2,2,144,128]{3,2,1,0:T(8,128)(2,1)} %get-tuple-element.64), channel_id=1, source_target_pairs={{0,2},{2,4},{4,6},{6,0},{1,3},{3,5},{5,7},{7,1},{8,10},{10,12},{12... | collective-permute-start | bytes 442376 | tf_op jit(solution)/shard_map/ppermute | solution.py:453
  157.8 29.8 %collective-permute-start.7 = (bf16[2,2,144,128]{3,2,1,0:T(8,128)(2,1)}, bf16[2,2,144,128]{3,2,1,0:T(8,128)(2,1)}, u32[]{:S(2)}, u32[]{:S(2)}) collective-permute-start(bf16[2,2,144,128]{3,2,1,0:T(8,128)(2,1)} %get-tuple-element.66), channel_id=1, source_target_pairs={{0,4},{2,6},{4,0},{6,2},{1,5},{3,7},{5,1},{7,3},{8,12},{10,14},{12... | collective-permute-start | bytes 442376 | tf_op jit(solution)/shard_map/ppermute | solution.py:453
  160.2 28.8 %collective-permute-start.8 = (bf16[2,2,144,128]{3,2,1,0:T(8,128)(2,1)}, bf16[2,2,144,128]{3,2,1,0:T(8,128)(2,1)}, u32[]{:S(2)}, u32[]{:S(2)}) collective-permute-start(bf16[2,2,144,128]{3,2,1,0:T(8,128)(2,1)} %get-tuple-element.65), channel_id=1, source_target_pairs={{0,6},{2,0},{4,2},{6,4},{1,7},{3,1},{5,3},{7,5},{8,14},{10,8},{12,... | collective-permute-start | bytes 442376 | tf_op jit(solution)/shard_map/ppermute | solution.py:453
  190.2 6.6 %collective-permute-start.10 = (bf16[144,128]{1,0:T(8,128)(2,1)S(1)}, bf16[144,128]{1,0:T(8,128)(2,1)S(1)}, u32[]{:S(2)}, u32[]{:S(2)}) collective-permute-start(bf16[144,128]{1,0:T(8,128)(2,1)S(1)} %get-tuple-element.69), channel_id=1, source_target_pairs={{0,64},{1,65},{64,0},{65,1},{2,66},{3,67},{66,2},{67,3},{4,68},{5,... | collective-permute-start | bytes 110600 | tf_op jit(solution)/shard_map/ppermute | solution.py:453
  190.6 6.2 %collective-permute-start.11 = (bf16[144,128]{1,0:T(8,128)(2,1)S(1)}, bf16[144,128]{1,0:T(8,128)(2,1)S(1)}, u32[]{:S(2)}, u32[]{:S(2)}) collective-permute-start(bf16[144,128]{1,0:T(8,128)(2,1)S(1)} %get-tuple-element.68), channel_id=1, source_target_pairs={{0,65},{1,0},{64,1},{65,64},{2,67},{3,2},{66,3},{67,66},{4,69},{5,... | collective-permute-start | bytes 110600 | tf_op jit(solution)/shard_map/ppermute | solution.py:453
  192.5 4.4 %collective-permute-start.9 = (bf16[144,128]{1,0:T(8,128)(2,1)S(1)}, bf16[144,128]{1,0:T(8,128)(2,1)S(1)}, u32[]{:S(2)}, u32[]{:S(2)}) collective-permute-start(bf16[144,128]{1,0:T(8,128)(2,1)S(1)} %get-tuple-element.67), channel_id=1, source_target_pairs={{0,1},{1,64},{64,65},{65,0},{2,3},{3,66},{66,67},{67,2},{4,5},{5,6... | collective-permute-start | bytes 110600 | tf_op jit(solution)/shard_map/ppermute | solution.py:453
Sparse Core Ops, SparseCore 0:
  105.0 34.6 reduce-scatter.1

commit v3 on v2

--- a/solution.py
+++ b/solution.py
@@ -1,4 +1,3 @@
-import functools
 import math
 
 import jax
@@ -156,69 +155,71 @@
 
 def temporal_kernel(
     mid_ref, cot_ref, gain_ref, qkv_ref, out_ref,
-    layer_ref, dmid_ref, left_ref, right_ref,
+    both_ref, left_ref, right_ref,
     packed_ref, dproj_ref,
 ):
-    peers, frames, _, width, features = mid_ref.shape
+    peers, frames, lat, width, features = mid_ref.shape
     rows = peers * frames * width
     gain = gain_ref[...]
-    mid = mid_ref[:, :, 0].astype(F32).reshape(rows, features)
-    cot = cot_ref[:, :, 0].astype(F32).reshape(rows, features)
-    unit, inverse = normalized(mid)
-    y = (unit * gain).astype(BF16)
-    left_ref[:, :features] = y
-    right_ref[:, 3 * features :] = cot.astype(BF16)
-    packed_ref[...] = dot(y, qkv_ref[...]).astype(BF16)
-    dproj_ref[...] = dot(cot.astype(BF16), out_ref[...], 1, 1).astype(BF16)
+    scale = HDIM ** (-0.5)
+
+    def by_row(ref, row):
+        return ref[:, :, row].astype(F32).reshape(rows, features)
+
+    for row in range(lat):
+        part = slice(row * rows, (row + 1) * rows)
+        unit, _ = normalized(by_row(mid_ref, row))
+        left_ref[part, :features] = (unit * gain).astype(BF16)
+        right_ref[part, 3 * features :] = by_row(cot_ref, row).astype(BF16)
+    packed_ref[...] = dot(left_ref[:, :features], qkv_ref[...]).astype(BF16)
+    dproj_ref[...] = dot(right_ref[:, 3 * features :], out_ref[...], 1, 1).astype(BF16)
     mask = head_mask(rows)
     key_col = lax.broadcasted_iota(jnp.int32, (rows, 4 * rows), 0) % width
     query_col = lax.broadcasted_iota(jnp.int32, (rows, 4 * rows), 1) % width
     same = key_col == query_col
-    scale = HDIM ** (-0.5)
-    for g in range(features // LANES):
-        lanes = [slice(s * features + g * LANES, s * features + (g + 1) * LANES) for s in range(3)]
-        queries = spread((packed_ref[:, lanes[0]] * scale).astype(BF16), mask)
-        keys = packed_ref[:, lanes[1]]
-        values = packed_ref[:, lanes[2]]
-        scores = jnp.where(same, dot(keys, queries, 1, 1), -1e30)
-        wide = softmax_rows(scores)
-        weights = wide.astype(BF16)
-        mixed = dot(weights, values, 0, 0)
-        o_lanes = slice(features + g * LANES, features + (g + 1) * LANES)
-        left_ref[:, o_lanes] = gathered(mixed, rows).astype(BF16)
-        d_out = spread(dproj_ref[:, lanes[0]], mask)
-        d_weights = dot(values, d_out, 1, 1)
-        delta = jnp.sum(wide * d_weights, axis=0, keepdims=True)
-        d_scores = (wide * (d_weights - delta)).astype(BF16)
-        d_query = gathered(dot(d_scores, keys, 0, 0), rows) * scale
-        right_ref[:, lanes[0]] = d_query.astype(BF16)
-        right_ref[:, lanes[1]] = dot(d_scores, queries).astype(BF16)
-        right_ref[:, lanes[2]] = dot(weights, d_out).astype(BF16)
-    layer = mid + dot(left_ref[:, features:], out_ref[...])
-    layer_ref[:, :, 0] = layer.reshape(peers, frames, width, features).astype(BF16)
+    for row in range(lat):
+        part = slice(row * rows, (row + 1) * rows)
+        for g in range(features // LANES):
+            lanes = [
+                slice(s * features + g * LANES, s * features + (g + 1) * LANES) for s in range(3)
+            ]
+            queries = spread((packed_ref[part, lanes[0]] * scale).astype(BF16), mask)
+            keys = packed_ref[part, lanes[1]]
+            values = packed_ref[part, lanes[2]]
+            scores = jnp.where(same, dot(keys, queries, 1, 1), -1e30)
+            wide = softmax_rows(scores)
+            weights = wide.astype(BF16)
+            mixed = dot(weights, values, 0, 0)
+            left_ref[part, lanes[1]] = gathered(mixed, rows).astype(BF16)
+            d_out = spread(dproj_ref[part, lanes[0]], mask)
+            d_weights = dot(values, d_out, 1, 1)
+            delta = jnp.sum(wide * d_weights, axis=0, keepdims=True)
+            d_scores = (wide * (d_weights - delta)).astype(BF16)
+            d_query = gathered(dot(d_scores, keys, 0, 0), rows) * scale
+            right_ref[part, lanes[0]] = d_query.astype(BF16)
+            right_ref[part, lanes[1]] = dot(d_scores, queries).astype(BF16)
+            right_ref[part, lanes[2]] = dot(weights, d_out).astype(BF16)
+    layer = dot(left_ref[:, features:], out_ref[...])
     d_y = dot(right_ref[:, : 3 * features], qkv_ref[...], 1, 1)
-    d_mid = cot + norm_back(unit, inverse, gain, d_y)
-    dmid_ref[:, :, 0] = d_mid.reshape(peers, frames, width, features).astype(BF16)
+    shape = (peers, frames, width, features)
+    for row in range(lat):
+        part = slice(row * rows, (row + 1) * rows)
+        mid = by_row(mid_ref, row)
+        unit, inverse = normalized(mid)
+        d_mid = by_row(cot_ref, row) + norm_back(unit, inverse, gain, d_y[part])
+        both_ref[:, :frames, row] = d_mid.reshape(shape).astype(BF16)
+        both_ref[:, frames:, row] = (mid + layer[part]).reshape(shape).astype(BF16)
 
 
 def temporal(mid, cot, gain, qkv, out):
     peers, frames, lat, width, features = mid.shape
-    rows = peers * frames * width
-    moved = pl.BlockSpec((peers, frames, 1, width, features), lambda i: (0, 0, i, 0, 0))
-
-    def flat(columns):
-        return pl.BlockSpec((rows, columns), lambda i: (i, 0))
-
+    rows = peers * frames * lat * width
     return pl.pallas_call(
         temporal_kernel,
-        grid=(lat,),
-        in_specs=[moved, moved, full((1, features)), full(qkv.shape), full(out.shape)],
-        out_specs=[moved, moved, flat(2 * features), flat(4 * features)],
         out_shape=[
-            jax.ShapeDtypeStruct(mid.shape, BF16),
-            jax.ShapeDtypeStruct(mid.shape, BF16),
-            jax.ShapeDtypeStruct((lat * rows, 2 * features), BF16),
-            jax.ShapeDtypeStruct((lat * rows, 4 * features), BF16),
+            jax.ShapeDtypeStruct((peers, 2 * frames, lat, width, features), BF16),
+            jax.ShapeDtypeStruct((rows, 2 * features), BF16),
+            jax.ShapeDtypeStruct((rows, 4 * features), BF16),
         ],
         scratch_shapes=[
             pltpu.VMEM((rows, 3 * features), BF16),
@@ -230,17 +231,36 @@
     )(mid, cot, gain, qkv, out)
 
 
+def back_projection_kernel(dmid_ref, out_ref, dproj_ref):
+    rows, features = dproj_ref.shape[1:]
+    dmid = dmid_ref[...].astype(F32).reshape(rows, features).astype(BF16)
+    dproj_ref[0] = dot(dmid, out_ref[...], 1, 1).astype(BF16)
+
+
+def back_projection(dmid, out, frames):
+    peers, _, each, width, features = dmid.shape
+    rows = peers * each * width
+    return pl.pallas_call(
+        back_projection_kernel,
+        grid=(frames,),
+        in_specs=[grouped(peers, peers * each, width, features), full(out.shape)],
+        out_specs=per_step((rows, features)),
+        out_shape=jax.ShapeDtypeStruct((frames, rows, features), BF16),
+        compiler_params=pltpu.CompilerParams(vmem_limit_bytes=VMEM_LIMIT),
+        cost_estimate=cost(30),
+        name="back_projection",
+    )(dmid, out)
+
+
 def spatial_backward_kernel(
-    dmid_ref, out_ref, qkv_ref, q_ref, kv_ref, p_ref,
+    dproj_ref, qkv_ref, q_ref, kv_ref, p_ref,
     dq_ref, dkv_ref, own_ref, west_ref, east_ref,
-    dproj_ref, acc_ref,
+    acc_ref,
 ):
     _, lat, width, features = own_ref.shape
     rows = BH * width
     blocks = lat // BH
     step = 3 * rows
-    dmid = dmid_ref[...].astype(F32).reshape(lat * width, features).astype(BF16)
-    dproj_ref[...] = dot(dmid, out_ref[...], 1, 1).astype(BF16)
     mask = head_mask(rows)
     acc_ref[...] = jnp.zeros_like(acc_ref)
     offset = 0
@@ -251,7 +271,7 @@
             lanes = slice(g * LANES, (g + 1) * LANES)
             late = slice(features + g * LANES, features + (g + 1) * LANES)
             queries = spread(q_ref[0, block, lanes], mask)
-            d_out = spread(dproj_ref[block, lanes], mask)
+            d_out = spread(dproj_ref[0, block, lanes], mask)
             keys = kv_ref[0, low:high, lanes]
             values = kv_ref[0, low:high, late]
             weights = p_ref[0, g, offset : offset + span]
@@ -274,10 +294,9 @@
             ref[0, b * BH : (b + 1) * BH] = value.reshape(BH, width, features).astype(BF16)
 
 
-def spatial_backward(dmid, out, qkv, q, kv, p):
-    peers, frames, each, width, features = dmid.shape
-    lat = peers * each
-    rows = lat * width
+def spatial_backward(dproj, qkv, q, kv, p, lat):
+    frames, rows, features = dproj.shape
+    width = rows // lat
     outs = (
         (rows, features),
         (3 * rows, 2 * features),
@@ -289,8 +308,7 @@
         spatial_backward_kernel,
         grid=(frames,),
         in_specs=[
-            grouped(peers, lat, width, features),
-            full(out.shape),
+            per_step((rows, features)),
             full(qkv.shape),
             per_step(q.shape[1:]),
             per_step(kv.shape[1:]),
@@ -299,13 +317,12 @@
         out_specs=[per_step(shape) for shape in outs],
         out_shape=[jax.ShapeDtypeStruct((frames,) + shape, BF16) for shape in outs],
         scratch_shapes=[
-            pltpu.VMEM((rows, features), BF16),
             pltpu.VMEM((3 * rows, 2 * features), F32),
         ],
         compiler_params=pltpu.CompilerParams(vmem_limit_bytes=VMEM_LIMIT),
         cost_estimate=cost(20),
         name="spatial_backward",
-    )(dmid, out, qkv, q, kv, p)
+    )(dproj, qkv, q, kv, p)
 
 
 def final_kernel(tokens_ref, gain_ref, dmid_ref, own_ref, first_ref, second_ref, grad_ref):
@@ -337,19 +354,18 @@
     )(tokens, gain, dmid, own, first, second)
 
 
-def split_store(core_ref, term, keep_ref, send_ref, ring=1):
+def split_store(core_ref, term, keep_ref, send_ref):
     tiles, rows, columns = keep_ref.shape
     pairs = term.reshape(tiles, 2, rows, columns)
     first = core_ref[0] == 0
     for tile in range(tiles):
-        at = tile % ring * (tiles // ring) + tile // ring
         even, odd = pairs[tile, 0], pairs[tile, 1]
-        keep_ref[at] = jnp.where(first, even, odd).astype(BF16)
-        send_ref[at] = jnp.where(first, odd, even).astype(BF16)
-
-
-def term_time_kernel(ring, core_ref, left_ref, right_ref, keep_ref, send_ref):
-    split_store(core_ref, dot(left_ref[...], right_ref[...], 0, 0), keep_ref, send_ref, ring)
+        keep_ref[tile] = jnp.where(first, even, odd).astype(BF16)
+        send_ref[tile] = jnp.where(first, odd, even).astype(BF16)
+
+
+def term_time_kernel(core_ref, left_ref, right_ref, keep_ref, send_ref):
+    split_store(core_ref, dot(left_ref[...], right_ref[...], 0, 0), keep_ref, send_ref)
 
 
 def split_call(kernel, core, operands, specs, features, tiles, name, flops):
@@ -362,12 +378,12 @@
         ),
         out_shape=[jax.ShapeDtypeStruct(shape, BF16)] * 2,
         compiler_params=pltpu.CompilerParams(vmem_limit_bytes=VMEM_LIMIT),
-        cost_estimate=pl.CostEstimate(flops=flops, bytes_accessed=12 << 20, transcendentals=0),
+        cost_estimate=pl.CostEstimate(flops=flops, bytes_accessed=1, transcendentals=0),
         name=name,
     )(core, *operands)
 
 
-def term_time(core, left, right, tiles, ring):
+def term_time(core, left, right, tiles):
     rows, double = left.shape
     features = double // 2
     specs = [
@@ -375,8 +391,8 @@
         pl.BlockSpec((rows, features), lambda i, core: (0, i)),
     ]
     return split_call(
-        functools.partial(term_time_kernel, ring), core, (left, right), specs, features, tiles,
-        "term_time", 2 * 10**9,
+        term_time_kernel, core, (left, right), specs, features, tiles,
+        "term_time", 1,
     )
 
 
@@ -423,17 +439,31 @@
         whole(dq),
         pl.BlockSpec(dkv.shape[:2] + (features,), lambda i, core: (0, 0, jnp.clip(i - 1, 0, 1))),
         whole(o),
-        whole(dmid),
+        pl.BlockSpec(
+            (dmid.shape[0], y.shape[0]) + dmid.shape[2:], lambda i, core: (0,) * dmid.ndim
+        ),
     ]
     return split_call(
-        term_space_kernel, core, (y, dq, dkv, o, dmid), specs, features, tiles, "term_space",
-        4 * 10**9,
-    )
+        term_space_kernel, core, (y, dq, dkv, o, dmid), specs, features, tiles, "term_space", 1,
+    )
+
+
+def add_kernel(left_ref, right_ref, sum_ref):
+    sum_ref[...] = (left_ref[...].astype(F32) + right_ref[...].astype(F32)).astype(BF16)
 
 
 def paired(keep, send):
     got = lax.ppermute(send, "core", [(0, 1), (1, 0)])
-    return (keep.astype(F32) + got.astype(F32)).astype(BF16)
+    block = pl.BlockSpec((1,) + keep.shape[1:], lambda i: (i, 0, 0))
+    return pl.pallas_call(
+        add_kernel,
+        grid=(keep.shape[0],),
+        in_specs=[block, block],
+        out_specs=block,
+        out_shape=jax.ShapeDtypeStruct(keep.shape, BF16),
+        cost_estimate=pl.CostEstimate(flops=1, bytes_accessed=1, transcendentals=0),
+        name="pair_sum",
+    )(keep, got)
 
 
 def folded(array, *lead):
@@ -455,17 +485,10 @@
     return total
 
 
-def summed_over_y(mine):
-    return lax.psum_scatter(
-        mine.reshape(-1, mine.shape[-1]), "y", scatter_dimension=0, tiled=True
-    )
-
-
-def summed_over_zx(part):
-    halves, z, xhi = lax.axis_size("xlo"), lax.axis_size("z"), lax.axis_size("xhi")
-    pieces = folded(part, halves, z, xhi).transpose(1, 0, 2, 3, 4)
-    after_z = ring_sum(pieces, "z").astype(BF16)
-    return ring_sum(after_z.reshape((halves * xhi,) + after_z.shape[2:]), ("xlo", "xhi"))
+def summed_by_frame(part):
+    z, xhi = lax.axis_size("z"), lax.axis_size("xhi")
+    after_z = ring_sum(folded(part, z, xhi), "z").astype(BF16)
+    return ring_sum(after_z, "xhi")
 
 
 def summed_at_once(mine):
@@ -515,26 +538,26 @@
     y_s, q_s, kv_s, p_s, o_s, mid = spatial_forward(
         tokens, west, east, gain_s, qkv_space, out_space, peers
     )
-    layer_rows, dmid_rows, left_t, right_t = temporal(
-        exchanged(mid), cot_rows, gain_t, qkv_time, out_time
-    )
-    dmid = exchanged(dmid_rows)
-    keep_t, send_t = term_time(core, left_t, right_t, tiles, lax.axis_size("y"))
+    both_rows, left_t, right_t = temporal(exchanged(mid), cot_rows, gain_t, qkv_time, out_time)
+    both = exchanged(both_rows)
+    keep_t, send_t = term_time(core, left_t, right_t, tiles)
     mine_t = paired(keep_t, send_t)
-    dmid, mine_t, layer_rows = lax.optimization_barrier((dmid, mine_t, layer_rows))
-    part_t = summed_over_y(mine_t)
-    layer_chunks = exchanged(layer_rows)
-    dq, dkv, own, for_west, for_east = spatial_backward(dmid, out_space, qkv_space, q_s, kv_s, p_s)
+    dproj = back_projection(both, out_space, frames)
+    dproj, mine_t = lax.optimization_barrier((dproj, mine_t))
+    arrived_t = lax.all_to_all(mine_t, ("xlo", "y"), 0, 0, tiled=False)
+    dq, dkv, own, for_west, for_east = spatial_backward(dproj, qkv_space, q_s, kv_s, p_s, lat)
     from_east = shifted(for_west, -1)
     from_west = shifted(for_east, 1)
-    keep_s, send_s = term_space(core, y_s, dq, dkv, o_s, dmid, tiles)
-    send_s, layer_chunks = lax.optimization_barrier((send_s, layer_chunks))
+    keep_s, send_s = term_space(core, y_s, dq, dkv, o_s, both, tiles)
+    send_s, arrived_t, from_east, from_west = lax.optimization_barrier(
+        (send_s, arrived_t, from_east, from_west)
+    )
     mine_s = paired(keep_s, send_s)
-    mine_s, part_t = lax.optimization_barrier((mine_s, part_t))
     summed_space = summed_at_once(mine_s)
-    summed_time = summed_over_zx(part_t)
-    layer_out = layer_chunks.transpose(1, 0, 2, 3, 4).reshape(tokens.shape)
-    grad_tokens = final_norm(tokens, gain_s, dmid, own, from_east, from_west)
+    part_t = jnp.sum(arrived_t.astype(F32), axis=0).astype(BF16)
+    summed_time = summed_by_frame(part_t)
+    layer_out = both[:, frames:].transpose(1, 0, 2, 3, 4).reshape(tokens.shape)
+    grad_tokens = final_norm(tokens, gain_s, both, own, from_east, from_west)
     return (
         (layer_out, grad_tokens)
         + finished(summed_space, qkv_space, gain_space, total)

time: 211 us -> 209 us (level)
  between operations: 14.2 us -> 0.81 us
  Pallas kernels: 70.5 us -> 82.5 us
  waiting for transfers between devices: 50.2 us -> 41.5 us
  starting transfers between devices: 50 us -> 56.7 us
  local copies, waits for them, and re-layouts: 12.4 us -> 17.9 us
  other arithmetic: 12.7 us -> 8.63 us
    all_to_all x0 -> x1, starting transfers between devices: none -> 13.5 us  [shards(): arrived_t = lax.all_to_all(mine_t, ('xlo', 'y'), 0, 0, tiled=False)]
    pallas_call x2 -> x5, Pallas kernels: 37.5 us -> 49.4 us  [the longest x1 18.6 us: spatial_backward(): pl.pallas_call(spatial_backward_kernel, grid=(frames,), in_specs=[per_ste...]
    convert_element_type x3 -> x1, other arithmetic: 7.85 us -> 0.93 us  [summed_by_frame(): after_z = ring_sum(folded(part, z, xhi), 'z').astype(BF16)]
    all_to_all x1, starting transfers between devices: 10.3 us -> 4.7 us  [summed_at_once(): arrived = lax.all_to_all(folded(mine, count), rest, 0, 0, tiled=False)]
    ppermute x6 -> x4, waiting for transfers between devices: 26.9 us -> 21.9 us  [ring_sum(): lax.ppermute(chunk(by), axis, [(i, (i + by) % size) for i in range(size)])]
    all_to_all x4 -> x3, waiting for transfers between devices: 16.4 us -> 11.6 us  [exchanged(): return lax.all_to_all(chunks, FRAME, 0, 0, tiled=False)]
    all_to_all x4 -> x3, starting transfers between devices: 21.2 us -> 17.7 us  [exchanged(): return lax.all_to_all(chunks, FRAME, 0, 0, tiled=False)]
    ppermute x4, waiting for transfers between devices: 0.01 us -> 3.5 us  [shifted(): lax.ppermute(shard, TILE, [(i, (i + by) % size) for i in range(size)])]
  transfers between devices with their start and end apart: 18 -> 15, of which waited for: 9 -> 7; matrix products, arithmetic and copies ran while one was open for 8% -> 6% of each run, Pallas kernels for 22% -> 26%
where the time goes in v3:
time: 209 us; the launch traced here: 208 us
  Pallas kernels  82.5 us (39%)
  starting transfers between devices  56.7 us (27%)
  waiting for transfers between devices  41.5 us (20%)
  local copies, waits for them, and re-layouts  17.9 us (9%)
  other arithmetic  8.63 us (4%)
    ppermute x4, waiting for transfers between devices, ring_sum(): lax.ppermute(chunk(by), axis, [(i, (i + by) % size) for i in range(size)])  21.9 us
    pallas_call x1, Pallas kernels, spatial_backward(): pl.pallas_call(spatial_backward_kernel, grid=(frames,), in_specs=[per_ste...  18.6 us
    all_to_all x3, starting transfers between devices, exchanged(): return lax.all_to_all(chunks, FRAME, 0, 0, tiled=False)  17.7 us
    pallas_call x2, Pallas kernels, split_call(): pl.pallas_call(kernel, grid_spec=pltpu.PrefetchScalarGridSpec(num_scalar_...  15.7 us
    pallas_call x1, Pallas kernels, temporal(): pl.pallas_call(temporal_kernel, out_shape=[jax.ShapeDtypeStruct((peers, 2...  14.8 us
    pallas_call x1, Pallas kernels, spatial_forward(): pl.pallas_call(spatial_forward_kernel, grid=(frames,), in_specs=[per_step...  14.3 us
    all_to_all x1, starting transfers between devices, shards(): arrived_t = lax.all_to_all(mine_t, ('xlo', 'y'), 0, 0, tiled=False)  13.5 us
    pallas_call x2, Pallas kernels, paired(): pl.pallas_call(add_kernel, grid=(keep.shape[0],), in_specs=[block, block]...  12.8 us
  transfers between devices with their start and end apart: 15, of which 7 were waited for; matrix products, arithmetic and copies ran while one was open for 6% of the time, Pallas kernels for 26%

profile of v3, /device:TPU:1, one launch (start us, length us, event | category | flops | bytes accessed | tf_op | source)
XLA Modules:
  0.0 208.1 jit_solution(14663659277463352894)
XLA Ops:
  0.6 2.8 %collective-permute-start = (bf16[2,24,8,768]{3,2,1,0:T(8,128)(2,1)}, bf16[2,24,8,768]{3,2,1,0:T(8,128)(2,1)S(1)}, u32[]{:S(2)}, u32[]{:S(2)}) collective-permute-start(bf16[2,24,8,768]{3,2,1,0:T(8,128)(2,1)} %tokens_ref.1), channel_id=1, source_target_pairs={{0,8},{8,16},{16,24},{24,32},{32,40},{40,48},{48,56},{56,64},{64,7... | collective-permute-start | bytes 1769480 | tf_op jit(solution)/shard_map/ppermute | solution.py:503
  3.4 1.9 copy.19
  5.3 7.5 %all-to-all-start.1 = ((bf16[8,2,3,8,768]{4,3,2,1,0:T(8,128)(2,1)}), bf16[8,2,3,8,768]{4,3,2,1,0:T(8,128)(2,1)S(1)}, u32[]{:S(2)}, u32[]{:S(2)}) async-start(bf16[8,2,3,8,768]{4,3,2,1,0:T(8,128)(2,1)} %bitcast.21), calls=%async_computation.1 | async-start | bytes 1179648 | tf_op jit(solution)/shard_map/all_to_all | solution.py:532
  15.1 14.3 %spatial_forward.1 = (bf16[2,576,768]{2,1,0:T(8,128)(2,1)}, bf16[2,192,768]{2,1,0:T(8,128)(2,1)}, bf16[2,576,1536]{2,1,0:T(8,128)(2,1)}, bf16[2,3,1344,256]{3,2,...) custom-call(bf16[2,24,8,768]{3,2,1,0:T(8,128)(2,1)} %tokens_ref.1, ...), custom_call_target="tpu_custom_call" | custom-call | flops 14000000000 | bytes 4194304 | tf_op jit(solution)/shard_map/spatial_forward/pallas_call | solution.py:142
  29.4 6.7 %all-to-all-start = ((bf16[8,2,3,8,768]{4,3,2,1,0:T(8,128)(2,1)}), bf16[8,2,3,8,768]{4,3,2,1,0:T(8,128)(2,1)S(1)}, u32[]{:S(2)}, u32[]{:S(2)}) async-start(bf16[8,2,3,8,768]{4,3,2,1,0:T(8,128)(2,1)} %get-tuple-element.32), calls=%async_computation | async-start | bytes 1179648 | tf_op jit(solution)/shard_map/all_to_all | solution.py:532
  36.6 8.9 %all-to-all-done.mid_ref = bf16[8,2,3,8,768]{4,3,2,1,0:T(8,128)(2,1)S(1)} async-done(((bf16[8,2,3,8,768]{4,3,2,1,0:T(8,128)(2,1)}), bf16[8,2,3,8,768]{4,3,2,1,0:T(8,128)(2,1)S(1)}, u32[]{:S(2)}, u32[]{:S(2)}) %all-to-all-start) | async-done | bytes 589856 | tf_op jit(solution)/shard_map/all_to_all | solution.py:532
  46.4 14.8 %temporal.1 = (bf16[8,4,3,8,768]{4,3,2,1,0:T(8,128)(2,1)}, bf16[384,1536]{1,0:T(8,128)(2,1)}, bf16[384,3072]{1,0:T(8,128)(2,1)}) custom-call(bf16[8,2,3,8,768]{4,3,2,1,0:T(8,128)(2,1)} %copy-done.5, bf16[8,2,3,8,768]{4,3,2,1,0:T(8,128)(2,1)} %copy-done.4, f32[1,768]{1,0:T(1,128)} %reshape.49.gain_ref, bf16[768,2304]{1,0:T(8,128)(2,1)} %qkv_ref.4, ...), custom_call_target="tpu_custom_call" | custom-call | flops 17999998976 | bytes 4194304 | tf_op jit(solution)/shard_map/temporal/pallas_call | solution.py:217
  61.2 3.6 %all-to-all-start.2 = ((bf16[8,4,3,8,768]{4,3,2,1,0:T(8,128)(2,1)}), bf16[8,4,3,8,768]{4,3,2,1,0:T(8,128)(2,1)S(1)}, u32[]{:S(2)}, u32[]{:S(2)}) async-start(bf16[8,4,3,8,768]{4,3,2,1,0:T(8,128)(2,1)} %get-tuple-element.33), calls=%async_computation.2 | async-start | bytes 2359296 | tf_op jit(solution)/shard_map/all_to_all | solution.py:532
  64.8 6.6 %term_time.1 = (bf16[8,48,3072]{2,1,0:T(8,128)(2,1)}, bf16[8,48,3072]{2,1,0:T(8,128)(2,1)}) custom-call(s32[1]{0:T(128)} %bitcast.4.core_ref, bf16[384,1536]{1,0:T(8,128)(2,1)} %get-tuple-element.34.left_ref, bf16[384,3072]{1,0:T(8,128)(2,1)} %get-tuple-element.35.right_ref), custom_call_target="tpu_custom_call" | custom-call | flops 1 | bytes 1 | tf_op jit(solution)/shard_map/term_time/pallas_call | solution.py:374
  71.3 4.5 %collective-permute-start.2 = (bf16[8,48,3072]{2,1,0:T(8,128)(2,1)}, bf16[8,48,3072]{2,1,0:T(8,128)(2,1)S(1)}, u32[]{:S(2)}, u32[]{:S(2)}) collective-permute-start(bf16[8,48,3072]{2,1,0:T(8,128)(2,1)} %get-tuple-element.37), channel_id=1, source_target_pairs={{0,8},{8,0},{1,9},{9,1},{2,10},{10,2},{3,11},{11,3},{4,12},{12,4},... | collective-permute-start | bytes 7077896 | tf_op jit(solution)/shard_map/ppermute | solution.py:456
  75.9 2.7 %all-to-all-done.2.dmid_ref = bf16[8,4,3,8,768]{4,3,2,1,0:T(8,128)(2,1)S(1)} async-done(((bf16[8,4,3,8,768]{4,3,2,1,0:T(8,128)(2,1)}), bf16[8,4,3,8,768]{4,3,2,1,0:T(8,128)(2,1)S(1)}, u32[]{:S(2)}, u32[]{:S(2)}) %all-to-all-start.2) | async-done | bytes 1179680 | tf_op jit(solution)/shard_map/all_to_all | solution.py:532
  79.6 3.2 %back_projection.1.dproj_ref = bf16[2,192,768]{2,1,0:T(8,128)(2,1)} custom-call(bf16[8,4,3,8,768]{4,3,2,1,0:T(8,128)(2,1)} %copy-done.1, bf16[768,768]{1,0:T(8,128)(2,1)} %out_ref.5), custom_call_target="tpu_custom_call" | custom-call | flops 30000001024 | bytes 4194304 | tf_op jit(solution)/shard_map/back_projection/pallas_call | solution.py:243
  84.2 6.4 %pair_sum.2 = bf16[8,48,3072]{2,1,0:T(8,128)(2,1)} custom-call(bf16[8,48,3072]{2,1,0:T(8,128)(2,1)} %get-tuple-element.36.left_ref, bf16[8,48,3072]{2,1,0:T(8,128)(2,1)} %copy-done.3), custom_call_target="tpu_custom_call" | custom-call | flops 1 | bytes 1 | tf_op jit(solution)/shard_map/pair_sum/pallas_call | solution.py:458
  90.6 13.5 %all-to-all-start.3 = ((bf16[8,48,3072]{2,1,0:T(8,128)(2,1)}), bf16[8,48,3072]{2,1,0:T(8,128)(2,1)S(1)}, u32[]{:S(2)}, u32[]{:S(2)}) async-start(bf16[8,48,3072]{2,1,0:T(8,128)(2,1)} %pair_sum.2), calls=%async_computation.3 | async-start | bytes 4718592 | tf_op jit(solution)/shard_map/all_to_all | solution.py:547
  104.1 18.6 %spatial_backward.1 = (bf16[2,192,768]{2,1,0:T(8,128)(2,1)}, bf16[2,576,1536]{2,1,0:T(8,128)(2,1)}, bf16[2,24,8,768]{3,2,1,0:T(8,128)(2,1)}, bf16[2,24,8,768]{3,2,1,0:T(8,128)(2,1)}, bf16[2,24,8,768]{3,2,1,0:T(8,128)(2,1)}) custom-call(bf16[2,192,768]{2,1,0:T(8,128)(2,1)} %back_projection.1.dproj_ref, bf16[768,2304]{1,0:T(8,128)(2,1)} %qkv_ref.5, ...), custom_call_target="tpu_custom_call" | custom-call | flops 20000000000 | bytes 4194304 | tf_op jit(solution)/shard_map/spatial_backward/pallas_call | solution.py:307
  124.3 1.7 collective-permute-start.4
  126.1 9.1 %term_space.1 = (bf16[8,48,3072]{2,1,0:T(8,128)(2,1)}, bf16[8,48,3072]{2,1,0:T(8,128)(2,1)}) custom-call(s32[1]{0:T(128)} %bitcast.4.core_ref, bf16[2,576,768]{2,1,0:T(8,128)(2,1)} %get-tuple-element.43.y_ref, bf16[2,192,768]{2,1,0:T(8,128)(2,1)} %get-tuple-element.44.dq_ref, bf16[2,576,1536]{2,1,0:T(8,128)(2,1)} %get-tuple-element.45.dkv_ref, ...), custom_call_target="tpu_custom_call" | custom-call | flops 1 | bytes 1 | tf_op jit(solution)/shard_map/term_space/pallas_call | solution.py:374
  135.1 3.5 %collective-permute-done.3.first_ref = bf16[2,24,8,768]{3,2,1,0:T(8,128)(2,1)S(1)} collective-permute-done((bf16[2,24,8,768]{3,2,1,0:T(8,128)(2,1)}, bf16[2,24,8,768]{3,2,1,0:T(8,128)(2,1)S(1)}, u32[]{:S(2)}, u32[]{:S(2)}) %collective-permute-start.3) | collective-permute-done | bytes 589856 | tf_op jit(solution)/shard_map/ppermute | solution.py:503
  138.7 3.0 %collective-permute-start.5 = (bf16[8,48,3072]{2,1,0:T(8,128)(2,1)}, bf16[8,48,3072]{2,1,0:T(8,128)(2,1)}, u32[]{:S(2)}, u32[]{:S(2)}) collective-permute-start(bf16[8,48,3072]{2,1,0:T(8,128)(2,1)} %get-tuple-element.54), channel_id=1, source_target_pairs={{0,8},{8,0},{1,9},{9,1},{2,10},{10,2},{3,11},{11,3},{4,12},{12,4},... | collective-permute-start | bytes 7077896 | tf_op jit(solution)/shard_map/ppermute | solution.py:456
  141.7 4.5 %collective-permute-done.5.right_ref = bf16[8,48,3072]{2,1,0:T(8,128)(2,1)} collective-permute-done((bf16[8,48,3072]{2,1,0:T(8,128)(2,1)}, bf16[8,48,3072]{2,1,0:T(8,128)(2,1)}, u32[]{:S(2)}, u32[]{:S(2)}) %collective-permute-start.5) | collective-permute-done | bytes 2359328 | tf_op jit(solution)/shard_map/ppermute | solution.py:456
  146.2 6.4 %pair_sum.3 = bf16[8,48,3072]{2,1,0:T(8,128)(2,1)} custom-call(bf16[8,48,3072]{2,1,0:T(8,128)(2,1)} %get-tuple-element.53.left_ref, bf16[8,48,3072]{2,1,0:T(8,128)(2,1)} %collective-permute-done.5.right_ref), custom_call_target="tpu_custom_call" | custom-call | flops 1 | bytes 1 | tf_op jit(solution)/shard_map/pair_sum/pallas_call | solution.py:458
  152.6 4.9 %reshape.52 = bf16[64,144,128]{2,1,0:T(8,128)(2,1)} reshape(bf16[8,48,3072]{2,1,0:T(8,128)(2,1)} %pair_sum.3) | data formatting | bytes 4718592 | tf_op jit(solution)/shard_map/reshape | solution.py:470
  157.5 4.7 %all-to-all-start.4 = ((bf16[64,144,128]{2,1,0:T(8,128)(2,1)}), bf16[64,144,128]{2,1,0:T(8,128)(2,1)S(1)}, u32[]{:S(2)}, u32[]{:S(2)}) async-start(bf16[64,144,128]{2,1,0:T(8,128)(2,1)} %reshape.52), calls=%async_computation.4 | async-start | bytes 4718592 | tf_op jit(solution)/shard_map/all_to_all | solution.py:497
  162.2 2.9 %reduce_sum.41 = bf16[48,3072]{1,0:T(8,128)(2,1)} reduce(bf16[8,48,3072]{2,1,0:T(8,128)(2,1)} %copy-done, bf16[]{:T(256)} %constant.47.clone.1), dimensions={0}, to_apply=%region_2.3 | reduce | flops 1032192 | bytes 2654210 | tf_op jit(solution)/shard_map/reduce_sum | solution.py:557
  165.1 1.8 reshape.53
  168.9 2.4 %collective-permute-start.7 = (bf16[2,144,128]{2,1,0:T(8,128)(2,1)S(1)}, bf16[2,144,128]{2,1,0:T(8,128)(2,1)S(1)}, u32[]{:S(2)}, u32[]{:S(2)}) collective-permute-start(bf16[2,144,128]{2,1,0:T(8,128)(2,1)S(1)} %get-tuple-element.62), channel_id=1, source_target_pairs={{0,4},{2,6},{4,0},{6,2},{1,5},{3,7},{5,1},{7,3},{8,12},{10,14},{12... | collective-permute-start | bytes 221192 | tf_op jit(solution)/shard_map/ppermute | solution.py:483
  174.8 13.5 %collective-permute-done.7 = bf16[2,144,128]{2,1,0:T(8,128)(2,1)S(1)} collective-permute-done((bf16[2,144,128]{2,1,0:T(8,128)(2,1)S(1)}, bf16[2,144,128]{2,1,0:T(8,128)(2,1)S(1)}, u32[]{:S(2)}, u32[]{:S(2)}) %collective-permute-start.7) | collective-permute-done | bytes 73760 | tf_op jit(solution)/shard_map/ppermute | solution.py:483
  188.3 6.9 %collective-permute-done.8 = bf16[2,144,128]{2,1,0:T(8,128)(2,1)S(1)} collective-permute-done((bf16[2,144,128]{2,1,0:T(8,128)(2,1)S(1)}, bf16[2,144,128]{2,1,0:T(8,128)(2,1)S(1)}, u32[]{:S(2)}, u32[]{:S(2)}) %collective-permute-start.8) | collective-permute-done | bytes 73760 | tf_op jit(solution)/shard_map/ppermute | solution.py:483
  196.2 2.6 %collective-permute-start.9 = (bf16[144,128]{1,0:T(8,128)(2,1)S(1)}, bf16[144,128]{1,0:T(8,128)(2,1)S(1)}, u32[]{:S(2)}, u32[]{:S(2)}) collective-permute-start(bf16[144,128]{1,0:T(8,128)(2,1)S(1)} %dynamic-slice_bitcast_fusion.3), channel_id=1, source_target_pairs={{0,1},{1,0},{2,3},{3,2},{4,5},{5,4},{6,7},{7,6},{8,9},{9,8},{10,11... | collective-permute-start | bytes 110600 | tf_op jit(solution)/shard_map/ppermute | solution.py:483
  198.8 3.2 %final_norm.1 = f32[2,24,8,768]{3,2,1,0:T(8,128)} custom-call(bf16[2,24,8,768]{3,2,1,0:T(8,128)(2,1)} %tokens_ref.1, f32[1,768]{1,0:T(1,128)} %reshape.47.gain_ref, bf16[8,4,3,8,768]{4,3,2,1,0:T(8,128)(2,1)} %copy-done.1, bf16[2,24,8,768]{3,2,1,0:T(8,128)(2,1)} %get-tuple-element.42.own_ref, bf16[2,24,8,768]{3,2,1,0:T(8,128)(2,1)} %copy-done.8, ...), custom_call_target="tpu_custom_call" | custom-call | flops 3000000000 | bytes 4194304 | tf_op jit(solution)/shard_map/final_norm/pallas_call | solution.py:344
  202.6 1.6 multiply_reduce_fusion
  205.2 1.6 multiply_reduce_fusion.1
  (53 shorter events, 16.9 us)
Async XLA Ops:
  0.6 12.2 %copy-start.7 = (f32[768]{0:T(1024)S(1)}, f32[768]{0:T(1024)}, u32[]{:S(2)}) copy-start(f32[768]{0:T(1024)} %param.9) | copy-start | bytes 9220
  0.6 12.8 %collective-permute-start = (bf16[2,24,8,768]{3,2,1,0:T(8,128)(2,1)}, bf16[2,24,8,768]{3,2,1,0:T(8,128)(2,1)S(1)}, u32[]{:S(2)}, u32[]{:S(2)}) collective-permute-start(bf16[2,24,8,768]{3,2,1,0:T(8,128)(2,1)} %tokens_ref.1), channel_id=1, source_target_pairs={{0,8},{8,16},{16,24},{24,32},{32,40},{40,48},{48,56},{56,64},{64,7... | collective-permute-start | bytes 1769480 | tf_op jit(solution)/shard_map/ppermute | solution.py:503
  3.4 10.0 %collective-permute-start.1 = (bf16[2,24,8,768]{3,2,1,0:T(8,128)(2,1)}, bf16[2,24,8,768]{3,2,1,0:T(8,128)(2,1)S(1)}, u32[]{:S(2)}, u32[]{:S(2)}) collective-permute-start(bf16[2,24,8,768]{3,2,1,0:T(8,128)(2,1)} %tokens_ref.1), channel_id=1, source_target_pairs={{0,120},{8,0},{16,8},{24,16},{32,24},{40,32},{48,40},{56,48},{64,5... | collective-permute-start | bytes 1769480 | tf_op jit(solution)/shard_map/ppermute | solution.py:503
  5.3 24.0 %all-to-all-start.1 = ((bf16[8,2,3,8,768]{4,3,2,1,0:T(8,128)(2,1)}), bf16[8,2,3,8,768]{4,3,2,1,0:T(8,128)(2,1)S(1)}, u32[]{:S(2)}, u32[]{:S(2)}) async-start(bf16[8,2,3,8,768]{4,3,2,1,0:T(8,128)(2,1)} %bitcast.21), calls=%async_computation.1 | async-start | bytes 1179648 | tf_op jit(solution)/shard_map/all_to_all | solution.py:532
  13.4 22.6 %copy-start.6 = (f32[768]{0:T(1024)S(1)}, f32[768]{0:T(1024)}, u32[]{:S(2)}) copy-start(f32[768]{0:T(1024)} %param.12) | copy-start | bytes 9220
  13.4 0.8 copy-start.10
  14.2 0.8 copy-start.11
  29.4 16.2 %copy-start.4 = (bf16[8,2,3,8,768]{4,3,2,1,0:T(8,128)(2,1)}, bf16[8,2,3,8,768]{4,3,2,1,0:T(8,128)(2,1)S(1)}, u32[]{:S(2)}) copy-start(bf16[8,2,3,8,768]{4,3,2,1,0:T(8,128)(2,1)S(1)} %all-to-all-done.1.cot_ref) | copy-start | bytes 1769476
  29.4 16.2 %all-to-all-start = ((bf16[8,2,3,8,768]{4,3,2,1,0:T(8,128)(2,1)}), bf16[8,2,3,8,768]{4,3,2,1,0:T(8,128)(2,1)S(1)}, u32[]{:S(2)}, u32[]{:S(2)}) async-start(bf16[8,2,3,8,768]{4,3,2,1,0:T(8,128)(2,1)} %get-tuple-element.32), calls=%async_computation | async-start | bytes 1179648 | tf_op jit(solution)/shard_map/all_to_all | solution.py:532
  45.6 0.8 copy-start.5
  61.2 17.4 %all-to-all-start.2 = ((bf16[8,4,3,8,768]{4,3,2,1,0:T(8,128)(2,1)}), bf16[8,4,3,8,768]{4,3,2,1,0:T(8,128)(2,1)S(1)}, u32[]{:S(2)}, u32[]{:S(2)}) async-start(bf16[8,4,3,8,768]{4,3,2,1,0:T(8,128)(2,1)} %get-tuple-element.33), calls=%async_computation.2 | async-start | bytes 2359296 | tf_op jit(solution)/shard_map/all_to_all | solution.py:532
  71.3 11.5 %collective-permute-start.2 = (bf16[8,48,3072]{2,1,0:T(8,128)(2,1)}, bf16[8,48,3072]{2,1,0:T(8,128)(2,1)S(1)}, u32[]{:S(2)}, u32[]{:S(2)}) collective-permute-start(bf16[8,48,3072]{2,1,0:T(8,128)(2,1)} %get-tuple-element.37), channel_id=1, source_target_pairs={{0,8},{8,0},{1,9},{9,1},{2,10},{10,2},{3,11},{11,3},{4,12},{12,4},... | collective-permute-start | bytes 7077896 | tf_op jit(solution)/shard_map/ppermute | solution.py:456
  78.5 1.0 copy-start.1
  82.8 1.4 copy-start.3
  90.6 48.0 %all-to-all-start.3 = ((bf16[8,48,3072]{2,1,0:T(8,128)(2,1)}), bf16[8,48,3072]{2,1,0:T(8,128)(2,1)S(1)}, u32[]{:S(2)}, u32[]{:S(2)}) async-start(bf16[8,48,3072]{2,1,0:T(8,128)(2,1)} %pair_sum.2), calls=%async_computation.3 | async-start | bytes 4718592 | tf_op jit(solution)/shard_map/all_to_all | solution.py:547
  122.7 15.9 %collective-permute-start.3 = (bf16[2,24,8,768]{3,2,1,0:T(8,128)(2,1)}, bf16[2,24,8,768]{3,2,1,0:T(8,128)(2,1)S(1)}, u32[]{:S(2)}, u32[]{:S(2)}) collective-permute-start(bf16[2,24,8,768]{3,2,1,0:T(8,128)(2,1)} %get-tuple-element.49), channel_id=1, source_target_pairs={{0,120},{8,0},{16,8},{24,16},{32,24},{40,32},{48,40},{56,48},{64,5... | collective-permute-start | bytes 1769480 | tf_op jit(solution)/shard_map/ppermute | solution.py:503
  124.3 14.3 %collective-permute-start.4 = (bf16[2,24,8,768]{3,2,1,0:T(8,128)(2,1)}, bf16[2,24,8,768]{3,2,1,0:T(8,128)(2,1)S(1)}, u32[]{:S(2)}, u32[]{:S(2)}) collective-permute-start(bf16[2,24,8,768]{3,2,1,0:T(8,128)(2,1)} %get-tuple-element.50), channel_id=1, source_target_pairs={{0,8},{8,16},{16,24},{24,32},{32,40},{40,48},{48,56},{56,64},{64,7... | collective-permute-start | bytes 1769480 | tf_op jit(solution)/shard_map/ppermute | solution.py:503
  138.6 13.9 %copy-start.8 = (bf16[2,24,8,768]{3,2,1,0:T(8,128)(2,1)}, bf16[2,24,8,768]{3,2,1,0:T(8,128)(2,1)S(1)}, u32[]{:S(2)}) copy-start(bf16[2,24,8,768]{3,2,1,0:T(8,128)(2,1)S(1)} %collective-permute-done.3.first_ref) | copy-start | bytes 1769476
  138.6 13.9 %copy-start.9 = (bf16[2,24,8,768]{3,2,1,0:T(8,128)(2,1)}, bf16[2,24,8,768]{3,2,1,0:T(8,128)(2,1)S(1)}, u32[]{:S(2)}) copy-start(bf16[2,24,8,768]{3,2,1,0:T(8,128)(2,1)S(1)} %collective-permute-done.4.second_ref) | copy-start | bytes 1769476
  138.6 13.9 %copy-start = (bf16[8,48,3072]{2,1,0:T(8,128)(2,1)}, bf16[8,48,3072]{2,1,0:T(8,128)(2,1)S(1)}, u32[]{:S(2)}) copy-start(bf16[8,48,3072]{2,1,0:T(8,128)(2,1)S(1)} %all-to-all-done.3) | copy-start | bytes 7077892
  138.7 7.5 %collective-permute-start.5 = (bf16[8,48,3072]{2,1,0:T(8,128)(2,1)}, bf16[8,48,3072]{2,1,0:T(8,128)(2,1)}, u32[]{:S(2)}, u32[]{:S(2)}) collective-permute-start(bf16[8,48,3072]{2,1,0:T(8,128)(2,1)} %get-tuple-element.54), channel_id=1, source_target_pairs={{0,8},{8,0},{1,9},{9,1},{2,10},{10,2},{3,11},{11,3},{4,12},{12,4},... | collective-permute-start | bytes 7077896 | tf_op jit(solution)/shard_map/ppermute | solution.py:456
  157.5 47.4 %all-to-all-start.4 = ((bf16[64,144,128]{2,1,0:T(8,128)(2,1)}), bf16[64,144,128]{2,1,0:T(8,128)(2,1)S(1)}, u32[]{:S(2)}, u32[]{:S(2)}) async-start(bf16[64,144,128]{2,1,0:T(8,128)(2,1)} %reshape.52), calls=%async_computation.4 | async-start | bytes 4718592 | tf_op jit(solution)/shard_map/all_to_all | solution.py:497
  162.2 10.3 %copy-start.2 = (bf16[8,4,3,8,768]{4,3,2,1,0:T(8,128)(2,1)S(1)}, bf16[8,4,3,8,768]{4,3,2,1,0:T(8,128)(2,1)}, u32[]{:S(2)}) copy-start(bf16[8,4,3,8,768]{4,3,2,1,0:T(8,128)(2,1)} %copy-done.1) | copy-start | bytes 3538948
  167.9 6.9 %collective-permute-start.6 = (bf16[2,144,128]{2,1,0:T(8,128)(2,1)S(1)}, bf16[2,144,128]{2,1,0:T(8,128)(2,1)S(1)}, u32[]{:S(2)}, u32[]{:S(2)}) collective-permute-start(bf16[2,144,128]{2,1,0:T(8,128)(2,1)S(1)} %get-tuple-element.60), channel_id=1, source_target_pairs={{0,2},{2,4},{4,6},{6,0},{1,3},{3,5},{5,7},{7,1},{8,10},{10,12},{12... | collective-permute-start | bytes 221192 | tf_op jit(solution)/shard_map/ppermute | solution.py:483
  168.9 19.4 %collective-permute-start.7 = (bf16[2,144,128]{2,1,0:T(8,128)(2,1)S(1)}, bf16[2,144,128]{2,1,0:T(8,128)(2,1)S(1)}, u32[]{:S(2)}, u32[]{:S(2)}) collective-permute-start(bf16[2,144,128]{2,1,0:T(8,128)(2,1)S(1)} %get-tuple-element.62), channel_id=1, source_target_pairs={{0,4},{2,6},{4,0},{6,2},{1,5},{3,7},{5,1},{7,3},{8,12},{10,14},{12... | collective-permute-start | bytes 221192 | tf_op jit(solution)/shard_map/ppermute | solution.py:483
  171.3 23.9 %collective-permute-start.8 = (bf16[2,144,128]{2,1,0:T(8,128)(2,1)S(1)}, bf16[2,144,128]{2,1,0:T(8,128)(2,1)S(1)}, u32[]{:S(2)}, u32[]{:S(2)}) collective-permute-start(bf16[2,144,128]{2,1,0:T(8,128)(2,1)S(1)} %get-tuple-element.61), channel_id=1, source_target_pairs={{0,6},{2,0},{4,2},{6,4},{1,7},{3,1},{5,3},{7,5},{8,14},{10,8},{12,... | collective-permute-start | bytes 221192 | tf_op jit(solution)/shard_map/ppermute | solution.py:483
  196.2 5.8 %collective-permute-start.9 = (bf16[144,128]{1,0:T(8,128)(2,1)S(1)}, bf16[144,128]{1,0:T(8,128)(2,1)S(1)}, u32[]{:S(2)}, u32[]{:S(2)}) collective-permute-start(bf16[144,128]{1,0:T(8,128)(2,1)S(1)} %dynamic-slice_bitcast_fusion.3), channel_id=1, source_target_pairs={{0,1},{1,0},{2,3},{3,2},{4,5},{5,4},{6,7},{7,6},{8,9},{9,8},{10,11... | collective-permute-start | bytes 110600 | tf_op jit(solution)/shard_map/ppermute | solution.py:483

commit v4 on v3

--- a/solution.py
+++ b/solution.py
@@ -1,3 +1,4 @@
+import functools
 import math
 
 import jax
@@ -448,54 +449,47 @@
     )
 
 
-def add_kernel(left_ref, right_ref, sum_ref):
-    sum_ref[...] = (left_ref[...].astype(F32) + right_ref[...].astype(F32)).astype(BF16)
-
-
-def paired(keep, send):
+def pair_fold_kernel(peers, keep_ref, got_ref, sum_ref, row_ref):
+    tiles, rows, columns = keep_ref.shape
+    across = columns // 128
+    each = rows // peers
+    for tile in range(tiles):
+        total = keep_ref[tile].astype(F32) + got_ref[tile].astype(F32)
+        base = tile * across * rows
+        for c in range(across):
+            at = base + c * rows
+            row_ref[at : at + rows] = total[:, c * 128 : (c + 1) * 128]
+        for peer in range(peers):
+            for r in range(0, each, 2):
+                start = base + peer * each + r
+                pair = [row_ref[pl.ds(start + k, across, stride=rows)] for k in range(2)]
+                at = r * across
+                sum_ref[tile * peers + peer, at : at + 2 * across] = jnp.concatenate(
+                    pair, axis=0
+                ).astype(BF16)
+
+
+def paired(keep, send, peers):
     got = lax.ppermute(send, "core", [(0, 1), (1, 0)])
-    block = pl.BlockSpec((1,) + keep.shape[1:], lambda i: (i, 0, 0))
-    return pl.pallas_call(
-        add_kernel,
-        grid=(keep.shape[0],),
+    tiles, rows, columns = keep.shape
+    at_once = tiles // 4
+    height = rows // peers * columns // 128
+    block = pl.BlockSpec((at_once, rows, columns), lambda i: (i, 0, 0))
+    return pl.pallas_call(
+        functools.partial(pair_fold_kernel, peers),
+        grid=(4,),
         in_specs=[block, block],
-        out_specs=block,
-        out_shape=jax.ShapeDtypeStruct(keep.shape, BF16),
+        out_specs=pl.BlockSpec((at_once * peers, height, 128), lambda i: (i, 0, 0)),
+        out_shape=jax.ShapeDtypeStruct((tiles * peers, height, 128), BF16),
+        scratch_shapes=[pltpu.VMEM((at_once * columns // 128 * rows, 128), F32)],
+        compiler_params=pltpu.CompilerParams(vmem_limit_bytes=16 << 20),
         cost_estimate=pl.CostEstimate(flops=1, bytes_accessed=1, transcendentals=0),
-        name="pair_sum",
+        name="pair_fold",
     )(keep, got)
 
 
-def folded(array, *lead):
-    return array.reshape(lead + (-1, 128))
-
-
-def ring_sum(chunks, axis):
-    size = lax.axis_size(axis)
-    me = lax.axis_index(axis).astype(jnp.uint32)
-
-    def chunk(by):
-        at = lax.bitwise_and(me + jnp.uint32(by), jnp.uint32(size - 1))
-        return lax.dynamic_index_in_dim(chunks, at, 0, keepdims=False)
-
-    total = chunk(0).astype(F32)
-    for by in range(1, size):
-        moved = lax.ppermute(chunk(by), axis, [(i, (i + by) % size) for i in range(size)])
-        total = total + moved.astype(F32)
-    return total
-
-
-def summed_by_frame(part):
-    z, xhi = lax.axis_size("z"), lax.axis_size("xhi")
-    after_z = ring_sum(folded(part, z, xhi), "z").astype(BF16)
-    return ring_sum(after_z, "xhi")
-
-
-def summed_at_once(mine):
-    rest = ("xlo", "y", "z", "xhi")
-    count = lax.axis_size(rest)
-    arrived = lax.all_to_all(folded(mine, count), rest, 0, 0, tiled=False)
-    return jnp.sum(arrived.astype(F32), axis=0)
+def spread_out(mine):
+    return lax.all_to_all(mine, ("xlo", "y", "z", "xhi"), 0, 0, tiled=False)
 
 
 def shifted(shard, by):
@@ -510,8 +504,9 @@
     return lax.dynamic_slice_in_dim(weight, at, per_device, axis=0).astype(F32)
 
 
-def finished(total, qkv, gain, tokens):
+def finished(arrived, qkv, gain, tokens):
     features, wide = qkv.shape
+    total = jnp.sum(arrived.astype(F32), axis=0)
     summed = total.reshape(-1, wide + features) * (1.0 / math.sqrt(tokens))
     d_qkv = summed[:, :wide]
     d_gain = jnp.sum(own_rows(qkv) * d_qkv, axis=1) / own_rows(gain)
@@ -541,10 +536,10 @@
     both_rows, left_t, right_t = temporal(exchanged(mid), cot_rows, gain_t, qkv_time, out_time)
     both = exchanged(both_rows)
     keep_t, send_t = term_time(core, left_t, right_t, tiles)
-    mine_t = paired(keep_t, send_t)
+    mine_t = paired(keep_t, send_t, peers)
     dproj = back_projection(both, out_space, frames)
     dproj, mine_t = lax.optimization_barrier((dproj, mine_t))
-    arrived_t = lax.all_to_all(mine_t, ("xlo", "y"), 0, 0, tiled=False)
+    arrived_t = spread_out(mine_t)
     dq, dkv, own, for_west, for_east = spatial_backward(dproj, qkv_space, q_s, kv_s, p_s, lat)
     from_east = shifted(for_west, -1)
     from_west = shifted(for_east, 1)
@@ -552,16 +547,13 @@
     send_s, arrived_t, from_east, from_west = lax.optimization_barrier(
         (send_s, arrived_t, from_east, from_west)
     )
-    mine_s = paired(keep_s, send_s)
-    summed_space = summed_at_once(mine_s)
-    part_t = jnp.sum(arrived_t.astype(F32), axis=0).astype(BF16)
-    summed_time = summed_by_frame(part_t)
+    arrived_s = spread_out(paired(keep_s, send_s, peers))
     layer_out = both[:, frames:].transpose(1, 0, 2, 3, 4).reshape(tokens.shape)
     grad_tokens = final_norm(tokens, gain_s, both, own, from_east, from_west)
     return (
         (layer_out, grad_tokens)
-        + finished(summed_space, qkv_space, gain_space, total)
-        + finished(summed_time, qkv_time, gain_time, total)
+        + finished(arrived_s, qkv_space, gain_space, total)
+        + finished(arrived_t, qkv_time, gain_time, total)
     )
 
 

time: 209 us -> 195 us (0.933)
  local copies, waits for them, and re-layouts: 17.9 us -> 10.4 us
  Pallas kernels: 82.5 us -> 77.7 us
  waiting for transfers between devices: 41.5 us -> 46.2 us
  starting transfers between devices: 56.7 us -> 53.3 us
  other arithmetic: 8.63 us -> 5.29 us
    all_to_all x2, waiting for transfers between devices: 0.01 us -> 25.8 us  [spread_out(): return lax.all_to_all(mine, ('xlo', 'y', 'z', 'xhi'), 0, 0, tiled=False)]
    ppermute x4 -> x0, waiting for transfers between devices: 21.9 us -> none  [ring_sum(): lax.ppermute(chunk(by), axis, [(i, (i + by) % size) for i in range(size)])]
    ppermute x4 -> x0, starting transfers between devices: 7.21 us -> none  [ring_sum(): lax.ppermute(chunk(by), axis, [(i, (i + by) % size) for i in range(size)])]
    reshape x2 -> x0, local copies, waits for them, and re-layouts: 6.73 us -> none  [folded(): return array.reshape(lead + (-1, 128))]
    all_to_all x2, starting transfers between devices: 18.2 us -> 23.6 us  [spread_out(): return lax.all_to_all(mine, ('xlo', 'y', 'z', 'xhi'), 0, 0, tiled=False)]
    pallas_call x2, Pallas kernels: 12.8 us -> 8.07 us  [paired(): pl.pallas_call(functools.partial(pair_fold_kernel, peers), grid=(4,), in_...]
  transfers between devices with their start and end apart: 15 -> 11, of which waited for: 7 -> 5; matrix products, arithmetic and copies ran while one was open for 6% -> 3% of each run, Pallas kernels for 26% -> 28%
where the time goes in v4:
time: 195 us; the launch traced here: 194 us
  Pallas kernels  77.7 us (40%)
  starting transfers between devices  53.3 us (27%)
  waiting for transfers between devices  46.2 us (24%)
  local copies, waits for them, and re-layouts  10.4 us (5%)
  other arithmetic  5.29 us (3%)
    all_to_all x2, waiting for transfers between devices, spread_out(): return lax.all_to_all(mine, ('xlo', 'y', 'z', 'xhi'), 0, 0, tiled=False)  25.8 us
    all_to_all x2, starting transfers between devices, spread_out(): return lax.all_to_all(mine, ('xlo', 'y', 'z', 'xhi'), 0, 0, tiled=False)  23.6 us
    pallas_call x1, Pallas kernels, spatial_backward(): pl.pallas_call(spatial_backward_kernel, grid=(frames,), in_specs=[per_ste...  18.6 us
    all_to_all x3, starting transfers between devices, exchanged(): return lax.all_to_all(chunks, FRAME, 0, 0, tiled=False)  17.7 us
    pallas_call x2, Pallas kernels, split_call(): pl.pallas_call(kernel, grid_spec=pltpu.PrefetchScalarGridSpec(num_scalar_...  15.6 us
    pallas_call x1, Pallas kernels, temporal(): pl.pallas_call(temporal_kernel, out_shape=[jax.ShapeDtypeStruct((peers, 2...  14.8 us
    pallas_call x1, Pallas kernels, spatial_forward(): pl.pallas_call(spatial_forward_kernel, grid=(frames,), in_specs=[per_step...  14.3 us
    all_to_all x3, waiting for transfers between devices, exchanged(): return lax.all_to_all(chunks, FRAME, 0, 0, tiled=False)  11.7 us
  transfers between devices with their start and end apart: 11, of which 5 were waited for; matrix products, arithmetic and copies ran while one was open for 3% of the time, Pallas kernels for 28%

profile of v4, /device:TPU:1, one launch (start us, length us, event | category | flops | bytes accessed | tf_op | source)
XLA Modules:
  0.0 193.7 jit_solution(3629137764537415549)
XLA Ops:
  0.6 2.8 %collective-permute-start = (bf16[2,24,8,768]{3,2,1,0:T(8,128)(2,1)}, bf16[2,24,8,768]{3,2,1,0:T(8,128)(2,1)S(1)}, u32[]{:S(2)}, u32[]{:S(2)}) collective-permute-start(bf16[2,24,8,768]{3,2,1,0:T(8,128)(2,1)} %tokens_ref.1), channel_id=1, source_target_pairs={{0,8},{8,16},{16,24},{24,32},{32,40},{40,48},{48,56},{56,64},{64,7... | collective-permute-start | bytes 1769480 | tf_op jit(solution)/shard_map/ppermute | solution.py:497
  3.4 1.9 copy.19
  5.3 7.5 %all-to-all-start.1 = ((bf16[8,2,3,8,768]{4,3,2,1,0:T(8,128)(2,1)}), bf16[8,2,3,8,768]{4,3,2,1,0:T(8,128)(2,1)S(1)}, u32[]{:S(2)}, u32[]{:S(2)}) async-start(bf16[8,2,3,8,768]{4,3,2,1,0:T(8,128)(2,1)} %bitcast.7), calls=%async_computation.1 | async-start | bytes 1179648 | tf_op jit(solution)/shard_map/all_to_all | solution.py:527
  14.2 0.8 copy-done.11
  15.0 14.3 %spatial_forward.1 = (bf16[2,576,768]{2,1,0:T(8,128)(2,1)}, bf16[2,192,768]{2,1,0:T(8,128)(2,1)}, bf16[2,576,1536]{2,1,0:T(8,128)(2,1)}, bf16[2,3,1344,256]{3,2,...) custom-call(bf16[2,24,8,768]{3,2,1,0:T(8,128)(2,1)} %tokens_ref.1, ...), custom_call_target="tpu_custom_call" | custom-call | flops 14000000000 | bytes 4194304 | tf_op jit(solution)/shard_map/spatial_forward/pallas_call | solution.py:143
  29.4 6.7 %all-to-all-start = ((bf16[8,2,3,8,768]{4,3,2,1,0:T(8,128)(2,1)}), bf16[8,2,3,8,768]{4,3,2,1,0:T(8,128)(2,1)S(1)}, u32[]{:S(2)}, u32[]{:S(2)}) async-start(bf16[8,2,3,8,768]{4,3,2,1,0:T(8,128)(2,1)} %get-tuple-element.32), calls=%async_computation | async-start | bytes 1179648 | tf_op jit(solution)/shard_map/all_to_all | solution.py:527
  36.6 8.9 %all-to-all-done.mid_ref = bf16[8,2,3,8,768]{4,3,2,1,0:T(8,128)(2,1)S(1)} async-done(((bf16[8,2,3,8,768]{4,3,2,1,0:T(8,128)(2,1)}), bf16[8,2,3,8,768]{4,3,2,1,0:T(8,128)(2,1)S(1)}, u32[]{:S(2)}, u32[]{:S(2)}) %all-to-all-start) | async-done | bytes 589856 | tf_op jit(solution)/shard_map/all_to_all | solution.py:527
  45.5 0.8 copy-done.5
  46.3 14.8 %temporal.1 = (bf16[8,4,3,8,768]{4,3,2,1,0:T(8,128)(2,1)}, bf16[384,1536]{1,0:T(8,128)(2,1)}, bf16[384,3072]{1,0:T(8,128)(2,1)}) custom-call(bf16[8,2,3,8,768]{4,3,2,1,0:T(8,128)(2,1)} %copy-done.5, bf16[8,2,3,8,768]{4,3,2,1,0:T(8,128)(2,1)} %copy-done.4, f32[1,768]{1,0:T(1,128)} %reshape.39.gain_ref, bf16[768,2304]{1,0:T(8,128)(2,1)} %qkv_ref.4, ...), custom_call_target="tpu_custom_call" | custom-call | flops 17999998976 | bytes 4194304 | tf_op jit(solution)/shard_map/temporal/pallas_call | solution.py:218
  61.1 3.6 %all-to-all-start.2 = ((bf16[8,4,3,8,768]{4,3,2,1,0:T(8,128)(2,1)}), bf16[8,4,3,8,768]{4,3,2,1,0:T(8,128)(2,1)S(1)}, u32[]{:S(2)}, u32[]{:S(2)}) async-start(bf16[8,4,3,8,768]{4,3,2,1,0:T(8,128)(2,1)} %get-tuple-element.33), calls=%async_computation.2 | async-start | bytes 2359296 | tf_op jit(solution)/shard_map/all_to_all | solution.py:527
  64.7 6.5 %term_time.1 = (bf16[8,48,3072]{2,1,0:T(8,128)(2,1)}, bf16[8,48,3072]{2,1,0:T(8,128)(2,1)}) custom-call(s32[1]{0:T(128)} %bitcast.4.core_ref, bf16[384,1536]{1,0:T(8,128)(2,1)} %get-tuple-element.34.left_ref, bf16[384,3072]{1,0:T(8,128)(2,1)} %get-tuple-element.35.right_ref), custom_call_target="tpu_custom_call" | custom-call | flops 1 | bytes 1 | tf_op jit(solution)/shard_map/term_time/pallas_call | solution.py:375
  71.3 4.5 %collective-permute-start.2 = (bf16[8,48,3072]{2,1,0:T(8,128)(2,1)}, bf16[8,48,3072]{2,1,0:T(8,128)(2,1)}, u32[]{:S(2)}, u32[]{:S(2)}) collective-permute-start(bf16[8,48,3072]{2,1,0:T(8,128)(2,1)} %get-tuple-element.37), channel_id=1, source_target_pairs={{0,8},{8,0},{1,9},{9,1},{2,10},{10,2},{3,11},{11,3},{4,12},{12,4},... | collective-permute-start | bytes 7077896 | tf_op jit(solution)/shard_map/ppermute | solution.py:473
  75.8 2.8 %all-to-all-done.2.dmid_ref = bf16[8,4,3,8,768]{4,3,2,1,0:T(8,128)(2,1)S(1)} async-done(((bf16[8,4,3,8,768]{4,3,2,1,0:T(8,128)(2,1)}), bf16[8,4,3,8,768]{4,3,2,1,0:T(8,128)(2,1)S(1)}, u32[]{:S(2)}, u32[]{:S(2)}) %all-to-all-start.2) | async-done | bytes 1179680 | tf_op jit(solution)/shard_map/all_to_all | solution.py:527
  78.5 1.0 copy-done.2
  79.6 3.2 %back_projection.1.dproj_ref = bf16[2,192,768]{2,1,0:T(8,128)(2,1)} custom-call(bf16[8,4,3,8,768]{4,3,2,1,0:T(8,128)(2,1)} %copy-done.2, bf16[768,768]{1,0:T(8,128)(2,1)} %out_ref.5), custom_call_target="tpu_custom_call" | custom-call | flops 30000001024 | bytes 4194304 | tf_op jit(solution)/shard_map/back_projection/pallas_call | solution.py:244
  82.8 4.9 %pair_fold.2 = bf16[64,144,128]{2,1,0:T(8,128)(2,1)} custom-call(bf16[8,48,3072]{2,1,0:T(8,128)(2,1)S(1)} %copy-done.1, bf16[8,48,3072]{2,1,0:T(8,128)(2,1)} %collective-permute-done.2.got_ref), custom_call_target="tpu_custom_call" | custom-call | flops 1 | bytes 1 | tf_op jit(solution)/shard_map/pair_fold/pallas_call | solution.py:478
  87.6 16.1 %all-to-all-start.3 = ((bf16[64,144,128]{2,1,0:T(8,128)(2,1)}), bf16[64,144,128]{2,1,0:T(8,128)(2,1)S(1)}, u32[]{:S(2)}, u32[]{:S(2)}) async-start(bf16[64,144,128]{2,1,0:T(8,128)(2,1)} %pair_fold.2), calls=%async_computation.3 | async-start | bytes 4718592 | tf_op jit(solution)/shard_map/all_to_all | solution.py:492
  103.7 18.6 %spatial_backward.1 = (bf16[2,192,768]{2,1,0:T(8,128)(2,1)}, bf16[2,576,1536]{2,1,0:T(8,128)(2,1)}, bf16[2,24,8,768]{3,2,1,0:T(8,128)(2,1)}, bf16[2,24,8,768]{3,2,1,0:T(8,128)(2,1)}, bf16[2,24,8,768]{3,2,1,0:T(8,128)(2,1)}) custom-call(bf16[2,192,768]{2,1,0:T(8,128)(2,1)} %back_projection.1.dproj_ref, bf16[768,2304]{1,0:T(8,128)(2,1)} %qkv_ref.5, ...), custom_call_target="tpu_custom_call" | custom-call | flops 20000000000 | bytes 4194304 | tf_op jit(solution)/shard_map/spatial_backward/pallas_call | solution.py:308
  122.3 0.8 collective-permute-start.3
  123.2 1.3 collective-permute-start.4
  124.4 9.1 %term_space.1 = (bf16[8,48,3072]{2,1,0:T(8,128)(2,1)}, bf16[8,48,3072]{2,1,0:T(8,128)(2,1)}) custom-call(s32[1]{0:T(128)} %bitcast.4.core_ref, bf16[2,576,768]{2,1,0:T(8,128)(2,1)} %get-tuple-element.43.y_ref, bf16[2,192,768]{2,1,0:T(8,128)(2,1)} %get-tuple-element.44.dq_ref, bf16[2,576,1536]{2,1,0:T(8,128)(2,1)} %get-tuple-element.45.dkv_ref, ...), custom_call_target="tpu_custom_call" | custom-call | flops 1 | bytes 1 | tf_op jit(solution)/shard_map/term_space/pallas_call | solution.py:375
  133.5 4.3 %collective-permute-done.3.first_ref = bf16[2,24,8,768]{3,2,1,0:T(8,128)(2,1)S(1)} collective-permute-done((bf16[2,24,8,768]{3,2,1,0:T(8,128)(2,1)}, bf16[2,24,8,768]{3,2,1,0:T(8,128)(2,1)S(1)}, u32[]{:S(2)}, u32[]{:S(2)}) %collective-permute-start.3) | collective-permute-done | bytes 589856 | tf_op jit(solution)/shard_map/ppermute | solution.py:497
  137.8 2.6 %collective-permute-start.5 = (bf16[8,48,3072]{2,1,0:T(8,128)(2,1)}, bf16[8,48,3072]{2,1,0:T(8,128)(2,1)S(1)}, u32[]{:S(2)}, u32[]{:S(2)}) collective-permute-start(bf16[8,48,3072]{2,1,0:T(8,128)(2,1)} %get-tuple-element.54), channel_id=1, source_target_pairs={{0,8},{8,0},{1,9},{9,1},{2,10},{10,2},{3,11},{11,3},{4,12},{12,4},... | collective-permute-start | bytes 7077896 | tf_op jit(solution)/shard_map/ppermute | solution.py:473
  140.4 4.4 %collective-permute-done.5.got_ref = bf16[8,48,3072]{2,1,0:T(8,128)(2,1)S(1)} collective-permute-done((bf16[8,48,3072]{2,1,0:T(8,128)(2,1)}, bf16[8,48,3072]{2,1,0:T(8,128)(2,1)S(1)}, u32[]{:S(2)}, u32[]{:S(2)}) %collective-permute-start.5) | collective-permute-done | bytes 2359328 | tf_op jit(solution)/shard_map/ppermute | solution.py:473
  144.8 1.7 copy-done
  146.4 3.2 %pair_fold.3 = bf16[64,144,128]{2,1,0:T(8,128)(2,1)} custom-call(bf16[8,48,3072]{2,1,0:T(8,128)(2,1)S(1)} %copy-done, bf16[8,48,3072]{2,1,0:T(8,128)(2,1)S(1)} %collective-permute-done.5.got_ref), custom_call_target="tpu_custom_call" | custom-call | flops 1 | bytes 1 | tf_op jit(solution)/shard_map/pair_fold/pallas_call | solution.py:478
  149.7 7.5 %all-to-all-start.4 = ((bf16[64,144,128]{2,1,0:T(8,128)(2,1)}), bf16[64,144,128]{2,1,0:T(8,128)(2,1)}, u32[]{:S(2)}, u32[]{:S(2)}) async-start(bf16[64,144,128]{2,1,0:T(8,128)(2,1)} %pair_fold.3), calls=%async_computation.4 | async-start | bytes 4718592 | tf_op jit(solution)/shard_map/all_to_all | solution.py:492
  157.2 0.9 copy.17
  159.1 3.2 %final_norm.1 = f32[2,24,8,768]{3,2,1,0:T(8,128)} custom-call(bf16[2,24,8,768]{3,2,1,0:T(8,128)(2,1)} %tokens_ref.1, f32[1,768]{1,0:T(1,128)} %reshape.37.gain_ref, bf16[8,4,3,8,768]{4,3,2,1,0:T(8,128)(2,1)} %copy-done.2, bf16[2,24,8,768]{3,2,1,0:T(8,128)(2,1)} %get-tuple-element.42.own_ref, bf16[2,24,8,768]{3,2,1,0:T(8,128)(2,1)} %copy-done.8, ...), custom_call_target="tpu_custom_call" | custom-call | flops 3000000000 | bytes 4194304 | tf_op jit(solution)/shard_map/final_norm/pallas_call | solution.py:345
  162.2 25.8 %all-to-all-done.4 = bf16[64,144,128]{2,1,0:T(8,128)(2,1)} async-done(((bf16[64,144,128]{2,1,0:T(8,128)(2,1)}), bf16[64,144,128]{2,1,0:T(8,128)(2,1)}, u32[]{:S(2)}, u32[]{:S(2)}) %all-to-all-start.4) | async-done | bytes 2359328 | tf_op jit(solution)/shard_map/all_to_all | solution.py:492
  188.1 2.0 %convert_reduce_fusion.1 = f32[144,128]{1,0:T(8,128)S(1)} fusion(bf16[64,144,128]{2,1,0:T(8,128)(2,1)} %all-to-all-done.4), kind=kLoop, calls=%fused_computation.1 | loop fusion | flops 2340864 | bytes 2433024 | tf_op jit(solution)/shard_map/reduce_sum | solution.py:509
  190.7 1.7 multiply_reduce_fusion
  (39 shorter events, 4.9 us)
Async XLA Ops:
  0.6 12.2 %copy-start.7 = (f32[768]{0:T(1024)S(1)}, f32[768]{0:T(1024)}, u32[]{:S(2)}) copy-start(f32[768]{0:T(1024)} %param.9) | copy-start | bytes 9220
  0.6 12.8 %collective-permute-start = (bf16[2,24,8,768]{3,2,1,0:T(8,128)(2,1)}, bf16[2,24,8,768]{3,2,1,0:T(8,128)(2,1)S(1)}, u32[]{:S(2)}, u32[]{:S(2)}) collective-permute-start(bf16[2,24,8,768]{3,2,1,0:T(8,128)(2,1)} %tokens_ref.1), channel_id=1, source_target_pairs={{0,8},{8,16},{16,24},{24,32},{32,40},{40,48},{48,56},{56,64},{64,7... | collective-permute-start | bytes 1769480 | tf_op jit(solution)/shard_map/ppermute | solution.py:497
  3.4 10.0 %collective-permute-start.1 = (bf16[2,24,8,768]{3,2,1,0:T(8,128)(2,1)}, bf16[2,24,8,768]{3,2,1,0:T(8,128)(2,1)S(1)}, u32[]{:S(2)}, u32[]{:S(2)}) collective-permute-start(bf16[2,24,8,768]{3,2,1,0:T(8,128)(2,1)} %tokens_ref.1), channel_id=1, source_target_pairs={{0,120},{8,0},{16,8},{24,16},{32,24},{40,32},{48,40},{56,48},{64,5... | collective-permute-start | bytes 1769480 | tf_op jit(solution)/shard_map/ppermute | solution.py:497
  5.3 24.0 %all-to-all-start.1 = ((bf16[8,2,3,8,768]{4,3,2,1,0:T(8,128)(2,1)}), bf16[8,2,3,8,768]{4,3,2,1,0:T(8,128)(2,1)S(1)}, u32[]{:S(2)}, u32[]{:S(2)}) async-start(bf16[8,2,3,8,768]{4,3,2,1,0:T(8,128)(2,1)} %bitcast.7), calls=%async_computation.1 | async-start | bytes 1179648 | tf_op jit(solution)/shard_map/all_to_all | solution.py:527
  13.4 22.6 %copy-start.6 = (f32[768]{0:T(1024)S(1)}, f32[768]{0:T(1024)}, u32[]{:S(2)}) copy-start(f32[768]{0:T(1024)} %param.12) | copy-start | bytes 9220
  13.4 0.8 copy-start.10
  14.2 0.8 copy-start.11
  29.3 16.2 %copy-start.4 = (bf16[8,2,3,8,768]{4,3,2,1,0:T(8,128)(2,1)}, bf16[8,2,3,8,768]{4,3,2,1,0:T(8,128)(2,1)S(1)}, u32[]{:S(2)}) copy-start(bf16[8,2,3,8,768]{4,3,2,1,0:T(8,128)(2,1)S(1)} %all-to-all-done.1.cot_ref) | copy-start | bytes 1769476
  29.4 16.2 %all-to-all-start = ((bf16[8,2,3,8,768]{4,3,2,1,0:T(8,128)(2,1)}), bf16[8,2,3,8,768]{4,3,2,1,0:T(8,128)(2,1)S(1)}, u32[]{:S(2)}, u32[]{:S(2)}) async-start(bf16[8,2,3,8,768]{4,3,2,1,0:T(8,128)(2,1)} %get-tuple-element.32), calls=%async_computation | async-start | bytes 1179648 | tf_op jit(solution)/shard_map/all_to_all | solution.py:527
  45.5 0.8 copy-start.5
  61.1 17.4 %all-to-all-start.2 = ((bf16[8,4,3,8,768]{4,3,2,1,0:T(8,128)(2,1)}), bf16[8,4,3,8,768]{4,3,2,1,0:T(8,128)(2,1)S(1)}, u32[]{:S(2)}, u32[]{:S(2)}) async-start(bf16[8,4,3,8,768]{4,3,2,1,0:T(8,128)(2,1)} %get-tuple-element.33), calls=%async_computation.2 | async-start | bytes 2359296 | tf_op jit(solution)/shard_map/all_to_all | solution.py:527
  71.3 11.5 %copy-start.1 = (bf16[8,48,3072]{2,1,0:T(8,128)(2,1)S(1)}, bf16[8,48,3072]{2,1,0:T(8,128)(2,1)}, u32[]{:S(2)}) copy-start(bf16[8,48,3072]{2,1,0:T(8,128)(2,1)} %get-tuple-element.36.keep_ref) | copy-start | bytes 7077892
  71.3 11.5 %collective-permute-start.2 = (bf16[8,48,3072]{2,1,0:T(8,128)(2,1)}, bf16[8,48,3072]{2,1,0:T(8,128)(2,1)}, u32[]{:S(2)}, u32[]{:S(2)}) collective-permute-start(bf16[8,48,3072]{2,1,0:T(8,128)(2,1)} %get-tuple-element.37), channel_id=1, source_target_pairs={{0,8},{8,0},{1,9},{9,1},{2,10},{10,2},{3,11},{11,3},{4,12},{12,4},... | collective-permute-start | bytes 7077896 | tf_op jit(solution)/shard_map/ppermute | solution.py:473
  78.5 1.0 copy-start.2
  87.6 50.2 %all-to-all-start.3 = ((bf16[64,144,128]{2,1,0:T(8,128)(2,1)}), bf16[64,144,128]{2,1,0:T(8,128)(2,1)S(1)}, u32[]{:S(2)}, u32[]{:S(2)}) async-start(bf16[64,144,128]{2,1,0:T(8,128)(2,1)} %pair_fold.2), calls=%async_computation.3 | async-start | bytes 4718592 | tf_op jit(solution)/shard_map/all_to_all | solution.py:492
  122.3 15.4 %collective-permute-start.3 = (bf16[2,24,8,768]{3,2,1,0:T(8,128)(2,1)}, bf16[2,24,8,768]{3,2,1,0:T(8,128)(2,1)S(1)}, u32[]{:S(2)}, u32[]{:S(2)}) collective-permute-start(bf16[2,24,8,768]{3,2,1,0:T(8,128)(2,1)} %get-tuple-element.49), channel_id=1, source_target_pairs={{0,120},{8,0},{16,8},{24,16},{32,24},{40,32},{48,40},{56,48},{64,5... | collective-permute-start | bytes 1769480 | tf_op jit(solution)/shard_map/ppermute | solution.py:497
  123.2 14.6 %collective-permute-start.4 = (bf16[2,24,8,768]{3,2,1,0:T(8,128)(2,1)}, bf16[2,24,8,768]{3,2,1,0:T(8,128)(2,1)S(1)}, u32[]{:S(2)}, u32[]{:S(2)}) collective-permute-start(bf16[2,24,8,768]{3,2,1,0:T(8,128)(2,1)} %get-tuple-element.50), channel_id=1, source_target_pairs={{0,8},{8,16},{16,24},{24,32},{32,40},{40,48},{48,56},{56,64},{64,7... | collective-permute-start | bytes 1769480 | tf_op jit(solution)/shard_map/ppermute | solution.py:497
  137.8 7.0 %copy-start.8 = (bf16[2,24,8,768]{3,2,1,0:T(8,128)(2,1)}, bf16[2,24,8,768]{3,2,1,0:T(8,128)(2,1)S(1)}, u32[]{:S(2)}) copy-start(bf16[2,24,8,768]{3,2,1,0:T(8,128)(2,1)S(1)} %collective-permute-done.3.first_ref) | copy-start | bytes 1769476
  137.8 7.0 %copy-start.9 = (bf16[2,24,8,768]{3,2,1,0:T(8,128)(2,1)}, bf16[2,24,8,768]{3,2,1,0:T(8,128)(2,1)S(1)}, u32[]{:S(2)}) copy-start(bf16[2,24,8,768]{3,2,1,0:T(8,128)(2,1)S(1)} %collective-permute-done.4.second_ref) | copy-start | bytes 1769476
  137.8 7.0 %collective-permute-start.5 = (bf16[8,48,3072]{2,1,0:T(8,128)(2,1)}, bf16[8,48,3072]{2,1,0:T(8,128)(2,1)S(1)}, u32[]{:S(2)}, u32[]{:S(2)}) collective-permute-start(bf16[8,48,3072]{2,1,0:T(8,128)(2,1)} %get-tuple-element.54), channel_id=1, source_target_pairs={{0,8},{8,0},{1,9},{9,1},{2,10},{10,2},{3,11},{11,3},{4,12},{12,4},... | collective-permute-start | bytes 7077896 | tf_op jit(solution)/shard_map/ppermute | solution.py:473
  144.8 1.7 copy-start
  149.7 7.5 %copy-start.3 = (bf16[8,4,3,8,768]{4,3,2,1,0:T(8,128)(2,1)S(1)}, bf16[8,4,3,8,768]{4,3,2,1,0:T(8,128)(2,1)}, u32[]{:S(2)}) copy-start(bf16[8,4,3,8,768]{4,3,2,1,0:T(8,128)(2,1)} %copy-done.2) | copy-start | bytes 3538948
  149.7 38.4 %all-to-all-start.4 = ((bf16[64,144,128]{2,1,0:T(8,128)(2,1)}), bf16[64,144,128]{2,1,0:T(8,128)(2,1)}, u32[]{:S(2)}, u32[]{:S(2)}) async-start(bf16[64,144,128]{2,1,0:T(8,128)(2,1)} %pair_fold.3), calls=%async_computation.4 | async-start | bytes 4718592 | tf_op jit(solution)/shard_map/all_to_all | solution.py:492

commit v5 on v4

--- a/solution.py
+++ b/solution.py
@@ -17,7 +17,6 @@
 BF16 = jnp.bfloat16
 TILE = ("xlo", "y", "core")
 FRAME = ("z", "xhi")
-VMEM_LIMIT = 56 * 1024 * 1024
 
 
 def dot(left, right, left_dim=1, right_dim=0):
@@ -109,7 +108,7 @@
 
 
 def full(shape):
-    return pl.BlockSpec(shape, lambda *_: (0,) * len(shape))
+    return pl.BlockSpec(shape, lambda *_: (0,) * len(shape), pipeline_mode=pl.Buffered(1))
 
 
 def per_step(shape):
@@ -146,12 +145,12 @@
         in_specs=[per_step((lat, width, features))] * 3
         + [full((1, features)), full(qkv.shape), full(out.shape)],
         out_specs=[per_step(shape) for shape, _ in outs] + [grouped(peers, lat, width, features)],
-        out_shape=[jax.ShapeDtypeStruct((frames,) + shape, kind) for shape, kind in outs]
-        + [jax.ShapeDtypeStruct(mid_shape, BF16)],
-        compiler_params=pltpu.CompilerParams(vmem_limit_bytes=VMEM_LIMIT),
+        out_shape=[pltpu.HBM((frames,) + shape, kind) for shape, kind in outs]
+        + [pltpu.HBM(mid_shape, BF16)],
+        compiler_params=pltpu.CompilerParams(vmem_limit_bytes=36 << 20),
         cost_estimate=cost(14),
         name="spatial_forward",
-    )(own, west, east, gain, qkv, out)
+    )(*[from_hbm(a) for a in (own, west, east)], gain, from_hbm(qkv), from_hbm(out))
 
 
 def temporal_kernel(
@@ -218,15 +217,15 @@
     return pl.pallas_call(
         temporal_kernel,
         out_shape=[
-            jax.ShapeDtypeStruct((peers, 2 * frames, lat, width, features), BF16),
-            jax.ShapeDtypeStruct((rows, 2 * features), BF16),
-            jax.ShapeDtypeStruct((rows, 4 * features), BF16),
+            pltpu.HBM((peers, 2 * frames, lat, width, features), BF16),
+            pltpu.HBM((rows, 2 * features), BF16),
+            pltpu.HBM((rows, 4 * features), BF16),
         ],
         scratch_shapes=[
             pltpu.VMEM((rows, 3 * features), BF16),
             pltpu.VMEM((rows, features), BF16),
         ],
-        compiler_params=pltpu.CompilerParams(vmem_limit_bytes=VMEM_LIMIT),
+        compiler_params=pltpu.CompilerParams(vmem_limit_bytes=56 << 20),
         cost_estimate=cost(18),
         name="temporal",
     )(mid, cot, gain, qkv, out)
@@ -246,8 +245,8 @@
         grid=(frames,),
         in_specs=[grouped(peers, peers * each, width, features), full(out.shape)],
         out_specs=per_step((rows, features)),
-        out_shape=jax.ShapeDtypeStruct((frames, rows, features), BF16),
-        compiler_params=pltpu.CompilerParams(vmem_limit_bytes=VMEM_LIMIT),
+        out_shape=pltpu.HBM((frames, rows, features), BF16),
+        compiler_params=pltpu.CompilerParams(vmem_limit_bytes=12 << 20),
         cost_estimate=cost(30),
         name="back_projection",
     )(dmid, out)
@@ -316,14 +315,17 @@
             per_step(p.shape[1:]),
         ],
         out_specs=[per_step(shape) for shape in outs],
-        out_shape=[jax.ShapeDtypeStruct((frames,) + shape, BF16) for shape in outs],
+        out_shape=[
+            (pltpu.HBM if at >= 2 else jax.ShapeDtypeStruct)((frames,) + shape, BF16)
+            for at, shape in enumerate(outs)
+        ],
         scratch_shapes=[
             pltpu.VMEM((3 * rows, 2 * features), F32),
         ],
-        compiler_params=pltpu.CompilerParams(vmem_limit_bytes=VMEM_LIMIT),
+        compiler_params=pltpu.CompilerParams(vmem_limit_bytes=36 << 20),
         cost_estimate=cost(20),
         name="spatial_backward",
-    )(dproj, qkv, q, kv, p)
+    )(*[from_hbm(a) for a in (dproj, qkv, q, kv, p)])
 
 
 def final_kernel(tokens_ref, gain_ref, dmid_ref, own_ref, first_ref, second_ref, grad_ref):
@@ -349,7 +351,7 @@
         + [block] * 3,
         out_specs=block,
         out_shape=jax.ShapeDtypeStruct(tokens.shape, F32),
-        compiler_params=pltpu.CompilerParams(vmem_limit_bytes=VMEM_LIMIT),
+        compiler_params=pltpu.CompilerParams(vmem_limit_bytes=16 << 20),
         cost_estimate=cost(3),
         name="final_norm",
     )(tokens, gain, dmid, own, first, second)
@@ -377,8 +379,8 @@
         grid_spec=pltpu.PrefetchScalarGridSpec(
             num_scalar_prefetch=1, grid=(4,), in_specs=specs, out_specs=[block, block]
         ),
-        out_shape=[jax.ShapeDtypeStruct(shape, BF16)] * 2,
-        compiler_params=pltpu.CompilerParams(vmem_limit_bytes=VMEM_LIMIT),
+        out_shape=[pltpu.HBM(shape, BF16)] * 2,
+        compiler_params=pltpu.CompilerParams(vmem_limit_bytes=24 << 20),
         cost_estimate=pl.CostEstimate(flops=flops, bytes_accessed=1, transcendentals=0),
         name=name,
     )(core, *operands)
@@ -392,7 +394,7 @@
         pl.BlockSpec((rows, features), lambda i, core: (0, i)),
     ]
     return split_call(
-        term_time_kernel, core, (left, right), specs, features, tiles,
+        term_time_kernel, core, (from_hbm(left), from_hbm(right)), specs, features, tiles,
         "term_time", 1,
     )
 
@@ -433,7 +435,9 @@
     features = y.shape[-1]
 
     def whole(array):
-        return pl.BlockSpec(array.shape, lambda i, core: (0,) * array.ndim)
+        return pl.BlockSpec(
+            array.shape, lambda i, core: (0,) * array.ndim, pipeline_mode=pl.Buffered(1)
+        )
 
     specs = [
         whole(y),
@@ -441,7 +445,9 @@
         pl.BlockSpec(dkv.shape[:2] + (features,), lambda i, core: (0, 0, jnp.clip(i - 1, 0, 1))),
         whole(o),
         pl.BlockSpec(
-            (dmid.shape[0], y.shape[0]) + dmid.shape[2:], lambda i, core: (0,) * dmid.ndim
+            (dmid.shape[0], y.shape[0]) + dmid.shape[2:],
+            lambda i, core: (0,) * dmid.ndim,
+            pipeline_mode=pl.Buffered(1),
         ),
     ]
     return split_call(
@@ -449,28 +455,37 @@
     )
 
 
+def fold(total, row_ref, base, peers, put):
+    rows, columns = total.shape
+    across = columns // 128
+    each = rows // peers
+    for c in range(across):
+        at = base + c * rows
+        row_ref[at : at + rows] = total[:, c * 128 : (c + 1) * 128]
+    for peer in range(peers):
+        for r in range(0, each, 2):
+            start = base + peer * each + r
+            pair = [row_ref[pl.ds(start + k, across, stride=rows)] for k in range(2)]
+            put(peer, slice(r * across, (r + 2) * across), jnp.concatenate(pair, axis=0).astype(BF16))
+
+
 def pair_fold_kernel(peers, keep_ref, got_ref, sum_ref, row_ref):
     tiles, rows, columns = keep_ref.shape
-    across = columns // 128
-    each = rows // peers
     for tile in range(tiles):
+
+        def put(peer, at, value):
+            sum_ref[tile * peers + peer, at] = value
+
         total = keep_ref[tile].astype(F32) + got_ref[tile].astype(F32)
-        base = tile * across * rows
-        for c in range(across):
-            at = base + c * rows
-            row_ref[at : at + rows] = total[:, c * 128 : (c + 1) * 128]
-        for peer in range(peers):
-            for r in range(0, each, 2):
-                start = base + peer * each + r
-                pair = [row_ref[pl.ds(start + k, across, stride=rows)] for k in range(2)]
-                at = r * across
-                sum_ref[tile * peers + peer, at : at + 2 * across] = jnp.concatenate(
-                    pair, axis=0
-                ).astype(BF16)
+        fold(total, row_ref, tile * rows * columns // 128, peers, put)
+
+
+def exchanged_pair(send):
+    return lax.ppermute(send, "core", [(0, 1), (1, 0)])
 
 
 def paired(keep, send, peers):
-    got = lax.ppermute(send, "core", [(0, 1), (1, 0)])
+    got = exchanged_pair(send)
     tiles, rows, columns = keep.shape
     at_once = tiles // 4
     height = rows // peers * columns // 128
@@ -485,7 +500,48 @@
         compiler_params=pltpu.CompilerParams(vmem_limit_bytes=16 << 20),
         cost_estimate=pl.CostEstimate(flops=1, bytes_accessed=1, transcendentals=0),
         name="pair_fold",
-    )(keep, got)
+    )(from_hbm(keep), got)
+
+
+def sum_fold_kernel(arrived_ref, sum_ref, row_ref):
+    def put(peer, at, value):
+        sum_ref[peer, at] = value
+
+    total = jnp.sum(arrived_ref[...].astype(F32), axis=0)
+    fold(total, row_ref, 0, sum_ref.shape[0], put)
+
+
+def sum_fold(arrived, peers):
+    _, rows, columns = arrived.shape
+    return pl.pallas_call(
+        sum_fold_kernel,
+        out_shape=jax.ShapeDtypeStruct((peers, rows // peers * columns // 128, 128), BF16),
+        scratch_shapes=[pltpu.VMEM((columns // 128 * rows, 128), F32)],
+        compiler_params=pltpu.CompilerParams(vmem_limit_bytes=16 << 20),
+        cost_estimate=cost(3),
+        name="sum_fold",
+    )(arrived)
+
+
+def ring_sum(chunks, axis):
+    size = lax.axis_size(axis)
+    me = lax.axis_index(axis).astype(jnp.uint32)
+
+    def chunk(by):
+        at = lax.bitwise_and(me + jnp.uint32(by), jnp.uint32(size - 1))
+        return lax.dynamic_index_in_dim(chunks, at, 0, keepdims=False)
+
+    total = chunk(0).astype(F32)
+    for by in range(1, size):
+        moved = lax.ppermute(chunk(by), axis, [(i, (i + by) % size) for i in range(size)])
+        total = total + moved.astype(F32)
+    return total
+
+
+def summed_by_frame(chunks):
+    z, xhi = lax.axis_size("z"), lax.axis_size("xhi")
+    after_z = ring_sum(chunks.reshape((z, xhi) + chunks.shape[1:]), "z").astype(BF16)
+    return ring_sum(after_z, "xhi")
 
 
 def spread_out(mine):
@@ -495,6 +551,10 @@
 def shifted(shard, by):
     size = lax.axis_size(TILE)
     return lax.ppermute(shard, TILE, [(i, (i + by) % size) for i in range(size)])
+
+
+def from_hbm(array):
+    return pltpu.with_memory_space_constraint(array, pltpu.HBM)
 
 
 def own_rows(weight):
@@ -504,13 +564,37 @@
     return lax.dynamic_slice_in_dim(weight, at, per_device, axis=0).astype(F32)
 
 
-def finished(arrived, qkv, gain, tokens):
-    features, wide = qkv.shape
-    total = jnp.sum(arrived.astype(F32), axis=0)
-    summed = total.reshape(-1, wide + features) * (1.0 / math.sqrt(tokens))
-    d_qkv = summed[:, :wide]
-    d_gain = jnp.sum(own_rows(qkv) * d_qkv, axis=1) / own_rows(gain)
-    return d_gain, d_qkv, summed[:, wide:]
+def finish_kernel(scale, arrived_ref, weight_ref, gain_ref, d_gain_ref, d_qkv_ref, d_out_ref):
+    rows, wide = d_qkv_ref.shape
+    total = jnp.sum(arrived_ref[...].astype(F32), axis=0) * scale
+    across = total.shape[0] // rows
+    own = wide // 128
+    for r in range(rows):
+        for c in range(across):
+            part = total[r * across + c : r * across + c + 1]
+            if c < own:
+                d_qkv_ref[r : r + 1, c * 128 : (c + 1) * 128] = part
+            else:
+                d_out_ref[r : r + 1, (c - own) * 128 : (c - own + 1) * 128] = part
+    along = jnp.sum(weight_ref[...] * d_qkv_ref[...], axis=1, keepdims=True)
+    d_gain_ref[...] = along / gain_ref[...]
+
+
+def finished(arrived, weight, gain, tokens):
+    rows, wide = weight.shape
+    features = arrived.shape[1] * 128 // rows - wide
+    d_gain, d_qkv, d_out = pl.pallas_call(
+        functools.partial(finish_kernel, 1.0 / math.sqrt(tokens)),
+        out_shape=[
+            jax.ShapeDtypeStruct((rows, 1), F32),
+            jax.ShapeDtypeStruct((rows, wide), F32),
+            jax.ShapeDtypeStruct((rows, features), F32),
+        ],
+        compiler_params=pltpu.CompilerParams(vmem_limit_bytes=12 << 20),
+        cost_estimate=cost(2),
+        name="finish",
+    )(arrived, weight, gain.reshape(rows, 1))
+    return d_gain.reshape(rows), d_qkv, d_out
 
 
 def shards(tokens, gain_space, qkv_space, out_space, gain_time, qkv_time, out_time, cotangent):
@@ -536,24 +620,23 @@
     both_rows, left_t, right_t = temporal(exchanged(mid), cot_rows, gain_t, qkv_time, out_time)
     both = exchanged(both_rows)
     keep_t, send_t = term_time(core, left_t, right_t, tiles)
-    mine_t = paired(keep_t, send_t, peers)
+    mine_t = (keep_t.astype(F32) + exchanged_pair(send_t).astype(F32)).astype(BF16)
     dproj = back_projection(both, out_space, frames)
     dproj, mine_t = lax.optimization_barrier((dproj, mine_t))
-    arrived_t = spread_out(mine_t)
+    arrived_t = lax.all_to_all(mine_t, ("xlo", "y"), 0, 0, tiled=False)
     dq, dkv, own, for_west, for_east = spatial_backward(dproj, qkv_space, q_s, kv_s, p_s, lat)
     from_east = shifted(for_west, -1)
     from_west = shifted(for_east, 1)
     keep_s, send_s = term_space(core, y_s, dq, dkv, o_s, both, tiles)
-    send_s, arrived_t, from_east, from_west = lax.optimization_barrier(
-        (send_s, arrived_t, from_east, from_west)
-    )
+    send_s, arrived_t = lax.optimization_barrier((send_s, arrived_t))
     arrived_s = spread_out(paired(keep_s, send_s, peers))
+    summed_t = summed_by_frame(sum_fold(arrived_t, peers))[None]
     layer_out = both[:, frames:].transpose(1, 0, 2, 3, 4).reshape(tokens.shape)
     grad_tokens = final_norm(tokens, gain_s, both, own, from_east, from_west)
     return (
         (layer_out, grad_tokens)
-        + finished(arrived_s, qkv_space, gain_space, total)
-        + finished(arrived_t, qkv_time, gain_time, total)
+        + finished(arrived_s, own_rows(qkv_space), own_rows(gain_space), total)
+        + finished(summed_t, own_rows(qkv_time), own_rows(gain_time), total)
     )
 
 

time: 195 us -> 188 us (0.964)
  waiting for transfers between devices: 46.2 us -> 42.2 us
  Pallas kernels: 77.7 us -> 73.8 us
  local copies, waits for them, and re-layouts: 10.4 us -> 7.51 us
  other arithmetic: 5.29 us -> 7.83 us
    all_to_all x2 -> x1, waiting for transfers between devices: 25.8 us -> 0.01 us  [spread_out(): return lax.all_to_all(mine, ('xlo', 'y', 'z', 'xhi'), 0, 0, tiled=False)]
    ppermute x2 -> x6, waiting for transfers between devices: 4.37 us -> 26.2 us  [the longest x4 22.2 us: ring_sum(): lax.ppermute(chunk(by), axis, [(i, (i + by) % size) for i in range(size)])]
    all_to_all x2 -> x1, starting transfers between devices: 23.6 us -> 6.27 us  [spread_out(): return lax.all_to_all(mine, ('xlo', 'y', 'z', 'xhi'), 0, 0, tiled=False)]
    all_to_all x0 -> x1, starting transfers between devices: none -> 12.9 us  [shards(): arrived_t = lax.all_to_all(mine_t, ('xlo', 'y'), 0, 0, tiled=False)]
    convert_element_type x0 -> x4, other arithmetic: none -> 6.57 us  [the longest x1 4.08 us: shards(): (keep_t.astype(F32) + exchanged_pair(send_t).astype(F32)).astype(BF16)]
    ppermute x2 -> x6, starting transfers between devices: 7.12 us -> 12.6 us  [the longest x4 7.53 us: ring_sum(): lax.ppermute(chunk(by), axis, [(i, (i + by) % size) for i in range(size)])]
    reduce_sum x3 -> x0, other arithmetic: 4.09 us -> none  [the longest x2 2.36 us: finished(): total = jnp.sum(arrived.astype(F32), axis=0)]
    pallas_call x1 -> x4, Pallas kernels: 14.8 us -> 18.9 us  [the longest x1 14.8 us: temporal(): pl.pallas_call(temporal_kernel, out_shape=[pltpu.HBM((peers, 2 * frames,...]
  transfers between devices with their start and end apart: 11 -> 15, of which waited for: 5 -> 8; matrix products, arithmetic and copies ran while one was open for 3% -> 4% of each run, Pallas kernels for 28% -> 28%
where the time goes in v5:
time: 188 us; the launch traced here: 187 us
  Pallas kernels  73.8 us (39%)
  starting transfers between devices  54.3 us (29%)
  waiting for transfers between devices  42.2 us (22%)
  other arithmetic  7.83 us (4%)
  local copies, waits for them, and re-layouts  7.51 us (4%)
    ppermute x4, waiting for transfers between devices, ring_sum(): lax.ppermute(chunk(by), axis, [(i, (i + by) % size) for i in range(size)])  22.2 us
    pallas_call x1, Pallas kernels, spatial_backward(): pl.pallas_call(spatial_backward_kernel, grid=(frames,), in_specs=[per_ste...  18.7 us
    all_to_all x3, starting transfers between devices, exchanged(): return lax.all_to_all(chunks, FRAME, 0, 0, tiled=False)  18.1 us
    pallas_call x1, Pallas kernels, temporal(): pl.pallas_call(temporal_kernel, out_shape=[pltpu.HBM((peers, 2 * frames,...  14.8 us
    pallas_call x1, Pallas kernels, spatial_forward(): pl.pallas_call(spatial_forward_kernel, grid=(frames,), in_specs=[per_step...  14.2 us
    pallas_call x2, Pallas kernels, split_call(): pl.pallas_call(kernel, grid_spec=pltpu.PrefetchScalarGridSpec(num_scalar_...  13.4 us
    all_to_all x1, starting transfers between devices, shards(): arrived_t = lax.all_to_all(mine_t, ('xlo', 'y'), 0, 0, tiled=False)  12.9 us
    all_to_all x3, waiting for transfers between devices, exchanged(): return lax.all_to_all(chunks, FRAME, 0, 0, tiled=False)  12.3 us
  transfers between devices with their start and end apart: 15, of which 8 were waited for; matrix products, arithmetic and copies ran while one was open for 4% of the time, Pallas kernels for 28%

profile of v5, /device:TPU:1, one launch (start us, length us, event | category | flops | bytes accessed | tf_op | source)
XLA Modules:
  0.0 186.6 jit_solution(6428898410394507448)
XLA Ops:
  0.6 2.8 %collective-permute-start = (bf16[2,24,8,768]{3,2,1,0:T(8,128)(2,1)}, bf16[2,24,8,768]{3,2,1,0:T(8,128)(2,1)S(1)}, u32[]{:S(2)}, u32[]{:S(2)}) collective-permute-start(bf16[2,24,8,768]{3,2,1,0:T(8,128)(2,1)} %tokens_ref.1), channel_id=1, source_target_pairs={{0,8},{8,16},{16,24},{24,32},{32,40},{40,48},{48,56},{56,64},{64,7... | collective-permute-start | bytes 1769480 | tf_op jit(solution)/shard_map/ppermute | solution.py:553
  3.4 2.0 %copy.23 = bf16[2,8,3,8,768]{4,3,2,0,1:T(8,128)(2,1)} copy(bf16[2,8,3,8,768]{4,3,2,1,0:T(8,128)(2,1)} %bitcast.31) | data formatting | bytes 1179648 | tf_op jit(solution)/shard_map/reshape | solution.py:615
  5.4 7.5 %all-to-all-start.1 = ((bf16[8,2,3,8,768]{4,3,2,1,0:T(8,128)(2,1)}), bf16[8,2,3,8,768]{4,3,2,1,0:T(8,128)(2,1)S(1)}, u32[]{:S(2)}, u32[]{:S(2)}) async-start(bf16[8,2,3,8,768]{4,3,2,1,0:T(8,128)(2,1)} %bitcast.28), calls=%async_computation.1 | async-start | bytes 1179648 | tf_op jit(solution)/shard_map/all_to_all | solution.py:611
  14.6 14.2 %spatial_forward.1 = (bf16[2,576,768]{2,1,0:T(8,128)(2,1)}, bf16[2,192,768]{2,1,0:T(8,128)(2,1)}, bf16[2,576,1536]{2,1,0:T(8,128)(2,1)}, bf16[2,3,1344,256]{3,2,...) custom-call(bf16[2,24,8,768]{3,2,1,0:T(8,128)(2,1)} %tokens_ref.1, ...), custom_call_target="tpu_custom_call" | custom-call | flops 14000000000 | bytes 4194304 | tf_op jit(solution)/shard_map/spatial_forward/pallas_call | solution.py:142
  28.8 7.0 %all-to-all-start = ((bf16[8,2,3,8,768]{4,3,2,1,0:T(8,128)(2,1)}), bf16[8,2,3,8,768]{4,3,2,1,0:T(8,128)(2,1)S(1)}, u32[]{:S(2)}, u32[]{:S(2)}) async-start(bf16[8,2,3,8,768]{4,3,2,1,0:T(8,128)(2,1)} %get-tuple-element.36), calls=%async_computation | async-start | bytes 1179648 | tf_op jit(solution)/shard_map/all_to_all | solution.py:611
  36.4 8.9 %all-to-all-done.mid_ref = bf16[8,2,3,8,768]{4,3,2,1,0:T(8,128)(2,1)S(1)} async-done(((bf16[8,2,3,8,768]{4,3,2,1,0:T(8,128)(2,1)}), bf16[8,2,3,8,768]{4,3,2,1,0:T(8,128)(2,1)S(1)}, u32[]{:S(2)}, u32[]{:S(2)}) %all-to-all-start) | async-done | bytes 589856 | tf_op jit(solution)/shard_map/all_to_all | solution.py:611
  46.1 14.8 %temporal.1 = (bf16[8,4,3,8,768]{4,3,2,1,0:T(8,128)(2,1)}, bf16[384,1536]{1,0:T(8,128)(2,1)}, bf16[384,3072]{1,0:T(8,128)(2,1)}) custom-call(bf16[8,2,3,8,768]{4,3,2,1,0:T(8,128)(2,1)} %copy-done.10, bf16[8,2,3,8,768]{4,3,2,1,0:T(8,128)(2,1)} %copy-done.9, f32[1,768]{1,0:T(1,128)} %reshape.52.gain_ref, bf16[768,2304]{1,0:T(8,128)(2,1)} %qkv_ref.4, ...), custom_call_target="tpu_custom_call" | custom-call | flops 17999998976 | bytes 4194304 | tf_op jit(solution)/shard_map/temporal/pallas_call | solution.py:217
  60.9 3.6 %all-to-all-start.2 = ((bf16[8,4,3,8,768]{4,3,2,1,0:T(8,128)(2,1)}), bf16[8,4,3,8,768]{4,3,2,1,0:T(8,128)(2,1)S(1)}, u32[]{:S(2)}, u32[]{:S(2)}) async-start(bf16[8,4,3,8,768]{4,3,2,1,0:T(8,128)(2,1)} %get-tuple-element.37), calls=%async_computation.2 | async-start | bytes 2359296 | tf_op jit(solution)/shard_map/all_to_all | solution.py:611
  64.5 6.7 %term_time.1 = (bf16[8,48,3072]{2,1,0:T(8,128)(2,1)}, bf16[8,48,3072]{2,1,0:T(8,128)(2,1)}) custom-call(s32[1]{0:T(128)} %bitcast.4.core_ref, bf16[384,1536]{1,0:T(8,128)(2,1)} %get-tuple-element.38.left_ref, bf16[384,3072]{1,0:T(8,128)(2,1)} %get-tuple-element.39.right_ref), custom_call_target="tpu_custom_call" | custom-call | flops 1 | bytes 1 | tf_op jit(solution)/shard_map/term_time/pallas_call | solution.py:377
  71.2 4.2 %collective-permute-start.2 = (bf16[8,48,3072]{2,1,0:T(8,128)(2,1)}, bf16[8,48,3072]{2,1,0:T(8,128)(2,1)}, u32[]{:S(2)}, u32[]{:S(2)}) collective-permute-start(bf16[8,48,3072]{2,1,0:T(8,128)(2,1)} %get-tuple-element.41), channel_id=1, source_target_pairs={{0,8},{8,0},{1,9},{9,1},{2,10},{10,2},{3,11},{11,3},{4,12},{12,4},... | collective-permute-start | bytes 7077896 | tf_op jit(solution)/shard_map/ppermute | solution.py:484
  75.4 3.3 %all-to-all-done.2.dmid_ref = bf16[8,4,3,8,768]{4,3,2,1,0:T(8,128)(2,1)S(1)} async-done(((bf16[8,4,3,8,768]{4,3,2,1,0:T(8,128)(2,1)}), bf16[8,4,3,8,768]{4,3,2,1,0:T(8,128)(2,1)S(1)}, u32[]{:S(2)}, u32[]{:S(2)}) %all-to-all-start.2) | async-done | bytes 1179680 | tf_op jit(solution)/shard_map/all_to_all | solution.py:611
  78.7 1.9 %back_projection.1.dproj_ref = bf16[2,192,768]{2,1,0:T(8,128)(2,1)} custom-call(bf16[8,4,3,8,768]{4,3,2,1,0:T(8,128)(2,1)S(1)} %all-to-all-done.2.dmid_ref, bf16[768,768]{1,0:T(8,128)(2,1)S(1)} %copy-done.5), custom_call_target="tpu_custom_call" | custom-call | flops 30000001024 | bytes 4194304 | tf_op jit(solution)/shard_map/back_projection/pallas_call | solution.py:243
  80.6 4.1 %add_convert_fusion = bf16[8,48,3072]{2,1,0:T(8,128)(2,1)} fusion(bf16[8,48,3072]{2,1,0:T(8,128)(2,1)} %collective-permute-done.2, bf16[8,48,3072]{2,1,0:T(8,128)(2,1)S(1)} %copy-done.8), kind=kLoop, calls=%fused_computation | loop fusion | flops 4718592 | bytes 7077888 | tf_op jit(solution)/shard_map/convert_element_type | solution.py:623
  84.7 12.9 %all-to-all-start.3 = ((bf16[8,48,3072]{2,1,0:T(8,128)(2,1)}), bf16[8,48,3072]{2,1,0:T(8,128)(2,1)S(1)}, u32[]{:S(2)}, u32[]{:S(2)}) async-start(bf16[8,48,3072]{2,1,0:T(8,128)(2,1)} %add_convert_fusion), calls=%async_computation.3 | async-start | bytes 4718592 | tf_op jit(solution)/shard_map/all_to_all | solution.py:626
  97.6 18.7 %spatial_backward.1 = (bf16[2,192,768]{2,1,0:T(8,128)(2,1)S(1)}, bf16[2,576,1536]{2,1,0:T(8,128)(2,1)S(1)}, bf16[2,24,8,768]{3,2,1,0:T(8,128)(2,1)}, bf16[2,24,8...) custom-call(bf16[2,192,768]{2,1,0:T(8,128)(2,1)} %back_projection.1.dproj_ref, bf16[768,2304]{1,0:T(8,128)(2,1)} %qkv_ref.5, ...), custom_call_target="tpu_custom_call" | custom-call | flops 20000000000 | bytes 4194304 | tf_op jit(solution)/shard_map/spatial_backward/pallas_call | solution.py:307
  116.4 6.7 %term_space.1 = (bf16[8,48,3072]{2,1,0:T(8,128)(2,1)}, bf16[8,48,3072]{2,1,0:T(8,128)(2,1)}) custom-call(s32[1]{0:T(128)} %bitcast.4.core_ref, bf16[2,576,768]{2,1,0:T(8,128)(2,1)S(1)} %copy-done.2, bf16[2,192,768]{2,1,0:T(8,128)(2,1)S(1)} %get-tuple-element.50.dq_ref, bf16[2,576,1536]{2,1,0:T(8,128)(2,1)S(1)} %get-tuple-element.51.dkv_ref, ...), custom_call_target="tpu_custom_call" | custom-call | flops 1 | bytes 1 | tf_op jit(solution)/shard_map/term_space/pallas_call | solution.py:377
  123.1 3.4 %all-to-all-done.3.arrived_ref = bf16[8,48,3072]{2,1,0:T(8,128)(2,1)S(1)} async-done(((bf16[8,48,3072]{2,1,0:T(8,128)(2,1)}), bf16[8,48,3072]{2,1,0:T(8,128)(2,1)S(1)}, u32[]{:S(2)}, u32[]{:S(2)}) %all-to-all-start.3) | async-done | bytes 2359328 | tf_op jit(solution)/shard_map/all_to_all | solution.py:626
  126.5 1.5 copy-done
  129.2 4.0 %collective-permute-done.5.got_ref = bf16[8,48,3072]{2,1,0:T(8,128)(2,1)S(1)} collective-permute-done((bf16[8,48,3072]{2,1,0:T(8,128)(2,1)}, bf16[8,48,3072]{2,1,0:T(8,128)(2,1)S(1)}, u32[]{:S(2)}, u32[]{:S(2)}) %collective-permute-start.5) | collective-permute-done | bytes 2359328 | tf_op jit(solution)/shard_map/ppermute | solution.py:484
  133.2 4.8 %pair_fold.1 = bf16[64,144,128]{2,1,0:T(8,128)(2,1)} custom-call(bf16[8,48,3072]{2,1,0:T(8,128)(2,1)} %get-tuple-element.53.keep_ref, bf16[8,48,3072]{2,1,0:T(8,128)(2,1)S(1)} %collective-permute-done.5.got_ref), custom_call_target="tpu_custom_call" | custom-call | flops 1 | bytes 1 | tf_op jit(solution)/shard_map/pair_fold/pallas_call | solution.py:493
  138.0 6.3 %all-to-all-start.4 = ((bf16[64,144,128]{2,1,0:T(8,128)(2,1)}), bf16[64,144,128]{2,1,0:T(8,128)(2,1)}, u32[]{:S(2)}, u32[]{:S(2)}) async-start(bf16[64,144,128]{2,1,0:T(8,128)(2,1)} %pair_fold.1), calls=%async_computation.4 | async-start | bytes 4718592 | tf_op jit(solution)/shard_map/all_to_all | solution.py:548
  145.2 1.5 dynamic-slice_convert_fusion.1.weight_ref
  147.4 1.1 collective-permute-start.4
  149.2 1.3 collective-permute-start.6
  150.4 2.4 %collective-permute-start.7 = (bf16[2,144,128]{2,1,0:T(8,128)(2,1)S(1)}, bf16[2,144,128]{2,1,0:T(8,128)(2,1)S(1)}, u32[]{:S(2)}, u32[]{:S(2)}) collective-permute-start(bf16[2,144,128]{2,1,0:T(8,128)(2,1)S(1)} %get-tuple-element.66), channel_id=1, source_target_pairs={{0,4},{2,6},{4,0},{6,2},{1,5},{3,7},{5,1},{7,3},{8,12},{10,14},{12... | collective-permute-start | bytes 221192 | tf_op jit(solution)/shard_map/ppermute | solution.py:536
  152.8 1.2 collective-permute-start.8
  154.9 2.0 %collective-permute-done.6 = bf16[2,144,128]{2,1,0:T(8,128)(2,1)S(1)} collective-permute-done((bf16[2,144,128]{2,1,0:T(8,128)(2,1)S(1)}, bf16[2,144,128]{2,1,0:T(8,128)(2,1)S(1)}, u32[]{:S(2)}, u32[]{:S(2)}) %collective-permute-start.6) | collective-permute-done | bytes 73760 | tf_op jit(solution)/shard_map/ppermute | solution.py:536
  156.9 12.4 %collective-permute-done.7 = bf16[2,144,128]{2,1,0:T(8,128)(2,1)S(1)} collective-permute-done((bf16[2,144,128]{2,1,0:T(8,128)(2,1)S(1)}, bf16[2,144,128]{2,1,0:T(8,128)(2,1)S(1)}, u32[]{:S(2)}, u32[]{:S(2)}) %collective-permute-start.7) | collective-permute-done | bytes 73760 | tf_op jit(solution)/shard_map/ppermute | solution.py:536
  169.3 7.8 %collective-permute-done.8 = bf16[2,144,128]{2,1,0:T(8,128)(2,1)S(1)} collective-permute-done((bf16[2,144,128]{2,1,0:T(8,128)(2,1)S(1)}, bf16[2,144,128]{2,1,0:T(8,128)(2,1)S(1)}, u32[]{:S(2)}, u32[]{:S(2)}) %collective-permute-start.8) | collective-permute-done | bytes 73760 | tf_op jit(solution)/shard_map/ppermute | solution.py:536
  177.2 2.7 %collective-permute-start.9 = (bf16[144,128]{1,0:T(8,128)(2,1)S(1)}, bf16[144,128]{1,0:T(8,128)(2,1)S(1)}, u32[]{:S(2)}, u32[]{:S(2)}) collective-permute-start(bf16[144,128]{1,0:T(8,128)(2,1)S(1)} %dynamic-slice_bitcast_fusion.3), channel_id=1, source_target_pairs={{0,1},{1,0},{2,3},{3,2},{4,5},{5,4},{6,7},{7,6},{8,9},{9,8},{10,11... | collective-permute-start | bytes 110600 | tf_op jit(solution)/shard_map/ppermute | solution.py:536
  179.9 1.9 %final_norm.1 = f32[2,24,8,768]{3,2,1,0:T(8,128)} custom-call(bf16[2,24,8,768]{3,2,1,0:T(8,128)(2,1)S(1)} %copy-done.6, f32[1,768]{1,0:T(1,128)S(1)} %reshape.50.gain_ref, bf16[8,4,3,8,768]{4,3,2,1,0:T(8,128)(2,1)S(1)} %all-to-all-done.2.dmid_ref, bf16[2,24,8,768]{3,2,1,0:T(8,128)(2,1)S(1)} %copy-done.7, ...), custom_call_target="tpu_custom_call" | custom-call | flops 3000000000 | bytes 4194304 | tf_op jit(solution)/shard_map/final_norm/pallas_call | solution.py:347
  183.1 2.8 %finish.2 = (f32[6,1]{1,0:T(8,128)S(1)}, f32[6,2304]{1,0:T(8,128)}, f32[6,768]{1,0:T(8,128)}) custom-call(bf16[64,144,128]{2,1,0:T(8,128)(2,1)} %all-to-all-done.4.arrived_ref, f32[6,2304]{1,0:T(8,128)S(1)} %copy-done.4, f32[6,1]{1,0:T(8,128)S(1)} %copy.20.gain_ref), custom_call_target="tpu_custom_call" | custom-call | flops 2000000000 | bytes 4194304 | tf_op jit(solution)/shard_map/finish/pallas_call | solution.py:586
  (57 shorter events, 9.4 us)
Async XLA Ops:
  0.6 12.3 %copy-start.12 = (f32[768]{0:T(1024)S(1)}, f32[768]{0:T(1024)}, u32[]{:S(2)}) copy-start(f32[768]{0:T(1024)} %param.9) | copy-start | bytes 9220
  0.6 12.3 %collective-permute-start = (bf16[2,24,8,768]{3,2,1,0:T(8,128)(2,1)}, bf16[2,24,8,768]{3,2,1,0:T(8,128)(2,1)S(1)}, u32[]{:S(2)}, u32[]{:S(2)}) collective-permute-start(bf16[2,24,8,768]{3,2,1,0:T(8,128)(2,1)} %tokens_ref.1), channel_id=1, source_target_pairs={{0,8},{8,16},{16,24},{24,32},{32,40},{40,48},{48,56},{56,64},{64,7... | collective-permute-start | bytes 1769480 | tf_op jit(solution)/shard_map/ppermute | solution.py:553
  3.4 9.8 %collective-permute-start.1 = (bf16[2,24,8,768]{3,2,1,0:T(8,128)(2,1)}, bf16[2,24,8,768]{3,2,1,0:T(8,128)(2,1)S(1)}, u32[]{:S(2)}, u32[]{:S(2)}) collective-permute-start(bf16[2,24,8,768]{3,2,1,0:T(8,128)(2,1)} %tokens_ref.1), channel_id=1, source_target_pairs={{0,120},{8,0},{16,8},{24,16},{32,24},{40,32},{48,40},{56,48},{64,5... | collective-permute-start | bytes 1769480 | tf_op jit(solution)/shard_map/ppermute | solution.py:553
  5.4 23.4 %all-to-all-start.1 = ((bf16[8,2,3,8,768]{4,3,2,1,0:T(8,128)(2,1)}), bf16[8,2,3,8,768]{4,3,2,1,0:T(8,128)(2,1)S(1)}, u32[]{:S(2)}, u32[]{:S(2)}) async-start(bf16[8,2,3,8,768]{4,3,2,1,0:T(8,128)(2,1)} %bitcast.28), calls=%async_computation.1 | async-start | bytes 1179648 | tf_op jit(solution)/shard_map/all_to_all | solution.py:611
  12.9 22.9 %copy-start.11 = (f32[768]{0:T(1024)S(1)}, f32[768]{0:T(1024)}, u32[]{:S(2)}) copy-start(f32[768]{0:T(1024)} %param.12) | copy-start | bytes 9220
  12.9 0.8 copy-start.13
  13.7 0.8 copy-start.14
  28.8 16.5 %copy-start.9 = (bf16[8,2,3,8,768]{4,3,2,1,0:T(8,128)(2,1)}, bf16[8,2,3,8,768]{4,3,2,1,0:T(8,128)(2,1)S(1)}, u32[]{:S(2)}) copy-start(bf16[8,2,3,8,768]{4,3,2,1,0:T(8,128)(2,1)S(1)} %all-to-all-done.1.cot_ref) | copy-start | bytes 1769476
  28.8 16.5 %all-to-all-start = ((bf16[8,2,3,8,768]{4,3,2,1,0:T(8,128)(2,1)}), bf16[8,2,3,8,768]{4,3,2,1,0:T(8,128)(2,1)S(1)}, u32[]{:S(2)}, u32[]{:S(2)}) async-start(bf16[8,2,3,8,768]{4,3,2,1,0:T(8,128)(2,1)} %get-tuple-element.36), calls=%async_computation | async-start | bytes 1179648 | tf_op jit(solution)/shard_map/all_to_all | solution.py:611
  45.3 0.8 copy-start.10
  60.9 17.8 %all-to-all-start.2 = ((bf16[8,4,3,8,768]{4,3,2,1,0:T(8,128)(2,1)}), bf16[8,4,3,8,768]{4,3,2,1,0:T(8,128)(2,1)S(1)}, u32[]{:S(2)}, u32[]{:S(2)}) async-start(bf16[8,4,3,8,768]{4,3,2,1,0:T(8,128)(2,1)} %get-tuple-element.37), calls=%async_computation.2 | async-start | bytes 2359296 | tf_op jit(solution)/shard_map/all_to_all | solution.py:611
  64.5 14.2 %copy-start.5 = (bf16[768,768]{1,0:T(8,128)(2,1)S(1)}, bf16[768,768]{1,0:T(8,128)(2,1)}, u32[]{:S(2)}) copy-start(bf16[768,768]{1,0:T(8,128)(2,1)} %out_ref.5) | copy-start | bytes 3538948
  71.2 9.4 %collective-permute-start.2 = (bf16[8,48,3072]{2,1,0:T(8,128)(2,1)}, bf16[8,48,3072]{2,1,0:T(8,128)(2,1)}, u32[]{:S(2)}, u32[]{:S(2)}) collective-permute-start(bf16[8,48,3072]{2,1,0:T(8,128)(2,1)} %get-tuple-element.41), channel_id=1, source_target_pairs={{0,8},{8,0},{1,9},{9,1},{2,10},{10,2},{3,11},{11,3},{4,12},{12,4},... | collective-permute-start | bytes 7077896 | tf_op jit(solution)/shard_map/ppermute | solution.py:484
  78.7 1.9 %copy-start.8 = (bf16[8,48,3072]{2,1,0:T(8,128)(2,1)S(1)}, bf16[8,48,3072]{2,1,0:T(8,128)(2,1)}, u32[]{:S(2)}) copy-start(bf16[8,48,3072]{2,1,0:T(8,128)(2,1)} %get-tuple-element.40) | copy-start | bytes 7077892
  84.7 41.9 %all-to-all-start.3 = ((bf16[8,48,3072]{2,1,0:T(8,128)(2,1)}), bf16[8,48,3072]{2,1,0:T(8,128)(2,1)S(1)}, u32[]{:S(2)}, u32[]{:S(2)}) async-start(bf16[8,48,3072]{2,1,0:T(8,128)(2,1)} %add_convert_fusion), calls=%async_computation.3 | async-start | bytes 4718592 | tf_op jit(solution)/shard_map/all_to_all | solution.py:626
  97.6 18.8 %copy-start.2 = (bf16[2,576,768]{2,1,0:T(8,128)(2,1)S(1)}, bf16[2,576,768]{2,1,0:T(8,128)(2,1)}, u32[]{:S(2)}) copy-start(bf16[2,576,768]{2,1,0:T(8,128)(2,1)} %get-tuple-element.49.y_ref) | copy-start | bytes 5308420
  97.6 18.8 %copy-start.3 = (bf16[2,192,768]{2,1,0:T(8,128)(2,1)S(1)}, bf16[2,192,768]{2,1,0:T(8,128)(2,1)}, u32[]{:S(2)}) copy-start(bf16[2,192,768]{2,1,0:T(8,128)(2,1)} %get-tuple-element.52.o_ref) | copy-start | bytes 1769476
  126.5 1.5 copy-start
  128.0 5.2 %collective-permute-start.5 = (bf16[8,48,3072]{2,1,0:T(8,128)(2,1)}, bf16[8,48,3072]{2,1,0:T(8,128)(2,1)S(1)}, u32[]{:S(2)}, u32[]{:S(2)}) collective-permute-start(bf16[8,48,3072]{2,1,0:T(8,128)(2,1)} %get-tuple-element.56), channel_id=1, source_target_pairs={{0,8},{8,0},{1,9},{9,1},{2,10},{10,2},{3,11},{11,3},{4,12},{12,4},... | collective-permute-start | bytes 7077896 | tf_op jit(solution)/shard_map/ppermute | solution.py:484
  138.0 10.5 %copy-start.1 = (bf16[8,48,3072]{2,1,0:T(8,128)(2,1)S(1)}, bf16[8,48,3072]{2,1,0:T(8,128)(2,1)}, u32[]{:S(2)}) copy-start(bf16[8,48,3072]{2,1,0:T(8,128)(2,1)} %copy-done) | copy-start | bytes 7077892
  138.0 45.1 %all-to-all-start.4 = ((bf16[64,144,128]{2,1,0:T(8,128)(2,1)}), bf16[64,144,128]{2,1,0:T(8,128)(2,1)}, u32[]{:S(2)}, u32[]{:S(2)}) async-start(bf16[64,144,128]{2,1,0:T(8,128)(2,1)} %pair_fold.1), calls=%async_computation.4 | async-start | bytes 4718592 | tf_op jit(solution)/shard_map/all_to_all | solution.py:548
  146.8 33.1 %collective-permute-start.3 = (bf16[2,24,8,768]{3,2,1,0:T(8,128)(2,1)}, bf16[2,24,8,768]{3,2,1,0:T(8,128)(2,1)S(1)}, u32[]{:S(2)}, u32[]{:S(2)}) collective-permute-start(bf16[2,24,8,768]{3,2,1,0:T(8,128)(2,1)} %get-tuple-element.47), channel_id=1, source_target_pairs={{0,120},{8,0},{16,8},{24,16},{32,24},{40,32},{48,40},{56,48},{64,5... | collective-permute-start | bytes 1769480 | tf_op jit(solution)/shard_map/ppermute | solution.py:553
  147.4 32.5 %collective-permute-start.4 = (bf16[2,24,8,768]{3,2,1,0:T(8,128)(2,1)}, bf16[2,24,8,768]{3,2,1,0:T(8,128)(2,1)S(1)}, u32[]{:S(2)}, u32[]{:S(2)}) collective-permute-start(bf16[2,24,8,768]{3,2,1,0:T(8,128)(2,1)} %get-tuple-element.48), channel_id=1, source_target_pairs={{0,8},{8,16},{16,24},{24,32},{32,40},{40,48},{48,56},{56,64},{64,7... | collective-permute-start | bytes 1769480 | tf_op jit(solution)/shard_map/ppermute | solution.py:553
  149.1 30.7 %copy-start.6 = (bf16[2,24,8,768]{3,2,1,0:T(8,128)(2,1)S(1)}, bf16[2,24,8,768]{3,2,1,0:T(8,128)(2,1)}, u32[]{:S(2)}) copy-start(bf16[2,24,8,768]{3,2,1,0:T(8,128)(2,1)} %tokens_ref.1) | copy-start | bytes 1769476
  149.1 30.7 %copy-start.7 = (bf16[2,24,8,768]{3,2,1,0:T(8,128)(2,1)S(1)}, bf16[2,24,8,768]{3,2,1,0:T(8,128)(2,1)}, u32[]{:S(2)}) copy-start(bf16[2,24,8,768]{3,2,1,0:T(8,128)(2,1)} %get-tuple-element.46.own_ref) | copy-start | bytes 1769476
  149.2 7.7 %collective-permute-start.6 = (bf16[2,144,128]{2,1,0:T(8,128)(2,1)S(1)}, bf16[2,144,128]{2,1,0:T(8,128)(2,1)S(1)}, u32[]{:S(2)}, u32[]{:S(2)}) collective-permute-start(bf16[2,144,128]{2,1,0:T(8,128)(2,1)S(1)} %get-tuple-element.64), channel_id=1, source_target_pairs={{0,2},{2,4},{4,6},{6,0},{1,3},{3,5},{5,7},{7,1},{8,10},{10,12},{12... | collective-permute-start | bytes 221192 | tf_op jit(solution)/shard_map/ppermute | solution.py:536
  150.4 18.9 %collective-permute-start.7 = (bf16[2,144,128]{2,1,0:T(8,128)(2,1)S(1)}, bf16[2,144,128]{2,1,0:T(8,128)(2,1)S(1)}, u32[]{:S(2)}, u32[]{:S(2)}) collective-permute-start(bf16[2,144,128]{2,1,0:T(8,128)(2,1)S(1)} %get-tuple-element.66), channel_id=1, source_target_pairs={{0,4},{2,6},{4,0},{6,2},{1,5},{3,7},{5,1},{7,3},{8,12},{10,14},{12... | collective-permute-start | bytes 221192 | tf_op jit(solution)/shard_map/ppermute | solution.py:536
  152.8 24.3 %collective-permute-start.8 = (bf16[2,144,128]{2,1,0:T(8,128)(2,1)S(1)}, bf16[2,144,128]{2,1,0:T(8,128)(2,1)S(1)}, u32[]{:S(2)}, u32[]{:S(2)}) collective-permute-start(bf16[2,144,128]{2,1,0:T(8,128)(2,1)S(1)} %get-tuple-element.65), channel_id=1, source_target_pairs={{0,6},{2,0},{4,2},{6,4},{1,7},{3,1},{5,3},{7,5},{8,14},{10,8},{12,... | collective-permute-start | bytes 221192 | tf_op jit(solution)/shard_map/ppermute | solution.py:536
  177.2 4.6 %collective-permute-start.9 = (bf16[144,128]{1,0:T(8,128)(2,1)S(1)}, bf16[144,128]{1,0:T(8,128)(2,1)S(1)}, u32[]{:S(2)}, u32[]{:S(2)}) collective-permute-start(bf16[144,128]{1,0:T(8,128)(2,1)S(1)} %dynamic-slice_bitcast_fusion.3), channel_id=1, source_target_pairs={{0,1},{1,0},{2,3},{3,2},{4,5},{5,4},{6,7},{7,6},{8,9},{9,8},{10,11... | collective-permute-start | bytes 110600 | tf_op jit(solution)/shard_map/ppermute | solution.py:536
  181.8 1.3 copy-start.4

commit v6 on v5

--- a/solution.py
+++ b/solution.py
@@ -515,10 +515,10 @@
     _, rows, columns = arrived.shape
     return pl.pallas_call(
         sum_fold_kernel,
-        out_shape=jax.ShapeDtypeStruct((peers, rows // peers * columns // 128, 128), BF16),
+        out_shape=pltpu.HBM((peers, rows // peers * columns // 128, 128), BF16),
         scratch_shapes=[pltpu.VMEM((columns // 128 * rows, 128), F32)],
         compiler_params=pltpu.CompilerParams(vmem_limit_bytes=16 << 20),
-        cost_estimate=cost(3),
+        cost_estimate=pl.CostEstimate(flops=1, bytes_accessed=1, transcendentals=0),
         name="sum_fold",
     )(arrived)
 
@@ -617,7 +617,10 @@
     y_s, q_s, kv_s, p_s, o_s, mid = spatial_forward(
         tokens, west, east, gain_s, qkv_space, out_space, peers
     )
-    both_rows, left_t, right_t = temporal(exchanged(mid), cot_rows, gain_t, qkv_time, out_time)
+    slices = [own_rows(a) for a in (qkv_space, gain_space, qkv_time, gain_time)]
+    mid, cot_rows = lax.optimization_barrier((mid, cot_rows))
+    mid_rows, slices = lax.optimization_barrier((exchanged(mid), slices))
+    both_rows, left_t, right_t = temporal(mid_rows, cot_rows, gain_t, qkv_time, out_time)
     both = exchanged(both_rows)
     keep_t, send_t = term_time(core, left_t, right_t, tiles)
     mine_t = (keep_t.astype(F32) + exchanged_pair(send_t).astype(F32)).astype(BF16)
@@ -628,15 +631,16 @@
     from_east = shifted(for_west, -1)
     from_west = shifted(for_east, 1)
     keep_s, send_s = term_space(core, y_s, dq, dkv, o_s, both, tiles)
-    send_s, arrived_t = lax.optimization_barrier((send_s, arrived_t))
+    folded_t = sum_fold(arrived_t, peers)
+    send_s, folded_t = lax.optimization_barrier((send_s, folded_t))
     arrived_s = spread_out(paired(keep_s, send_s, peers))
-    summed_t = summed_by_frame(sum_fold(arrived_t, peers))[None]
+    summed_t = summed_by_frame(folded_t)[None]
     layer_out = both[:, frames:].transpose(1, 0, 2, 3, 4).reshape(tokens.shape)
     grad_tokens = final_norm(tokens, gain_s, both, own, from_east, from_west)
     return (
         (layer_out, grad_tokens)
-        + finished(arrived_s, own_rows(qkv_space), own_rows(gain_space), total)
-        + finished(summed_t, own_rows(qkv_time), own_rows(gain_time), total)
+        + finished(arrived_s, slices[0], slices[1], total)
+        + finished(summed_t, slices[2], slices[3], total)
     )
 
 

time: 188 us -> 187 us (level)
    ppermute x4, waiting for transfers between devices: 22.2 us -> 24.2 us  [ring_sum(): lax.ppermute(chunk(by), axis, [(i, (i + by) % size) for i in range(size)])]
  transfers between devices with their start and end apart: 15 -> 15, of which waited for: 8 -> 8; matrix products, arithmetic and copies ran while one was open for 4% -> 4% of each run, Pallas kernels for 28% -> 27%
where the time goes in v6:
time: 187 us; the launch traced here: 186 us
  Pallas kernels  72.8 us (39%)
  starting transfers between devices  54.2 us (29%)
  waiting for transfers between devices  42.7 us (23%)
  other arithmetic  7.87 us (4%)
  local copies, waits for them, and re-layouts  7.47 us (4%)
    ppermute x4, waiting for transfers between devices, ring_sum(): lax.ppermute(chunk(by), axis, [(i, (i + by) % size) for i in range(size)])  24.2 us
    pallas_call x1, Pallas kernels, spatial_backward(): pl.pallas_call(spatial_backward_kernel, grid=(frames,), in_specs=[per_ste...  18.7 us
    all_to_all x3, starting transfers between devices, exchanged(): return lax.all_to_all(chunks, FRAME, 0, 0, tiled=False)  18 us
    pallas_call x1, Pallas kernels, temporal(): pl.pallas_call(temporal_kernel, out_shape=[pltpu.HBM((peers, 2 * frames,...  14.8 us
    pallas_call x1, Pallas kernels, spatial_forward(): pl.pallas_call(spatial_forward_kernel, grid=(frames,), in_specs=[per_step...  14.2 us
    pallas_call x2, Pallas kernels, split_call(): pl.pallas_call(kernel, grid_spec=pltpu.PrefetchScalarGridSpec(num_scalar_...  13.3 us
    all_to_all x1, starting transfers between devices, shards(): arrived_t = lax.all_to_all(mine_t, ('xlo', 'y'), 0, 0, tiled=False)  12.9 us
    all_to_all x3, waiting for transfers between devices, exchanged(): return lax.all_to_all(chunks, FRAME, 0, 0, tiled=False)  10.6 us
  transfers between devices with their start and end apart: 15, of which 8 were waited for; matrix products, arithmetic and copies ran while one was open for 4% of the time, Pallas kernels for 27%

profile of v6, /device:TPU:1, one launch (start us, length us, event | category | flops | bytes accessed | tf_op | source)
XLA Modules:
  0.0 185.8 jit_solution(9582924632639053870)
XLA Ops:
  0.6 2.8 %collective-permute-start = (bf16[2,24,8,768]{3,2,1,0:T(8,128)(2,1)}, bf16[2,24,8,768]{3,2,1,0:T(8,128)(2,1)S(1)}, u32[]{:S(2)}, u32[]{:S(2)}) collective-permute-start(bf16[2,24,8,768]{3,2,1,0:T(8,128)(2,1)} %tokens_ref.1), channel_id=1, source_target_pairs={{0,8},{8,16},{16,24},{24,32},{32,40},{40,48},{48,56},{56,64},{64,7... | collective-permute-start | bytes 1769480 | tf_op jit(solution)/shard_map/ppermute | solution.py:553
  3.4 2.0 %copy.23 = bf16[2,8,3,8,768]{4,3,2,0,1:T(8,128)(2,1)} copy(bf16[2,8,3,8,768]{4,3,2,1,0:T(8,128)(2,1)} %bitcast.29) | data formatting | bytes 1179648 | tf_op jit(solution)/shard_map/reshape | solution.py:615
  5.4 7.5 %all-to-all-start = ((bf16[8,2,3,8,768]{4,3,2,1,0:T(8,128)(2,1)}), bf16[8,2,3,8,768]{4,3,2,1,0:T(8,128)(2,1)S(1)}, u32[]{:S(2)}, u32[]{:S(2)}) async-start(bf16[8,2,3,8,768]{4,3,2,1,0:T(8,128)(2,1)} %bitcast.26), calls=%async_computation | async-start | bytes 1179648 | tf_op jit(solution)/shard_map/all_to_all | solution.py:611
  14.6 14.2 %spatial_forward.1 = (bf16[2,576,768]{2,1,0:T(8,128)(2,1)}, bf16[2,192,768]{2,1,0:T(8,128)(2,1)}, bf16[2,576,1536]{2,1,0:T(8,128)(2,1)}, bf16[2,3,1344,256]{3,2,...) custom-call(bf16[2,24,8,768]{3,2,1,0:T(8,128)(2,1)} %tokens_ref.1, ...), custom_call_target="tpu_custom_call" | custom-call | flops 14000000000 | bytes 4194304 | tf_op jit(solution)/shard_map/spatial_forward/pallas_call | solution.py:142
  28.8 7.0 %all-to-all-start.1 = ((bf16[8,2,3,8,768]{4,3,2,1,0:T(8,128)(2,1)}), bf16[8,2,3,8,768]{4,3,2,1,0:T(8,128)(2,1)S(1)}, u32[]{:S(2)}, u32[]{:S(2)}) async-start(bf16[8,2,3,8,768]{4,3,2,1,0:T(8,128)(2,1)} %get-tuple-element.44), calls=%async_computation.1 | async-start | bytes 1179648 | tf_op jit(solution)/shard_map/all_to_all | solution.py:611
  36.5 1.6 dynamic-slice_convert_fusion
  38.1 7.2 %all-to-all-done.1.mid_ref = bf16[8,2,3,8,768]{4,3,2,1,0:T(8,128)(2,1)S(1)} async-done(((bf16[8,2,3,8,768]{4,3,2,1,0:T(8,128)(2,1)}), bf16[8,2,3,8,768]{4,3,2,1,0:T(8,128)(2,1)S(1)}, u32[]{:S(2)}, u32[]{:S(2)}) %all-to-all-start.1) | async-done | bytes 589856 | tf_op jit(solution)/shard_map/all_to_all | solution.py:611
  46.1 14.8 %temporal.1 = (bf16[8,4,3,8,768]{4,3,2,1,0:T(8,128)(2,1)}, bf16[384,1536]{1,0:T(8,128)(2,1)}, bf16[384,3072]{1,0:T(8,128)(2,1)}) custom-call(bf16[8,2,3,8,768]{4,3,2,1,0:T(8,128)(2,1)} %copy-done.9, bf16[8,2,3,8,768]{4,3,2,1,0:T(8,128)(2,1)} %copy-done.8, f32[1,768]{1,0:T(1,128)} %reshape.52.gain_ref, bf16[768,2304]{1,0:T(8,128)(2,1)} %qkv_ref.4, ...), custom_call_target="tpu_custom_call" | custom-call | flops 17999998976 | bytes 4194304 | tf_op jit(solution)/shard_map/temporal/pallas_call | solution.py:217
  60.9 3.6 %all-to-all-start.2 = ((bf16[8,4,3,8,768]{4,3,2,1,0:T(8,128)(2,1)}), bf16[8,4,3,8,768]{4,3,2,1,0:T(8,128)(2,1)S(1)}, u32[]{:S(2)}, u32[]{:S(2)}) async-start(bf16[8,4,3,8,768]{4,3,2,1,0:T(8,128)(2,1)} %get-tuple-element.47), calls=%async_computation.2 | async-start | bytes 2359296 | tf_op jit(solution)/shard_map/all_to_all | solution.py:611
  64.5 6.6 %term_time.1 = (bf16[8,48,3072]{2,1,0:T(8,128)(2,1)}, bf16[8,48,3072]{2,1,0:T(8,128)(2,1)}) custom-call(s32[1]{0:T(128)} %bitcast.4.core_ref, bf16[384,1536]{1,0:T(8,128)(2,1)} %get-tuple-element.48.left_ref, bf16[384,3072]{1,0:T(8,128)(2,1)} %get-tuple-element.49.right_ref), custom_call_target="tpu_custom_call" | custom-call | flops 1 | bytes 1 | tf_op jit(solution)/shard_map/term_time/pallas_call | solution.py:377
  71.1 4.2 %collective-permute-start.2 = (bf16[8,48,3072]{2,1,0:T(8,128)(2,1)}, bf16[8,48,3072]{2,1,0:T(8,128)(2,1)}, u32[]{:S(2)}, u32[]{:S(2)}) collective-permute-start(bf16[8,48,3072]{2,1,0:T(8,128)(2,1)} %get-tuple-element.51), channel_id=1, source_target_pairs={{0,8},{8,0},{1,9},{9,1},{2,10},{10,2},{3,11},{11,3},{4,12},{12,4},... | collective-permute-start | bytes 7077896 | tf_op jit(solution)/shard_map/ppermute | solution.py:484
  75.3 3.4 %all-to-all-done.2.dmid_ref = bf16[8,4,3,8,768]{4,3,2,1,0:T(8,128)(2,1)S(1)} async-done(((bf16[8,4,3,8,768]{4,3,2,1,0:T(8,128)(2,1)}), bf16[8,4,3,8,768]{4,3,2,1,0:T(8,128)(2,1)S(1)}, u32[]{:S(2)}, u32[]{:S(2)}) %all-to-all-start.2) | async-done | bytes 1179680 | tf_op jit(solution)/shard_map/all_to_all | solution.py:611
  78.7 1.9 %back_projection.1.dproj_ref = bf16[2,192,768]{2,1,0:T(8,128)(2,1)} custom-call(bf16[8,4,3,8,768]{4,3,2,1,0:T(8,128)(2,1)S(1)} %all-to-all-done.2.dmid_ref, bf16[768,768]{1,0:T(8,128)(2,1)S(1)} %copy-done.4), custom_call_target="tpu_custom_call" | custom-call | flops 30000001024 | bytes 4194304 | tf_op jit(solution)/shard_map/back_projection/pallas_call | solution.py:243
  80.6 4.1 %add_convert_fusion = bf16[8,48,3072]{2,1,0:T(8,128)(2,1)} fusion(bf16[8,48,3072]{2,1,0:T(8,128)(2,1)} %collective-permute-done.2, bf16[8,48,3072]{2,1,0:T(8,128)(2,1)S(1)} %copy-done.7), kind=kLoop, calls=%fused_computation | loop fusion | flops 4718592 | bytes 7077888 | tf_op jit(solution)/shard_map/convert_element_type | solution.py:626
  84.6 12.9 %all-to-all-start.3 = ((bf16[8,48,3072]{2,1,0:T(8,128)(2,1)}), bf16[8,48,3072]{2,1,0:T(8,128)(2,1)S(1)}, u32[]{:S(2)}, u32[]{:S(2)}) async-start(bf16[8,48,3072]{2,1,0:T(8,128)(2,1)} %add_convert_fusion), calls=%async_computation.3 | async-start | bytes 4718592 | tf_op jit(solution)/shard_map/all_to_all | solution.py:629
  97.6 18.7 %spatial_backward.1 = (bf16[2,192,768]{2,1,0:T(8,128)(2,1)S(1)}, bf16[2,576,1536]{2,1,0:T(8,128)(2,1)S(1)}, bf16[2,24,8,768]{3,2,1,0:T(8,128)(2,1)}, bf16[2,24,8...) custom-call(bf16[2,192,768]{2,1,0:T(8,128)(2,1)} %back_projection.1.dproj_ref, bf16[768,2304]{1,0:T(8,128)(2,1)} %qkv_ref.5, ...), custom_call_target="tpu_custom_call" | custom-call | flops 20000000000 | bytes 4194304 | tf_op jit(solution)/shard_map/spatial_backward/pallas_call | solution.py:307
  116.3 6.7 %term_space.1 = (bf16[8,48,3072]{2,1,0:T(8,128)(2,1)}, bf16[8,48,3072]{2,1,0:T(8,128)(2,1)}) custom-call(s32[1]{0:T(128)} %bitcast.4.core_ref, bf16[2,576,768]{2,1,0:T(8,128)(2,1)S(1)} %copy-done, bf16[2,192,768]{2,1,0:T(8,128)(2,1)S(1)} %get-tuple-element.60.dq_ref, bf16[2,576,1536]{2,1,0:T(8,128)(2,1)S(1)} %get-tuple-element.61.dkv_ref, ...), custom_call_target="tpu_custom_call" | custom-call | flops 1 | bytes 1 | tf_op jit(solution)/shard_map/term_space/pallas_call | solution.py:377
  123.0 3.5 %all-to-all-done.3.arrived_ref = bf16[8,48,3072]{2,1,0:T(8,128)(2,1)S(1)} async-done(((bf16[8,48,3072]{2,1,0:T(8,128)(2,1)}), bf16[8,48,3072]{2,1,0:T(8,128)(2,1)S(1)}, u32[]{:S(2)}, u32[]{:S(2)}) %all-to-all-start.3) | async-done | bytes 2359328 | tf_op jit(solution)/shard_map/all_to_all | solution.py:629
  126.5 1.3 sum_fold.1
  129.1 4.2 %collective-permute-done.5.got_ref = bf16[8,48,3072]{2,1,0:T(8,128)(2,1)S(1)} collective-permute-done((bf16[8,48,3072]{2,1,0:T(8,128)(2,1)S(1)}, bf16[8,48,3072]{2,1,0:T(8,128)(2,1)S(1)}, u32[]{:S(2)}, u32[]{:S(2)}) %collective-permute-start.5) | collective-permute-done | bytes 2359328 | tf_op jit(solution)/shard_map/ppermute | solution.py:484
  133.3 4.8 %pair_fold.1 = bf16[64,144,128]{2,1,0:T(8,128)(2,1)} custom-call(bf16[8,48,3072]{2,1,0:T(8,128)(2,1)} %get-tuple-element.63.keep_ref, bf16[8,48,3072]{2,1,0:T(8,128)(2,1)S(1)} %collective-permute-done.5.got_ref), custom_call_target="tpu_custom_call" | custom-call | flops 1 | bytes 1 | tf_op jit(solution)/shard_map/pair_fold/pallas_call | solution.py:493
  138.1 6.0 %all-to-all-start.4 = ((bf16[64,144,128]{2,1,0:T(8,128)(2,1)}), bf16[64,144,128]{2,1,0:T(8,128)(2,1)S(1)}, u32[]{:S(2)}, u32[]{:S(2)}) async-start(bf16[64,144,128]{2,1,0:T(8,128)(2,1)} %pair_fold.1), calls=%async_computation.4 | async-start | bytes 4718592 | tf_op jit(solution)/shard_map/all_to_all | solution.py:548
  145.0 1.3 collective-permute-start.4
  147.2 1.3 collective-permute-start.6
  148.4 2.4 %collective-permute-start.7 = (bf16[2,144,128]{2,1,0:T(8,128)(2,1)S(1)}, bf16[2,144,128]{2,1,0:T(8,128)(2,1)S(1)}, u32[]{:S(2)}, u32[]{:S(2)}) collective-permute-start(bf16[2,144,128]{2,1,0:T(8,128)(2,1)S(1)} %get-tuple-element.80), channel_id=1, source_target_pairs={{0,4},{2,6},{4,0},{6,2},{1,5},{3,7},{5,1},{7,3},{8,12},{10,14},{12... | collective-permute-start | bytes 221192 | tf_op jit(solution)/shard_map/ppermute | solution.py:536
  150.8 1.2 collective-permute-start.8
  152.9 4.6 %collective-permute-done.6 = bf16[2,144,128]{2,1,0:T(8,128)(2,1)S(1)} collective-permute-done((bf16[2,144,128]{2,1,0:T(8,128)(2,1)S(1)}, bf16[2,144,128]{2,1,0:T(8,128)(2,1)S(1)}, u32[]{:S(2)}, u32[]{:S(2)}) %collective-permute-start.6) | collective-permute-done | bytes 73760 | tf_op jit(solution)/shard_map/ppermute | solution.py:536
  157.5 14.5 %collective-permute-done.7 = bf16[2,144,128]{2,1,0:T(8,128)(2,1)S(1)} collective-permute-done((bf16[2,144,128]{2,1,0:T(8,128)(2,1)S(1)}, bf16[2,144,128]{2,1,0:T(8,128)(2,1)S(1)}, u32[]{:S(2)}, u32[]{:S(2)}) %collective-permute-start.7) | collective-permute-done | bytes 73760 | tf_op jit(solution)/shard_map/ppermute | solution.py:536
  172.0 5.1 %collective-permute-done.8 = bf16[2,144,128]{2,1,0:T(8,128)(2,1)S(1)} collective-permute-done((bf16[2,144,128]{2,1,0:T(8,128)(2,1)S(1)}, bf16[2,144,128]{2,1,0:T(8,128)(2,1)S(1)}, u32[]{:S(2)}, u32[]{:S(2)}) %collective-permute-start.8) | collective-permute-done | bytes 73760 | tf_op jit(solution)/shard_map/ppermute | solution.py:536
  178.1 2.7 %collective-permute-start.9 = (bf16[144,128]{1,0:T(8,128)(2,1)S(1)}, bf16[144,128]{1,0:T(8,128)(2,1)S(1)}, u32[]{:S(2)}, u32[]{:S(2)}) collective-permute-start(bf16[144,128]{1,0:T(8,128)(2,1)S(1)} %dynamic-slice_bitcast_fusion.3), channel_id=1, source_target_pairs={{0,1},{1,0},{2,3},{3,2},{4,5},{5,4},{6,7},{7,6},{8,9},{9,8},{10,11... | collective-permute-start | bytes 110600 | tf_op jit(solution)/shard_map/ppermute | solution.py:536
  180.8 1.9 %final_norm.1 = f32[2,24,8,768]{3,2,1,0:T(8,128)} custom-call(bf16[2,24,8,768]{3,2,1,0:T(8,128)(2,1)S(1)} %copy-done.5, f32[1,768]{1,0:T(1,128)S(1)} %reshape.50.gain_ref, bf16[8,4,3,8,768]{4,3,2,1,0:T(8,128)(2,1)S(1)} %all-to-all-done.2.dmid_ref, bf16[2,24,8,768]{3,2,1,0:T(8,128)(2,1)S(1)} %copy-done.6, ...), custom_call_target="tpu_custom_call" | custom-call | flops 3000000000 | bytes 4194304 | tf_op jit(solution)/shard_map/final_norm/pallas_call | solution.py:347
  184.1 1.1 finish.2
  (56 shorter events, 10.1 us)
Async XLA Ops:
  0.6 12.3 %copy-start.10 = (f32[768]{0:T(1024)S(1)}, f32[768]{0:T(1024)}, u32[]{:S(2)}) copy-start(f32[768]{0:T(1024)} %param.9) | copy-start | bytes 9220
  0.6 12.3 %collective-permute-start = (bf16[2,24,8,768]{3,2,1,0:T(8,128)(2,1)}, bf16[2,24,8,768]{3,2,1,0:T(8,128)(2,1)S(1)}, u32[]{:S(2)}, u32[]{:S(2)}) collective-permute-start(bf16[2,24,8,768]{3,2,1,0:T(8,128)(2,1)} %tokens_ref.1), channel_id=1, source_target_pairs={{0,8},{8,16},{16,24},{24,32},{32,40},{40,48},{48,56},{56,64},{64,7... | collective-permute-start | bytes 1769480 | tf_op jit(solution)/shard_map/ppermute | solution.py:553
  3.4 9.8 %collective-permute-start.1 = (bf16[2,24,8,768]{3,2,1,0:T(8,128)(2,1)}, bf16[2,24,8,768]{3,2,1,0:T(8,128)(2,1)S(1)}, u32[]{:S(2)}, u32[]{:S(2)}) collective-permute-start(bf16[2,24,8,768]{3,2,1,0:T(8,128)(2,1)} %tokens_ref.1), channel_id=1, source_target_pairs={{0,120},{8,0},{16,8},{24,16},{32,24},{40,32},{48,40},{56,48},{64,5... | collective-permute-start | bytes 1769480 | tf_op jit(solution)/shard_map/ppermute | solution.py:553
  5.4 23.4 %all-to-all-start = ((bf16[8,2,3,8,768]{4,3,2,1,0:T(8,128)(2,1)}), bf16[8,2,3,8,768]{4,3,2,1,0:T(8,128)(2,1)S(1)}, u32[]{:S(2)}, u32[]{:S(2)}) async-start(bf16[8,2,3,8,768]{4,3,2,1,0:T(8,128)(2,1)} %bitcast.26), calls=%async_computation | async-start | bytes 1179648 | tf_op jit(solution)/shard_map/all_to_all | solution.py:611
  12.9 22.9 %copy-start.11 = (f32[768]{0:T(1024)S(1)}, f32[768]{0:T(1024)}, u32[]{:S(2)}) copy-start(f32[768]{0:T(1024)} %param.12) | copy-start | bytes 9220
  12.9 0.8 copy-start.13
  13.8 0.8 copy-start.14
  28.8 16.5 %copy-start.8 = (bf16[8,2,3,8,768]{4,3,2,1,0:T(8,128)(2,1)}, bf16[8,2,3,8,768]{4,3,2,1,0:T(8,128)(2,1)S(1)}, u32[]{:S(2)}) copy-start(bf16[8,2,3,8,768]{4,3,2,1,0:T(8,128)(2,1)S(1)} %all-to-all-done.cot_ref) | copy-start | bytes 1769476
  28.8 16.5 %all-to-all-start.1 = ((bf16[8,2,3,8,768]{4,3,2,1,0:T(8,128)(2,1)}), bf16[8,2,3,8,768]{4,3,2,1,0:T(8,128)(2,1)S(1)}, u32[]{:S(2)}, u32[]{:S(2)}) async-start(bf16[8,2,3,8,768]{4,3,2,1,0:T(8,128)(2,1)} %get-tuple-element.44), calls=%async_computation.1 | async-start | bytes 1179648 | tf_op jit(solution)/shard_map/all_to_all | solution.py:611
  45.3 0.8 copy-start.9
  60.9 17.8 %all-to-all-start.2 = ((bf16[8,4,3,8,768]{4,3,2,1,0:T(8,128)(2,1)}), bf16[8,4,3,8,768]{4,3,2,1,0:T(8,128)(2,1)S(1)}, u32[]{:S(2)}, u32[]{:S(2)}) async-start(bf16[8,4,3,8,768]{4,3,2,1,0:T(8,128)(2,1)} %get-tuple-element.47), calls=%async_computation.2 | async-start | bytes 2359296 | tf_op jit(solution)/shard_map/all_to_all | solution.py:611
  64.5 14.2 %copy-start.4 = (bf16[768,768]{1,0:T(8,128)(2,1)S(1)}, bf16[768,768]{1,0:T(8,128)(2,1)}, u32[]{:S(2)}) copy-start(bf16[768,768]{1,0:T(8,128)(2,1)} %out_ref.5) | copy-start | bytes 3538948
  71.1 9.5 %collective-permute-start.2 = (bf16[8,48,3072]{2,1,0:T(8,128)(2,1)}, bf16[8,48,3072]{2,1,0:T(8,128)(2,1)}, u32[]{:S(2)}, u32[]{:S(2)}) collective-permute-start(bf16[8,48,3072]{2,1,0:T(8,128)(2,1)} %get-tuple-element.51), channel_id=1, source_target_pairs={{0,8},{8,0},{1,9},{9,1},{2,10},{10,2},{3,11},{11,3},{4,12},{12,4},... | collective-permute-start | bytes 7077896 | tf_op jit(solution)/shard_map/ppermute | solution.py:484
  78.7 1.9 %copy-start.7 = (bf16[8,48,3072]{2,1,0:T(8,128)(2,1)S(1)}, bf16[8,48,3072]{2,1,0:T(8,128)(2,1)}, u32[]{:S(2)}) copy-start(bf16[8,48,3072]{2,1,0:T(8,128)(2,1)} %get-tuple-element.50) | copy-start | bytes 7077892
  84.6 41.9 %all-to-all-start.3 = ((bf16[8,48,3072]{2,1,0:T(8,128)(2,1)}), bf16[8,48,3072]{2,1,0:T(8,128)(2,1)S(1)}, u32[]{:S(2)}, u32[]{:S(2)}) async-start(bf16[8,48,3072]{2,1,0:T(8,128)(2,1)} %add_convert_fusion), calls=%async_computation.3 | async-start | bytes 4718592 | tf_op jit(solution)/shard_map/all_to_all | solution.py:629
  97.6 18.7 %copy-start = (bf16[2,576,768]{2,1,0:T(8,128)(2,1)S(1)}, bf16[2,576,768]{2,1,0:T(8,128)(2,1)}, u32[]{:S(2)}) copy-start(bf16[2,576,768]{2,1,0:T(8,128)(2,1)} %get-tuple-element.59.y_ref) | copy-start | bytes 5308420
  97.6 18.7 %copy-start.1 = (bf16[2,192,768]{2,1,0:T(8,128)(2,1)S(1)}, bf16[2,192,768]{2,1,0:T(8,128)(2,1)}, u32[]{:S(2)}) copy-start(bf16[2,192,768]{2,1,0:T(8,128)(2,1)} %get-tuple-element.62.o_ref) | copy-start | bytes 1769476
  126.5 1.8 copy-start.12
  128.3 5.0 %collective-permute-start.5 = (bf16[8,48,3072]{2,1,0:T(8,128)(2,1)S(1)}, bf16[8,48,3072]{2,1,0:T(8,128)(2,1)S(1)}, u32[]{:S(2)}, u32[]{:S(2)}) collective-permute-start(bf16[8,48,3072]{2,1,0:T(8,128)(2,1)S(1)} %copy-done.12), channel_id=1, source_target_pairs={{0,8},{8,0},{1,9},{9,1},{2,10},{10,2},{3,11},{11,3},{4,12},{12,4},... | collective-permute-start | bytes 7077896 | tf_op jit(solution)/shard_map/ppermute | solution.py:484
  138.1 46.0 %all-to-all-start.4 = ((bf16[64,144,128]{2,1,0:T(8,128)(2,1)}), bf16[64,144,128]{2,1,0:T(8,128)(2,1)S(1)}, u32[]{:S(2)}, u32[]{:S(2)}) async-start(bf16[64,144,128]{2,1,0:T(8,128)(2,1)} %pair_fold.1), calls=%async_computation.4 | async-start | bytes 4718592 | tf_op jit(solution)/shard_map/all_to_all | solution.py:548
  144.3 36.5 %copy-start.5 = (bf16[2,24,8,768]{3,2,1,0:T(8,128)(2,1)S(1)}, bf16[2,24,8,768]{3,2,1,0:T(8,128)(2,1)}, u32[]{:S(2)}) copy-start(bf16[2,24,8,768]{3,2,1,0:T(8,128)(2,1)} %tokens_ref.1) | copy-start | bytes 1769476
  144.3 36.5 %copy-start.6 = (bf16[2,24,8,768]{3,2,1,0:T(8,128)(2,1)S(1)}, bf16[2,24,8,768]{3,2,1,0:T(8,128)(2,1)}, u32[]{:S(2)}) copy-start(bf16[2,24,8,768]{3,2,1,0:T(8,128)(2,1)} %get-tuple-element.56.own_ref) | copy-start | bytes 1769476
  144.3 36.5 %collective-permute-start.3 = (bf16[2,24,8,768]{3,2,1,0:T(8,128)(2,1)}, bf16[2,24,8,768]{3,2,1,0:T(8,128)(2,1)S(1)}, u32[]{:S(2)}, u32[]{:S(2)}) collective-permute-start(bf16[2,24,8,768]{3,2,1,0:T(8,128)(2,1)} %get-tuple-element.57), channel_id=1, source_target_pairs={{0,120},{8,0},{16,8},{24,16},{32,24},{40,32},{48,40},{56,48},{64,5... | collective-permute-start | bytes 1769480 | tf_op jit(solution)/shard_map/ppermute | solution.py:553
  145.0 35.8 %collective-permute-start.4 = (bf16[2,24,8,768]{3,2,1,0:T(8,128)(2,1)}, bf16[2,24,8,768]{3,2,1,0:T(8,128)(2,1)S(1)}, u32[]{:S(2)}, u32[]{:S(2)}) collective-permute-start(bf16[2,24,8,768]{3,2,1,0:T(8,128)(2,1)} %get-tuple-element.58), channel_id=1, source_target_pairs={{0,8},{8,16},{16,24},{24,32},{32,40},{40,48},{48,56},{56,64},{64,7... | collective-permute-start | bytes 1769480 | tf_op jit(solution)/shard_map/ppermute | solution.py:553
  147.2 10.3 %collective-permute-start.6 = (bf16[2,144,128]{2,1,0:T(8,128)(2,1)S(1)}, bf16[2,144,128]{2,1,0:T(8,128)(2,1)S(1)}, u32[]{:S(2)}, u32[]{:S(2)}) collective-permute-start(bf16[2,144,128]{2,1,0:T(8,128)(2,1)S(1)} %get-tuple-element.78), channel_id=1, source_target_pairs={{0,2},{2,4},{4,6},{6,0},{1,3},{3,5},{5,7},{7,1},{8,10},{10,12},{12... | collective-permute-start | bytes 221192 | tf_op jit(solution)/shard_map/ppermute | solution.py:536
  148.4 23.6 %collective-permute-start.7 = (bf16[2,144,128]{2,1,0:T(8,128)(2,1)S(1)}, bf16[2,144,128]{2,1,0:T(8,128)(2,1)S(1)}, u32[]{:S(2)}, u32[]{:S(2)}) collective-permute-start(bf16[2,144,128]{2,1,0:T(8,128)(2,1)S(1)} %get-tuple-element.80), channel_id=1, source_target_pairs={{0,4},{2,6},{4,0},{6,2},{1,5},{3,7},{5,1},{7,3},{8,12},{10,14},{12... | collective-permute-start | bytes 221192 | tf_op jit(solution)/shard_map/ppermute | solution.py:536
  150.8 26.3 %collective-permute-start.8 = (bf16[2,144,128]{2,1,0:T(8,128)(2,1)S(1)}, bf16[2,144,128]{2,1,0:T(8,128)(2,1)S(1)}, u32[]{:S(2)}, u32[]{:S(2)}) collective-permute-start(bf16[2,144,128]{2,1,0:T(8,128)(2,1)S(1)} %get-tuple-element.79), channel_id=1, source_target_pairs={{0,6},{2,0},{4,2},{6,4},{1,7},{3,1},{5,3},{7,5},{8,14},{10,8},{12,... | collective-permute-start | bytes 221192 | tf_op jit(solution)/shard_map/ppermute | solution.py:536
  178.1 4.7 %collective-permute-start.9 = (bf16[144,128]{1,0:T(8,128)(2,1)S(1)}, bf16[144,128]{1,0:T(8,128)(2,1)S(1)}, u32[]{:S(2)}, u32[]{:S(2)}) collective-permute-start(bf16[144,128]{1,0:T(8,128)(2,1)S(1)} %dynamic-slice_bitcast_fusion.3), channel_id=1, source_target_pairs={{0,1},{1,0},{2,3},{3,2},{4,5},{5,4},{6,7},{7,6},{8,9},{9,8},{10,11... | collective-permute-start | bytes 110600 | tf_op jit(solution)/shard_map/ppermute | solution.py:536
  180.8 1.9 %copy-start.3 = (f32[6,2304]{1,0:T(8,128)S(1)}, f32[6,2304]{1,0:T(8,128)}, u32[]{:S(2)}) copy-start(f32[6,2304]{1,0:T(8,128)} %get-tuple-element.73.weight_ref) | copy-start | bytes 165892
  182.8 1.3 copy-start.2

commit v7 on v6

--- a/solution.py
+++ b/solution.py
@@ -538,10 +538,10 @@
     return total
 
 
-def summed_by_frame(chunks):
+def summed_over_xhi(chunks):
     z, xhi = lax.axis_size("z"), lax.axis_size("xhi")
-    after_z = ring_sum(chunks.reshape((z, xhi) + chunks.shape[1:]), "z").astype(BF16)
-    return ring_sum(after_z, "xhi")
+    split = chunks.reshape((z, xhi) + chunks.shape[1:])
+    return ring_sum(jnp.swapaxes(split, 0, 1), "xhi").astype(BF16)
 
 
 def spread_out(mine):
@@ -633,8 +633,11 @@
     keep_s, send_s = term_space(core, y_s, dq, dkv, o_s, both, tiles)
     folded_t = sum_fold(arrived_t, peers)
     send_s, folded_t = lax.optimization_barrier((send_s, folded_t))
-    arrived_s = spread_out(paired(keep_s, send_s, peers))
-    summed_t = summed_by_frame(folded_t)[None]
+    mine_s = paired(keep_s, send_s, peers)
+    after_x = summed_over_xhi(folded_t)
+    mine_s, after_x = lax.optimization_barrier((mine_s, after_x))
+    arrived_s = spread_out(mine_s)
+    summed_t = ring_sum(after_x, "z")[None]
     layer_out = both[:, frames:].transpose(1, 0, 2, 3, 4).reshape(tokens.shape)
     grad_tokens = final_norm(tokens, gain_s, both, own, from_east, from_west)
     return (

time: 187 us -> 193 us (1.032)
  waiting for transfers between devices: 42.7 us -> 46.2 us
    ppermute x4, waiting for transfers between devices: 0.27 us -> 25.9 us  [shifted(): lax.ppermute(shard, TILE, [(i, (i + by) % size) for i in range(size)])]
    ppermute x4, waiting for transfers between devices: 24.2 us -> 6.3 us  [ring_sum(): lax.ppermute(chunk(by), axis, [(i, (i + by) % size) for i in range(size)])]
    ppermute x2, waiting for transfers between devices: 4.16 us -> 0.01 us  [exchanged_pair(): return lax.ppermute(send, 'core', [(0, 1), (1, 0)])]
  transfers between devices with their start and end apart: 15 -> 15, of which waited for: 8 -> 6; matrix products, arithmetic and copies ran while one was open for 4% -> 5% of each run, Pallas kernels for 27% -> 27%
where the time goes in v7:
time: 193 us; the launch traced here: 190 us
  Pallas kernels  73.8 us (38%)
  starting transfers between devices  53.2 us (28%)
  waiting for transfers between devices  46.2 us (24%)
  other arithmetic  8.64 us (4%)
  local copies, waits for them, and re-layouts  7.64 us (4%)
    ppermute x4, waiting for transfers between devices, shifted(): lax.ppermute(shard, TILE, [(i, (i + by) % size) for i in range(size)])  25.9 us
    pallas_call x1, Pallas kernels, spatial_backward(): pl.pallas_call(spatial_backward_kernel, grid=(frames,), in_specs=[per_ste...  18.7 us
    all_to_all x3, starting transfers between devices, exchanged(): return lax.all_to_all(chunks, FRAME, 0, 0, tiled=False)  18 us
    pallas_call x1, Pallas kernels, temporal(): pl.pallas_call(temporal_kernel, out_shape=[pltpu.HBM((peers, 2 * frames,...  14.8 us
    pallas_call x1, Pallas kernels, spatial_forward(): pl.pallas_call(spatial_forward_kernel, grid=(frames,), in_specs=[per_step...  14.2 us
    pallas_call x2, Pallas kernels, split_call(): pl.pallas_call(kernel, grid_spec=pltpu.PrefetchScalarGridSpec(num_scalar_...  13.3 us
    all_to_all x1, starting transfers between devices, shards(): arrived_t = lax.all_to_all(mine_t, ('xlo', 'y'), 0, 0, tiled=False)  12.9 us
    all_to_all x3, waiting for transfers between devices, exchanged(): return lax.all_to_all(chunks, FRAME, 0, 0, tiled=False)  10.6 us
  transfers between devices with their start and end apart: 15, of which 6 were waited for; matrix products, arithmetic and copies ran while one was open for 5% of the time, Pallas kernels for 27%

profile of v7, /device:TPU:1, one launch (start us, length us, event | category | flops | bytes accessed | tf_op | source)
XLA Modules:
  0.0 190.3 jit_solution(166896433358977229)
XLA Ops:
  0.6 2.8 %collective-permute-start = (bf16[2,24,8,768]{3,2,1,0:T(8,128)(2,1)}, bf16[2,24,8,768]{3,2,1,0:T(8,128)(2,1)S(1)}, u32[]{:S(2)}, u32[]{:S(2)}) collective-permute-start(bf16[2,24,8,768]{3,2,1,0:T(8,128)(2,1)} %tokens_ref.1), channel_id=1, source_target_pairs={{0,8},{8,16},{16,24},{24,32},{32,40},{40,48},{48,56},{56,64},{64,7... | collective-permute-start | bytes 1769480 | tf_op jit(solution)/shard_map/ppermute | solution.py:553
  3.4 2.0 %copy.25 = bf16[2,8,3,8,768]{4,3,2,0,1:T(8,128)(2,1)} copy(bf16[2,8,3,8,768]{4,3,2,1,0:T(8,128)(2,1)} %bitcast.31) | data formatting | bytes 1179648 | tf_op jit(solution)/shard_map/reshape | solution.py:615
  5.4 7.5 %all-to-all-start = ((bf16[8,2,3,8,768]{4,3,2,1,0:T(8,128)(2,1)}), bf16[8,2,3,8,768]{4,3,2,1,0:T(8,128)(2,1)S(1)}, u32[]{:S(2)}, u32[]{:S(2)}) async-start(bf16[8,2,3,8,768]{4,3,2,1,0:T(8,128)(2,1)} %bitcast.28), calls=%async_computation | async-start | bytes 1179648 | tf_op jit(solution)/shard_map/all_to_all | solution.py:611
  14.6 14.2 %spatial_forward.1 = (bf16[2,576,768]{2,1,0:T(8,128)(2,1)}, bf16[2,192,768]{2,1,0:T(8,128)(2,1)}, bf16[2,576,1536]{2,1,0:T(8,128)(2,1)}, bf16[2,3,1344,256]{3,2,...) custom-call(bf16[2,24,8,768]{3,2,1,0:T(8,128)(2,1)} %tokens_ref.1, ...), custom_call_target="tpu_custom_call" | custom-call | flops 14000000000 | bytes 4194304 | tf_op jit(solution)/shard_map/spatial_forward/pallas_call | solution.py:142
  28.8 7.0 %all-to-all-start.1 = ((bf16[8,2,3,8,768]{4,3,2,1,0:T(8,128)(2,1)}), bf16[8,2,3,8,768]{4,3,2,1,0:T(8,128)(2,1)S(1)}, u32[]{:S(2)}, u32[]{:S(2)}) async-start(bf16[8,2,3,8,768]{4,3,2,1,0:T(8,128)(2,1)} %get-tuple-element.46), calls=%async_computation.1 | async-start | bytes 1179648 | tf_op jit(solution)/shard_map/all_to_all | solution.py:611
  36.5 1.6 dynamic-slice_convert_fusion
  38.1 7.2 %all-to-all-done.1.mid_ref = bf16[8,2,3,8,768]{4,3,2,1,0:T(8,128)(2,1)S(1)} async-done(((bf16[8,2,3,8,768]{4,3,2,1,0:T(8,128)(2,1)}), bf16[8,2,3,8,768]{4,3,2,1,0:T(8,128)(2,1)S(1)}, u32[]{:S(2)}, u32[]{:S(2)}) %all-to-all-start.1) | async-done | bytes 589856 | tf_op jit(solution)/shard_map/all_to_all | solution.py:611
  46.1 14.8 %temporal.1 = (bf16[8,4,3,8,768]{4,3,2,1,0:T(8,128)(2,1)}, bf16[384,1536]{1,0:T(8,128)(2,1)}, bf16[384,3072]{1,0:T(8,128)(2,1)}) custom-call(bf16[8,2,3,8,768]{4,3,2,1,0:T(8,128)(2,1)} %copy-done.9, bf16[8,2,3,8,768]{4,3,2,1,0:T(8,128)(2,1)} %copy-done.8, f32[1,768]{1,0:T(1,128)} %reshape.56.gain_ref, bf16[768,2304]{1,0:T(8,128)(2,1)} %qkv_ref.4, ...), custom_call_target="tpu_custom_call" | custom-call | flops 17999998976 | bytes 4194304 | tf_op jit(solution)/shard_map/temporal/pallas_call | solution.py:217
  60.9 3.6 %all-to-all-start.2 = ((bf16[8,4,3,8,768]{4,3,2,1,0:T(8,128)(2,1)}), bf16[8,4,3,8,768]{4,3,2,1,0:T(8,128)(2,1)S(1)}, u32[]{:S(2)}, u32[]{:S(2)}) async-start(bf16[8,4,3,8,768]{4,3,2,1,0:T(8,128)(2,1)} %get-tuple-element.49), calls=%async_computation.2 | async-start | bytes 2359296 | tf_op jit(solution)/shard_map/all_to_all | solution.py:611
  64.5 6.6 %term_time.1 = (bf16[8,48,3072]{2,1,0:T(8,128)(2,1)}, bf16[8,48,3072]{2,1,0:T(8,128)(2,1)}) custom-call(s32[1]{0:T(128)} %bitcast.4.core_ref, bf16[384,1536]{1,0:T(8,128)(2,1)} %get-tuple-element.50.left_ref, bf16[384,3072]{1,0:T(8,128)(2,1)} %get-tuple-element.51.right_ref), custom_call_target="tpu_custom_call" | custom-call | flops 1 | bytes 1 | tf_op jit(solution)/shard_map/term_time/pallas_call | solution.py:377
  71.1 4.2 %collective-permute-start.2 = (bf16[8,48,3072]{2,1,0:T(8,128)(2,1)}, bf16[8,48,3072]{2,1,0:T(8,128)(2,1)}, u32[]{:S(2)}, u32[]{:S(2)}) collective-permute-start(bf16[8,48,3072]{2,1,0:T(8,128)(2,1)} %get-tuple-element.53), channel_id=1, source_target_pairs={{0,8},{8,0},{1,9},{9,1},{2,10},{10,2},{3,11},{11,3},{4,12},{12,4},... | collective-permute-start | bytes 7077896 | tf_op jit(solution)/shard_map/ppermute | solution.py:484
  75.3 3.4 %all-to-all-done.2.dmid_ref = bf16[8,4,3,8,768]{4,3,2,1,0:T(8,128)(2,1)S(1)} async-done(((bf16[8,4,3,8,768]{4,3,2,1,0:T(8,128)(2,1)}), bf16[8,4,3,8,768]{4,3,2,1,0:T(8,128)(2,1)S(1)}, u32[]{:S(2)}, u32[]{:S(2)}) %all-to-all-start.2) | async-done | bytes 1179680 | tf_op jit(solution)/shard_map/all_to_all | solution.py:611
  78.7 1.9 back_projection.1.dproj_ref
  80.6 4.1 %add_convert_fusion = bf16[8,48,3072]{2,1,0:T(8,128)(2,1)} fusion(bf16[8,48,3072]{2,1,0:T(8,128)(2,1)} %collective-permute-done.2, bf16[8,48,3072]{2,1,0:T(8,128)(2,1)S(1)} %copy-done.7), kind=kLoop, calls=%fused_computation | loop fusion | flops 4718592 | bytes 7077888 | tf_op jit(solution)/shard_map/convert_element_type | solution.py:626
  84.6 12.9 %all-to-all-start.3 = ((bf16[8,48,3072]{2,1,0:T(8,128)(2,1)}), bf16[8,48,3072]{2,1,0:T(8,128)(2,1)S(1)}, u32[]{:S(2)}, u32[]{:S(2)}) async-start(bf16[8,48,3072]{2,1,0:T(8,128)(2,1)} %add_convert_fusion), calls=%async_computation.3 | async-start | bytes 4718592 | tf_op jit(solution)/shard_map/all_to_all | solution.py:629
  97.6 18.7 %spatial_backward.1 = (bf16[2,192,768]{2,1,0:T(8,128)(2,1)S(1)}, bf16[2,576,1536]{2,1,0:T(8,128)(2,1)S(1)}, bf16[2,24,8,768]{3,2,1,0:T(8,128)(2,1)}, bf16[2,24,8...) custom-call(bf16[2,192,768]{2,1,0:T(8,128)(2,1)} %back_projection.1.dproj_ref, bf16[768,2304]{1,0:T(8,128)(2,1)} %qkv_ref.5, ...), custom_call_target="tpu_custom_call" | custom-call | flops 20000000000 | bytes 4194304 | tf_op jit(solution)/shard_map/spatial_backward/pallas_call | solution.py:307
  116.3 6.7 %term_space.1 = (bf16[8,48,3072]{2,1,0:T(8,128)(2,1)}, bf16[8,48,3072]{2,1,0:T(8,128)(2,1)}) custom-call(s32[1]{0:T(128)} %bitcast.4.core_ref, bf16[2,576,768]{2,1,0:T(8,128)(2,1)S(1)} %copy-done, bf16[2,192,768]{2,1,0:T(8,128)(2,1)S(1)} %get-tuple-element.62.dq_ref, bf16[2,576,1536]{2,1,0:T(8,128)(2,1)S(1)} %get-tuple-element.63.dkv_ref, ...), custom_call_target="tpu_custom_call" | custom-call | flops 1 | bytes 1 | tf_op jit(solution)/shard_map/term_space/pallas_call | solution.py:377
  123.0 3.5 %all-to-all-done.3.arrived_ref = bf16[8,48,3072]{2,1,0:T(8,128)(2,1)S(1)} async-done(((bf16[8,48,3072]{2,1,0:T(8,128)(2,1)}), bf16[8,48,3072]{2,1,0:T(8,128)(2,1)S(1)}, u32[]{:S(2)}, u32[]{:S(2)}) %all-to-all-start.3) | async-done | bytes 2359328 | tf_op jit(solution)/shard_map/all_to_all | solution.py:629
  126.5 1.3 sum_fold.1
  128.7 1.6 dynamic-slice_bitcast_fusion
  131.3 6.3 %collective-permute-done.6 = bf16[4,144,128]{2,1,0:T(8,128)(2,1)} collective-permute-done((bf16[4,144,128]{2,1,0:T(8,128)(2,1)}, bf16[4,144,128]{2,1,0:T(8,128)(2,1)}, u32[]{:S(2)}, u32[]{:S(2)}) %collective-permute-start.6) | collective-permute-done | bytes 147488 | tf_op jit(solution)/shard_map/ppermute | solution.py:536
  137.5 1.7 fusion
  139.2 4.8 %pair_fold.1 = bf16[64,144,128]{2,1,0:T(8,128)(2,1)} custom-call(bf16[8,48,3072]{2,1,0:T(8,128)(2,1)} %get-tuple-element.65.keep_ref, bf16[8,48,3072]{2,1,0:T(8,128)(2,1)S(1)} %collective-permute-done.5.got_ref), custom_call_target="tpu_custom_call" | custom-call | flops 1 | bytes 1 | tf_op jit(solution)/shard_map/pair_fold/pallas_call | solution.py:493
  144.1 6.0 %all-to-all-start.4 = ((bf16[64,144,128]{2,1,0:T(8,128)(2,1)}), bf16[64,144,128]{2,1,0:T(8,128)(2,1)S(1)}, u32[]{:S(2)}, u32[]{:S(2)}) async-start(bf16[64,144,128]{2,1,0:T(8,128)(2,1)} %pair_fold.1), calls=%async_computation.4 | async-start | bytes 4718592 | tf_op jit(solution)/shard_map/all_to_all | solution.py:548
  150.0 1.1 collective-permute-start.3
  151.2 1.5 collective-permute-start.4
  153.8 1.3 collective-permute-start.7
  155.0 2.4 %collective-permute-start.8 = (bf16[144,128]{1,0:T(8,128)(2,1)S(1)}, bf16[144,128]{1,0:T(8,128)(2,1)S(1)}, u32[]{:S(2)}, u32[]{:S(2)}) collective-permute-start(bf16[144,128]{1,0:T(8,128)(2,1)S(1)} %get-tuple-element.84), channel_id=1, source_target_pairs={{0,4},{2,6},{4,0},{6,2},{1,5},{3,7},{5,1},{7,3},{8,12},{10,14},{12... | collective-permute-start | bytes 110600 | tf_op jit(solution)/shard_map/ppermute | solution.py:536
  157.4 1.2 collective-permute-start.9
  158.6 25.6 %collective-permute-done.3.first_ref = bf16[2,24,8,768]{3,2,1,0:T(8,128)(2,1)} collective-permute-done((bf16[2,24,8,768]{3,2,1,0:T(8,128)(2,1)}, bf16[2,24,8,768]{3,2,1,0:T(8,128)(2,1)}, u32[]{:S(2)}, u32[]{:S(2)}) %collective-permute-start.3) | collective-permute-done | bytes 589856 | tf_op jit(solution)/shard_map/ppermute | solution.py:553
  184.3 2.9 %final_norm.1 = f32[2,24,8,768]{3,2,1,0:T(8,128)} custom-call(bf16[2,24,8,768]{3,2,1,0:T(8,128)(2,1)S(1)} %copy-done.5, f32[1,768]{1,0:T(1,128)S(1)} %reshape.54.gain_ref, bf16[8,4,3,8,768]{4,3,2,1,0:T(8,128)(2,1)S(1)} %all-to-all-done.2.dmid_ref, bf16[2,24,8,768]{3,2,1,0:T(8,128)(2,1)S(1)} %copy-done.6, ...), custom_call_target="tpu_custom_call" | custom-call | flops 3000000000 | bytes 4194304 | tf_op jit(solution)/shard_map/final_norm/pallas_call | solution.py:347
  188.6 1.1 finish.2
  (56 shorter events, 8.2 us)
Async XLA Ops:
  0.6 12.3 %copy-start.11 = (f32[768]{0:T(1024)S(1)}, f32[768]{0:T(1024)}, u32[]{:S(2)}) copy-start(f32[768]{0:T(1024)} %param.9) | copy-start | bytes 9220
  0.6 12.3 %collective-permute-start = (bf16[2,24,8,768]{3,2,1,0:T(8,128)(2,1)}, bf16[2,24,8,768]{3,2,1,0:T(8,128)(2,1)S(1)}, u32[]{:S(2)}, u32[]{:S(2)}) collective-permute-start(bf16[2,24,8,768]{3,2,1,0:T(8,128)(2,1)} %tokens_ref.1), channel_id=1, source_target_pairs={{0,8},{8,16},{16,24},{24,32},{32,40},{40,48},{48,56},{56,64},{64,7... | collective-permute-start | bytes 1769480 | tf_op jit(solution)/shard_map/ppermute | solution.py:553
  3.4 9.8 %collective-permute-start.1 = (bf16[2,24,8,768]{3,2,1,0:T(8,128)(2,1)}, bf16[2,24,8,768]{3,2,1,0:T(8,128)(2,1)S(1)}, u32[]{:S(2)}, u32[]{:S(2)}) collective-permute-start(bf16[2,24,8,768]{3,2,1,0:T(8,128)(2,1)} %tokens_ref.1), channel_id=1, source_target_pairs={{0,120},{8,0},{16,8},{24,16},{32,24},{40,32},{48,40},{56,48},{64,5... | collective-permute-start | bytes 1769480 | tf_op jit(solution)/shard_map/ppermute | solution.py:553
  5.4 23.4 %all-to-all-start = ((bf16[8,2,3,8,768]{4,3,2,1,0:T(8,128)(2,1)}), bf16[8,2,3,8,768]{4,3,2,1,0:T(8,128)(2,1)S(1)}, u32[]{:S(2)}, u32[]{:S(2)}) async-start(bf16[8,2,3,8,768]{4,3,2,1,0:T(8,128)(2,1)} %bitcast.28), calls=%async_computation | async-start | bytes 1179648 | tf_op jit(solution)/shard_map/all_to_all | solution.py:611
  12.9 22.9 %copy-start.12 = (f32[768]{0:T(1024)S(1)}, f32[768]{0:T(1024)}, u32[]{:S(2)}) copy-start(f32[768]{0:T(1024)} %param.12) | copy-start | bytes 9220
  12.9 0.8 copy-start.13
  13.8 0.8 copy-start.14
  28.8 16.5 %copy-start.8 = (bf16[8,2,3,8,768]{4,3,2,1,0:T(8,128)(2,1)}, bf16[8,2,3,8,768]{4,3,2,1,0:T(8,128)(2,1)S(1)}, u32[]{:S(2)}) copy-start(bf16[8,2,3,8,768]{4,3,2,1,0:T(8,128)(2,1)S(1)} %all-to-all-done.cot_ref) | copy-start | bytes 1769476
  28.8 16.5 %all-to-all-start.1 = ((bf16[8,2,3,8,768]{4,3,2,1,0:T(8,128)(2,1)}), bf16[8,2,3,8,768]{4,3,2,1,0:T(8,128)(2,1)S(1)}, u32[]{:S(2)}, u32[]{:S(2)}) async-start(bf16[8,2,3,8,768]{4,3,2,1,0:T(8,128)(2,1)} %get-tuple-element.46), calls=%async_computation.1 | async-start | bytes 1179648 | tf_op jit(solution)/shard_map/all_to_all | solution.py:611
  45.3 0.8 copy-start.9
  60.9 17.8 %all-to-all-start.2 = ((bf16[8,4,3,8,768]{4,3,2,1,0:T(8,128)(2,1)}), bf16[8,4,3,8,768]{4,3,2,1,0:T(8,128)(2,1)S(1)}, u32[]{:S(2)}, u32[]{:S(2)}) async-start(bf16[8,4,3,8,768]{4,3,2,1,0:T(8,128)(2,1)} %get-tuple-element.49), calls=%async_computation.2 | async-start | bytes 2359296 | tf_op jit(solution)/shard_map/all_to_all | solution.py:611
  64.5 14.2 %copy-start.4 = (bf16[768,768]{1,0:T(8,128)(2,1)S(1)}, bf16[768,768]{1,0:T(8,128)(2,1)}, u32[]{:S(2)}) copy-start(bf16[768,768]{1,0:T(8,128)(2,1)} %out_ref.5) | copy-start | bytes 3538948
  71.1 9.5 %collective-permute-start.2 = (bf16[8,48,3072]{2,1,0:T(8,128)(2,1)}, bf16[8,48,3072]{2,1,0:T(8,128)(2,1)}, u32[]{:S(2)}, u32[]{:S(2)}) collective-permute-start(bf16[8,48,3072]{2,1,0:T(8,128)(2,1)} %get-tuple-element.53), channel_id=1, source_target_pairs={{0,8},{8,0},{1,9},{9,1},{2,10},{10,2},{3,11},{11,3},{4,12},{12,4},... | collective-permute-start | bytes 7077896 | tf_op jit(solution)/shard_map/ppermute | solution.py:484
  78.7 1.9 copy-start.7
  84.6 41.9 %all-to-all-start.3 = ((bf16[8,48,3072]{2,1,0:T(8,128)(2,1)}), bf16[8,48,3072]{2,1,0:T(8,128)(2,1)S(1)}, u32[]{:S(2)}, u32[]{:S(2)}) async-start(bf16[8,48,3072]{2,1,0:T(8,128)(2,1)} %add_convert_fusion), calls=%async_computation.3 | async-start | bytes 4718592 | tf_op jit(solution)/shard_map/all_to_all | solution.py:629
  97.6 18.7 %copy-start = (bf16[2,576,768]{2,1,0:T(8,128)(2,1)S(1)}, bf16[2,576,768]{2,1,0:T(8,128)(2,1)}, u32[]{:S(2)}) copy-start(bf16[2,576,768]{2,1,0:T(8,128)(2,1)} %get-tuple-element.61.y_ref) | copy-start | bytes 5308420
  97.6 18.7 %copy-start.1 = (bf16[2,192,768]{2,1,0:T(8,128)(2,1)S(1)}, bf16[2,192,768]{2,1,0:T(8,128)(2,1)}, u32[]{:S(2)}) copy-start(bf16[2,192,768]{2,1,0:T(8,128)(2,1)} %get-tuple-element.64.o_ref) | copy-start | bytes 1769476
  127.8 11.4 %collective-permute-start.5 = (bf16[8,48,3072]{2,1,0:T(8,128)(2,1)}, bf16[8,48,3072]{2,1,0:T(8,128)(2,1)S(1)}, u32[]{:S(2)}, u32[]{:S(2)}) collective-permute-start(bf16[8,48,3072]{2,1,0:T(8,128)(2,1)} %get-tuple-element.68), channel_id=1, source_target_pairs={{0,8},{8,0},{1,9},{9,1},{2,10},{10,2},{3,11},{11,3},{4,12},{12,4},... | collective-permute-start | bytes 7077896 | tf_op jit(solution)/shard_map/ppermute | solution.py:484
  130.2 7.3 %collective-permute-start.6 = (bf16[4,144,128]{2,1,0:T(8,128)(2,1)}, bf16[4,144,128]{2,1,0:T(8,128)(2,1)}, u32[]{:S(2)}, u32[]{:S(2)}) collective-permute-start(bf16[4,144,128]{2,1,0:T(8,128)(2,1)} %dynamic-slice_bitcast_fusion), channel_id=1, source_target_pairs={{0,1},{1,0},{2,3},{3,2},{4,5},{5,4},{6,7},{7,6},{8,9},{9,8},{10,11... | collective-permute-start | bytes 442376 | tf_op jit(solution)/shard_map/ppermute | solution.py:536
  144.1 44.5 %all-to-all-start.4 = ((bf16[64,144,128]{2,1,0:T(8,128)(2,1)}), bf16[64,144,128]{2,1,0:T(8,128)(2,1)S(1)}, u32[]{:S(2)}, u32[]{:S(2)}) async-start(bf16[64,144,128]{2,1,0:T(8,128)(2,1)} %pair_fold.1), calls=%async_computation.4 | async-start | bytes 4718592 | tf_op jit(solution)/shard_map/all_to_all | solution.py:548
  150.0 34.2 %collective-permute-start.3 = (bf16[2,24,8,768]{3,2,1,0:T(8,128)(2,1)}, bf16[2,24,8,768]{3,2,1,0:T(8,128)(2,1)}, u32[]{:S(2)}, u32[]{:S(2)}) collective-permute-start(bf16[2,24,8,768]{3,2,1,0:T(8,128)(2,1)} %get-tuple-element.59), channel_id=1, source_target_pairs={{0,120},{8,0},{16,8},{24,16},{32,24},{40,32},{48,40},{56,48},{64,5... | collective-permute-start | bytes 1769480 | tf_op jit(solution)/shard_map/ppermute | solution.py:553
  151.2 33.1 %collective-permute-start.4 = (bf16[2,24,8,768]{3,2,1,0:T(8,128)(2,1)}, bf16[2,24,8,768]{3,2,1,0:T(8,128)(2,1)}, u32[]{:S(2)}, u32[]{:S(2)}) collective-permute-start(bf16[2,24,8,768]{3,2,1,0:T(8,128)(2,1)} %get-tuple-element.60), channel_id=1, source_target_pairs={{0,8},{8,16},{16,24},{24,32},{32,40},{40,48},{48,56},{56,64},{64,7... | collective-permute-start | bytes 1769480 | tf_op jit(solution)/shard_map/ppermute | solution.py:553
  152.9 0.9 copy-start.10
  152.9 31.4 %copy-start.5 = (bf16[2,24,8,768]{3,2,1,0:T(8,128)(2,1)S(1)}, bf16[2,24,8,768]{3,2,1,0:T(8,128)(2,1)}, u32[]{:S(2)}) copy-start(bf16[2,24,8,768]{3,2,1,0:T(8,128)(2,1)} %tokens_ref.1) | copy-start | bytes 1769476
  152.9 31.4 %copy-start.6 = (bf16[2,24,8,768]{3,2,1,0:T(8,128)(2,1)S(1)}, bf16[2,24,8,768]{3,2,1,0:T(8,128)(2,1)}, u32[]{:S(2)}) copy-start(bf16[2,24,8,768]{3,2,1,0:T(8,128)(2,1)} %get-tuple-element.58.own_ref) | copy-start | bytes 1769476
  153.8 33.4 %collective-permute-start.7 = (bf16[144,128]{1,0:T(8,128)(2,1)S(1)}, bf16[144,128]{1,0:T(8,128)(2,1)S(1)}, u32[]{:S(2)}, u32[]{:S(2)}) collective-permute-start(bf16[144,128]{1,0:T(8,128)(2,1)S(1)} %get-tuple-element.82), channel_id=1, source_target_pairs={{0,2},{2,4},{4,6},{6,0},{1,3},{3,5},{5,7},{7,1},{8,10},{10,12},{12... | collective-permute-start | bytes 110600 | tf_op jit(solution)/shard_map/ppermute | solution.py:536
  155.0 32.1 %collective-permute-start.8 = (bf16[144,128]{1,0:T(8,128)(2,1)S(1)}, bf16[144,128]{1,0:T(8,128)(2,1)S(1)}, u32[]{:S(2)}, u32[]{:S(2)}) collective-permute-start(bf16[144,128]{1,0:T(8,128)(2,1)S(1)} %get-tuple-element.84), channel_id=1, source_target_pairs={{0,4},{2,6},{4,0},{6,2},{1,5},{3,7},{5,1},{7,3},{8,12},{10,14},{12... | collective-permute-start | bytes 110600 | tf_op jit(solution)/shard_map/ppermute | solution.py:536
  157.4 29.8 %collective-permute-start.9 = (bf16[144,128]{1,0:T(8,128)(2,1)S(1)}, bf16[144,128]{1,0:T(8,128)(2,1)S(1)}, u32[]{:S(2)}, u32[]{:S(2)}) collective-permute-start(bf16[144,128]{1,0:T(8,128)(2,1)S(1)} %get-tuple-element.83), channel_id=1, source_target_pairs={{0,6},{2,0},{4,2},{6,4},{1,7},{3,1},{5,3},{7,5},{8,14},{10,8},{12,... | collective-permute-start | bytes 110600 | tf_op jit(solution)/shard_map/ppermute | solution.py:536
  184.2 3.0 %copy-start.3 = (f32[6,2304]{1,0:T(8,128)S(1)}, f32[6,2304]{1,0:T(8,128)}, u32[]{:S(2)}) copy-start(f32[6,2304]{1,0:T(8,128)} %get-tuple-element.77.weight_ref) | copy-start | bytes 165892
  187.2 1.3 copy-start.2
